TPU v7x, 32 devices: a whole 2x2x4 slice. The times are simulated.
32 devices in a mesh: shot: 4 (over x, core), space: 8 (over z, y).
Axes of the slice: x: 2, y: 2, z: 4, core: 2. Of those that a mesh axis runs over, the one named last changes fastest.
Arguments:
- residual_traces: float32 [4, 12, 2048], P('shot', None, 'space'), may hold values from -6 to 6
- owners: int32 [4, 2048, 1], P('shot', 'space'), may hold values from 0 to 7; in each aligned block of 256 rows (0 to 255, 256 to 511, ..., all dimensions but the last counted through in order) at most 64 rows name the same one
- surface_cells: int32 [4, 2048], P('shot', 'space'), may hold values from 0 to 511
- trace_counts: int32 [4], P('shot'), may hold values from 512 to 2048, as said below
- start_current: float32 [4, 64, 64, 256], P('shot', 'space'), may hold values from -6 to 6
- start_later: float32 [4, 64, 64, 256], P('shot', 'space'), may hold values from -6 to 6
- forward_accel: bfloat16 [4, 12, 64, 64, 256], P('shot', None, 'space'), may hold values from -6 to 6
- courant_sq: float32 [64, 64, 256], P('space'), may hold values from 0.04 to 0.16
Outputs:
- adjoint_field: float32 [4, 64, 64, 256], P('shot', 'space')
- velocity_grad: float32 [64, 64, 256], P('space', 'shot')
Inputs may be any that keep to these rules, and one draw needn't show every extreme that they name: `owners`: among the receivers of one device, no subdomain is named more than 64 times. `trace_counts`: some shot has all 2048 traces live.
All inputs are finite; a program needn't handle non-finite values.
Results may differ from a plain program's by a relative error of at most 0.0003.
Values sent between devices are 32-bit elements; how exact they have to be, the bound alone decides.
No kernel may reach another device: no remote copies, remote signals or barrier semaphores. Data moves between devices by JAX's collectives and lax.ppermute only.
A program may use at most 64 MiB of HBM per device.

v0:
```python
import jax
import jax.numpy as jnp
from jax import lax
from jax.sharding import PartitionSpec as P

STENCIL_WEIGHTS = (-205.0 / 72.0, 8.0 / 5.0, -1.0 / 5.0, 8.0 / 315.0, -1.0 / 560.0)


def extended_2(shard, sides, width):
    for axis, dim in sides:
        size, length = (lax.axis_size(axis), shard.shape[dim])
        up = [(i, (i + 1) % size) for i in range(size - 1)]
        down = [(j, i) for i, j in up]
        last = lax.slice_in_dim(shard, length - width, length, axis=dim)
        leading = lax.slice_in_dim(shard, 0, width, axis=dim)
        before = lax.ppermute(last, axis, up)
        after = lax.ppermute(leading, axis, down)
        shard = jnp.concatenate([before, shard, after], axis=dim)
    return shard


def laplace(padded):
    length = padded.shape[0] - 8
    across = padded.shape[1] - 8
    height = padded.shape[2] - 8

    def window(off_x, off_y, off_z):
        return lax.slice(
            padded,
            (4 + off_x, 4 + off_y, 4 + off_z),
            (4 + off_x + length, 4 + off_y + across, 4 + off_z + height),
        )

    summed = 3.0 * STENCIL_WEIGHTS[0] * window(0, 0, 0)
    for offset in range(1, 5):
        six_taps = window(offset, 0, 0) + window(-offset, 0, 0) + window(0, offset, 0)
        six_taps = six_taps + window(0, -offset, 0) + window(0, 0, offset) + window(0, 0, -offset)
        summed = summed + STENCIL_WEIGHTS[offset] * six_taps
    return summed


def laplace_rim(extended):
    return laplace(jnp.pad(extended, ((0, 0), (4, 4), (4, 4))))


def onehot_cells(targets, plane_cells):
    return (targets[:, None] == jnp.arange(plane_cells, dtype=jnp.int32)[None, :]).astype(
        jnp.float32
    )


def shards(
    residual_traces,
    owners,
    surface_cells,
    trace_counts,
    start_current,
    start_later,
    forward_accel,
    courant_sq,
):
    traces = residual_traces[0]
    owner_row = owners[0, :, 0]
    surface = surface_cells[0]
    live_count = trace_counts[0]
    forward = forward_accel[0]
    first_field = start_current[0]
    prior_field = start_later[0]
    length, across, height = courant_sq.shape
    plane_cells = length * across
    steps_all = traces.shape[0]
    my_index = lax.axis_index("space")
    piece_traces = lax.all_gather(traces, "space", axis=1, tiled=True)
    piece_owner = lax.all_gather(owner_row[None, :], "space", axis=1, tiled=True)
    piece_surface = lax.all_gather(surface[None, :], "space", axis=1, tiled=True)
    number = jnp.arange(piece_traces.shape[1], dtype=jnp.int32)
    keep = (number < live_count) & (piece_owner[0] == my_index)
    targets = jnp.where(keep, piece_surface[0], -1)
    table = onehot_cells(targets, plane_cells)
    planes = jnp.dot(
        piece_traces, table, precision=lax.Precision.HIGHEST, preferred_element_type=jnp.float32
    )
    planes = planes.reshape(steps_all, length, across)
    empty = jnp.zeros((length, across, height), jnp.float32)

    def advance(section, state):
        current, later, gradient = state
        extended = extended_2(current, (("space", 0),), 4)
        fresh = 2.0 * current - later + courant_sq * laplace_rim(extended)
        fresh = fresh.at[:, :, 2].add(lax.dynamic_index_in_dim(planes, section, 0, keepdims=False))
        accel = lax.dynamic_index_in_dim(forward, section, 0, keepdims=False).astype(jnp.float32)
        return (fresh, current, gradient + fresh * accel)

    current, later, gradient = lax.fori_loop(
        0, steps_all, advance, (first_field, prior_field, empty)
    )
    velocity_grad = lax.psum_scatter(gradient, "shot", scatter_dimension=1, tiled=True)
    return (current[None], velocity_grad)


def solution(mesh):
    placed = (
        P("shot", None, "space"),
        P("shot", "space", None),
        P("shot", "space"),
        P("shot"),
        P("shot", "space", None, None),
        P("shot", "space", None, None),
        P("shot", None, "space", None, None),
        P("space", None, None),
    )
    return jax.shard_map(
        shards,
        mesh=mesh,
        in_specs=placed,
        out_specs=(P("shot", "space", None, None), P("space", "shot", None)),
        check_vma=False,
    )
```

profile of v0, /device:TPU:16, one launch (start us, length us, event | category | flops | bytes accessed | tf_op | source)
XLA Modules:
  0.0 557.7 jit_solution(151026177992258460)
XLA Ops:
  7.9 15.4 %all-gather = s32[1,2048,1]{1,2,0:T(1,128)S(1)} all-gather(s32[1,256,1]{1,2,0:T(1,128)} %param.13), channel_id=2, replica_groups=mesh['shot'=4,'space'=8] {'space'}, dimensions={1}, use_global_device_ids=true | all-gather | bytes 9216 | tf_op jit(solution)/shard_map/all_gather | solution.py:74
  23.3 17.2 %all_gather.10 = s32[1,2048]{1,0:T(1,128)S(1)} all-gather(s32[1,256]{1,0:T(1,128)} %param.14), channel_id=1, replica_groups=mesh['shot'=4,'space'=8] {'space'}, dimensions={1}, use_global_device_ids=true | all-gather | bytes 9216 | tf_op jit(solution)/shard_map/all_gather | solution.py:75
  40.5 19.3 %all-gather.1 = f32[1,12,2048]{2,0,1:T(1,128)S(1)} all-gather(f32[1,12,256]{2,0,1:T(1,128)} %param.12), channel_id=3, replica_groups=mesh['shot'=4,'space'=8] {'space'}, dimensions={2}, use_global_device_ids=true | all-gather | bytes 110592 | tf_op jit(solution)/shard_map/all_gather | solution.py:73
  72.7 454.1 %while.21 = (s32[]{:T(128)}, f32[8,64,256]{1,0,2:T(8,128)S(1)}, f32[8,64,256]{1,0,2:T(8,128)}, f32[8,64,256]{1,0,2:T(8,128)}, f32[8,64,256]{1,0,2:T(8,128)}, /*i...) while((s32[]{:T(128)}, f32[8,64,256]{1,0,2:T(8,128)S(1)}, ...), condition=%wide.region_1.2_spmd.clone, body=%wide.region_0.1_spmd.clone.sunk | while | flops 9936387 | bytes 35305808 | solution.py:94
  78.8 10.7 %collective-permute-done.1 = f32[4,64,256]{1,0,2:T(4,128)S(1)} collective-permute-done((f32[4,64,256]{1,0,2:T(4,128)S(1)}, f32[4,64,256]{1,0,2:T(4,128)S(1)}, u32[]{:S(2)}, u32[]{:S(2)}) %collective-permute-start.1) | collective-permute-done | bytes 262176 | tf_op jit(solution)/shard_map/while/body/eval_jaxpr/ppermute | solution.py:17
  94.1 10.2 %fusion.47 = f32[8,64,256]{1,0,2:T(8,128)} fusion(f32[8,64,256]{1,0,2:T(8,128)} %get-tuple-element.335, f32[8,64,256]{1,0,2:T(8,128)S(1)} %get-tuple-element.323, f32[4,64,256]{1,0,2:T(4,128)} %collective-permute-done, f32[16,72,264]{1,0,2:T(8,128)S(1)} %select_maximum_fusion.3, f32[12,64,256]{1,0,2:T(8,128)} %copy-done, ...), kind=kLoop, calls=%fused_computation.25.clone.1 | loop fusion | flops 4849664 | bytes 12845056 | tf_op jit(solution)/shard_map/while/body/eval_jaxpr/add | solution.py:89
  116.7 10.7 %collective-permute-done.1 = f32[4,64,256]{1,0,2:T(4,128)S(1)} collective-permute-done((f32[4,64,256]{1,0,2:T(4,128)S(1)}, f32[4,64,256]{1,0,2:T(4,128)S(1)}, u32[]{:S(2)}, u32[]{:S(2)}) %collective-permute-start.1) | collective-permute-done | bytes 262176 | tf_op jit(solution)/shard_map/while/body/eval_jaxpr/ppermute | solution.py:17
  131.9 10.2 %fusion.47 = f32[8,64,256]{1,0,2:T(8,128)} fusion(f32[8,64,256]{1,0,2:T(8,128)} %get-tuple-element.335, f32[8,64,256]{1,0,2:T(8,128)S(1)} %get-tuple-element.323, f32[4,64,256]{1,0,2:T(4,128)} %collective-permute-done, f32[16,72,264]{1,0,2:T(8,128)S(1)} %select_maximum_fusion.3, f32[12,64,256]{1,0,2:T(8,128)} %copy-done, ...), kind=kLoop, calls=%fused_computation.25.clone.1 | loop fusion | flops 4849664 | bytes 12845056 | tf_op jit(solution)/shard_map/while/body/eval_jaxpr/add | solution.py:89
  154.5 10.7 %collective-permute-done.1 = f32[4,64,256]{1,0,2:T(4,128)S(1)} collective-permute-done((f32[4,64,256]{1,0,2:T(4,128)S(1)}, f32[4,64,256]{1,0,2:T(4,128)S(1)}, u32[]{:S(2)}, u32[]{:S(2)}) %collective-permute-start.1) | collective-permute-done | bytes 262176 | tf_op jit(solution)/shard_map/while/body/eval_jaxpr/ppermute | solution.py:17
  169.8 10.2 %fusion.47 = f32[8,64,256]{1,0,2:T(8,128)} fusion(f32[8,64,256]{1,0,2:T(8,128)} %get-tuple-element.335, f32[8,64,256]{1,0,2:T(8,128)S(1)} %get-tuple-element.323, f32[4,64,256]{1,0,2:T(4,128)} %collective-permute-done, f32[16,72,264]{1,0,2:T(8,128)S(1)} %select_maximum_fusion.3, f32[12,64,256]{1,0,2:T(8,128)} %copy-done, ...), kind=kLoop, calls=%fused_computation.25.clone.1 | loop fusion | flops 4849664 | bytes 12845056 | tf_op jit(solution)/shard_map/while/body/eval_jaxpr/add | solution.py:89
  192.4 10.7 %collective-permute-done.1 = f32[4,64,256]{1,0,2:T(4,128)S(1)} collective-permute-done((f32[4,64,256]{1,0,2:T(4,128)S(1)}, f32[4,64,256]{1,0,2:T(4,128)S(1)}, u32[]{:S(2)}, u32[]{:S(2)}) %collective-permute-start.1) | collective-permute-done | bytes 262176 | tf_op jit(solution)/shard_map/while/body/eval_jaxpr/ppermute | solution.py:17
  207.6 10.2 %fusion.47 = f32[8,64,256]{1,0,2:T(8,128)} fusion(f32[8,64,256]{1,0,2:T(8,128)} %get-tuple-element.335, f32[8,64,256]{1,0,2:T(8,128)S(1)} %get-tuple-element.323, f32[4,64,256]{1,0,2:T(4,128)} %collective-permute-done, f32[16,72,264]{1,0,2:T(8,128)S(1)} %select_maximum_fusion.3, f32[12,64,256]{1,0,2:T(8,128)} %copy-done, ...), kind=kLoop, calls=%fused_computation.25.clone.1 | loop fusion | flops 4849664 | bytes 12845056 | tf_op jit(solution)/shard_map/while/body/eval_jaxpr/add | solution.py:89
  230.2 10.7 %collective-permute-done.1 = f32[4,64,256]{1,0,2:T(4,128)S(1)} collective-permute-done((f32[4,64,256]{1,0,2:T(4,128)S(1)}, f32[4,64,256]{1,0,2:T(4,128)S(1)}, u32[]{:S(2)}, u32[]{:S(2)}) %collective-permute-start.1) | collective-permute-done | bytes 262176 | tf_op jit(solution)/shard_map/while/body/eval_jaxpr/ppermute | solution.py:17
  245.4 10.2 %fusion.47 = f32[8,64,256]{1,0,2:T(8,128)} fusion(f32[8,64,256]{1,0,2:T(8,128)} %get-tuple-element.335, f32[8,64,256]{1,0,2:T(8,128)S(1)} %get-tuple-element.323, f32[4,64,256]{1,0,2:T(4,128)} %collective-permute-done, f32[16,72,264]{1,0,2:T(8,128)S(1)} %select_maximum_fusion.3, f32[12,64,256]{1,0,2:T(8,128)} %copy-done, ...), kind=kLoop, calls=%fused_computation.25.clone.1 | loop fusion | flops 4849664 | bytes 12845056 | tf_op jit(solution)/shard_map/while/body/eval_jaxpr/add | solution.py:89
  268.0 10.7 %collective-permute-done.1 = f32[4,64,256]{1,0,2:T(4,128)S(1)} collective-permute-done((f32[4,64,256]{1,0,2:T(4,128)S(1)}, f32[4,64,256]{1,0,2:T(4,128)S(1)}, u32[]{:S(2)}, u32[]{:S(2)}) %collective-permute-start.1) | collective-permute-done | bytes 262176 | tf_op jit(solution)/shard_map/while/body/eval_jaxpr/ppermute | solution.py:17
  283.3 10.2 %fusion.47 = f32[8,64,256]{1,0,2:T(8,128)} fusion(f32[8,64,256]{1,0,2:T(8,128)} %get-tuple-element.335, f32[8,64,256]{1,0,2:T(8,128)S(1)} %get-tuple-element.323, f32[4,64,256]{1,0,2:T(4,128)} %collective-permute-done, f32[16,72,264]{1,0,2:T(8,128)S(1)} %select_maximum_fusion.3, f32[12,64,256]{1,0,2:T(8,128)} %copy-done, ...), kind=kLoop, calls=%fused_computation.25.clone.1 | loop fusion | flops 4849664 | bytes 12845056 | tf_op jit(solution)/shard_map/while/body/eval_jaxpr/add | solution.py:89
  305.9 10.7 %collective-permute-done.1 = f32[4,64,256]{1,0,2:T(4,128)S(1)} collective-permute-done((f32[4,64,256]{1,0,2:T(4,128)S(1)}, f32[4,64,256]{1,0,2:T(4,128)S(1)}, u32[]{:S(2)}, u32[]{:S(2)}) %collective-permute-start.1) | collective-permute-done | bytes 262176 | tf_op jit(solution)/shard_map/while/body/eval_jaxpr/ppermute | solution.py:17
  321.1 10.2 %fusion.47 = f32[8,64,256]{1,0,2:T(8,128)} fusion(f32[8,64,256]{1,0,2:T(8,128)} %get-tuple-element.335, f32[8,64,256]{1,0,2:T(8,128)S(1)} %get-tuple-element.323, f32[4,64,256]{1,0,2:T(4,128)} %collective-permute-done, f32[16,72,264]{1,0,2:T(8,128)S(1)} %select_maximum_fusion.3, f32[12,64,256]{1,0,2:T(8,128)} %copy-done, ...), kind=kLoop, calls=%fused_computation.25.clone.1 | loop fusion | flops 4849664 | bytes 12845056 | tf_op jit(solution)/shard_map/while/body/eval_jaxpr/add | solution.py:89
  343.7 10.7 %collective-permute-done.1 = f32[4,64,256]{1,0,2:T(4,128)S(1)} collective-permute-done((f32[4,64,256]{1,0,2:T(4,128)S(1)}, f32[4,64,256]{1,0,2:T(4,128)S(1)}, u32[]{:S(2)}, u32[]{:S(2)}) %collective-permute-start.1) | collective-permute-done | bytes 262176 | tf_op jit(solution)/shard_map/while/body/eval_jaxpr/ppermute | solution.py:17
  381.5 10.7 %collective-permute-done.1 = f32[4,64,256]{1,0,2:T(4,128)S(1)} collective-permute-done((f32[4,64,256]{1,0,2:T(4,128)S(1)}, f32[4,64,256]{1,0,2:T(4,128)S(1)}, u32[]{:S(2)}, u32[]{:S(2)}) %collective-permute-start.1) | collective-permute-done | bytes 262176 | tf_op jit(solution)/shard_map/while/body/eval_jaxpr/ppermute | solution.py:17
  419.4 10.7 %collective-permute-done.1 = f32[4,64,256]{1,0,2:T(4,128)S(1)} collective-permute-done((f32[4,64,256]{1,0,2:T(4,128)S(1)}, f32[4,64,256]{1,0,2:T(4,128)S(1)}, u32[]{:S(2)}, u32[]{:S(2)}) %collective-permute-start.1) | collective-permute-done | bytes 262176 | tf_op jit(solution)/shard_map/while/body/eval_jaxpr/ppermute | solution.py:17
  457.2 10.7 %collective-permute-done.1 = f32[4,64,256]{1,0,2:T(4,128)S(1)} collective-permute-done((f32[4,64,256]{1,0,2:T(4,128)S(1)}, f32[4,64,256]{1,0,2:T(4,128)S(1)}, u32[]{:S(2)}, u32[]{:S(2)}) %collective-permute-start.1) | collective-permute-done | bytes 262176 | tf_op jit(solution)/shard_map/while/body/eval_jaxpr/ppermute | solution.py:17
  495.1 10.7 %collective-permute-done.1 = f32[4,64,256]{1,0,2:T(4,128)S(1)} collective-permute-done((f32[4,64,256]{1,0,2:T(4,128)S(1)}, f32[4,64,256]{1,0,2:T(4,128)S(1)}, u32[]{:S(2)}, u32[]{:S(2)}) %collective-permute-start.1) | collective-permute-done | bytes 262176 | tf_op jit(solution)/shard_map/while/body/eval_jaxpr/ppermute | solution.py:17
  530.3 20.5 %reduce-scatter.2.cloned.1.call-done = f32[8,16,256]{2,1,0:T(8,128)} async-done(((f32[8,64,256]{2,1,0:T(8,128)}), f32[8,16,256]{2,1,0:T(8,128)}) %reduce-scatter.2.cloned.1.call-update) | async-done | bytes 131088 | tf_op jit(solution)/shard_map/reduce_scatter | solution.py:97
  (274 shorter events, 269.4 us)
Async XLA Ops:
  7.2 543.7 %reduce-scatter.2.cloned.1.call-start = ((), (), s32[]{:S(2)}) async-start(), calls=%async_computation.1 | async-start | bytes 655360 | tf_op jit(solution)/shard_map/reduce_scatter | solution.py:97
  72.9 16.7 %collective-permute-start.1 = (f32[4,64,256]{1,0,2:T(4,128)S(1)}, f32[4,64,256]{1,0,2:T(4,128)S(1)}, u32[]{:S(2)}, u32[]{:S(2)}) collective-permute-start(f32[4,64,256]{1,0,2:T(4,128)S(1)} %get-tuple-element.312), channel_id=1, source_target_pairs={{1,0},{2,1},{3,2},{4,3},{5,4},{6,5},{7,6},{9,8},{10,9},{11,10},{12... | collective-permute-start | bytes 786440 | tf_op jit(solution)/shard_map/while/body/eval_jaxpr/ppermute | solution.py:17
  110.7 16.7 %collective-permute-start.1 = (f32[4,64,256]{1,0,2:T(4,128)S(1)}, f32[4,64,256]{1,0,2:T(4,128)S(1)}, u32[]{:S(2)}, u32[]{:S(2)}) collective-permute-start(f32[4,64,256]{1,0,2:T(4,128)S(1)} %get-tuple-element.312), channel_id=1, source_target_pairs={{1,0},{2,1},{3,2},{4,3},{5,4},{6,5},{7,6},{9,8},{10,9},{11,10},{12... | collective-permute-start | bytes 786440 | tf_op jit(solution)/shard_map/while/body/eval_jaxpr/ppermute | solution.py:17
  113.3 16.3 %collective-permute-start = (f32[4,64,256]{1,0,2:T(4,128)S(1)}, f32[4,64,256]{1,0,2:T(4,128)}, u32[]{:S(2)}, u32[]{:S(2)}) collective-permute-start(f32[4,64,256]{1,0,2:T(4,128)S(1)} %get-tuple-element.311), channel_id=1, source_target_pairs={{0,1},{1,2},{2,3},{3,4},{4,5},{5,6},{6,7},{8,9},{9,10},{10,11},{11... | collective-permute-start | bytes 786440 | tf_op jit(solution)/shard_map/while/body/eval_jaxpr/ppermute | solution.py:16
  148.6 16.7 %collective-permute-start.1 = (f32[4,64,256]{1,0,2:T(4,128)S(1)}, f32[4,64,256]{1,0,2:T(4,128)S(1)}, u32[]{:S(2)}, u32[]{:S(2)}) collective-permute-start(f32[4,64,256]{1,0,2:T(4,128)S(1)} %get-tuple-element.312), channel_id=1, source_target_pairs={{1,0},{2,1},{3,2},{4,3},{5,4},{6,5},{7,6},{9,8},{10,9},{11,10},{12... | collective-permute-start | bytes 786440 | tf_op jit(solution)/shard_map/while/body/eval_jaxpr/ppermute | solution.py:17
  150.5 16.9 %collective-permute-start = (f32[4,64,256]{1,0,2:T(4,128)S(1)}, f32[4,64,256]{1,0,2:T(4,128)}, u32[]{:S(2)}, u32[]{:S(2)}) collective-permute-start(f32[4,64,256]{1,0,2:T(4,128)S(1)} %get-tuple-element.311), channel_id=1, source_target_pairs={{0,1},{1,2},{2,3},{3,4},{4,5},{5,6},{6,7},{8,9},{9,10},{10,11},{11... | collective-permute-start | bytes 786440 | tf_op jit(solution)/shard_map/while/body/eval_jaxpr/ppermute | solution.py:16
  186.4 16.7 %collective-permute-start.1 = (f32[4,64,256]{1,0,2:T(4,128)S(1)}, f32[4,64,256]{1,0,2:T(4,128)S(1)}, u32[]{:S(2)}, u32[]{:S(2)}) collective-permute-start(f32[4,64,256]{1,0,2:T(4,128)S(1)} %get-tuple-element.312), channel_id=1, source_target_pairs={{1,0},{2,1},{3,2},{4,3},{5,4},{6,5},{7,6},{9,8},{10,9},{11,10},{12... | collective-permute-start | bytes 786440 | tf_op jit(solution)/shard_map/while/body/eval_jaxpr/ppermute | solution.py:17
  188.3 16.9 %collective-permute-start = (f32[4,64,256]{1,0,2:T(4,128)S(1)}, f32[4,64,256]{1,0,2:T(4,128)}, u32[]{:S(2)}, u32[]{:S(2)}) collective-permute-start(f32[4,64,256]{1,0,2:T(4,128)S(1)} %get-tuple-element.311), channel_id=1, source_target_pairs={{0,1},{1,2},{2,3},{3,4},{4,5},{5,6},{6,7},{8,9},{9,10},{10,11},{11... | collective-permute-start | bytes 786440 | tf_op jit(solution)/shard_map/while/body/eval_jaxpr/ppermute | solution.py:16
  224.2 16.7 %collective-permute-start.1 = (f32[4,64,256]{1,0,2:T(4,128)S(1)}, f32[4,64,256]{1,0,2:T(4,128)S(1)}, u32[]{:S(2)}, u32[]{:S(2)}) collective-permute-start(f32[4,64,256]{1,0,2:T(4,128)S(1)} %get-tuple-element.312), channel_id=1, source_target_pairs={{1,0},{2,1},{3,2},{4,3},{5,4},{6,5},{7,6},{9,8},{10,9},{11,10},{12... | collective-permute-start | bytes 786440 | tf_op jit(solution)/shard_map/while/body/eval_jaxpr/ppermute | solution.py:17
  226.2 16.9 %collective-permute-start = (f32[4,64,256]{1,0,2:T(4,128)S(1)}, f32[4,64,256]{1,0,2:T(4,128)}, u32[]{:S(2)}, u32[]{:S(2)}) collective-permute-start(f32[4,64,256]{1,0,2:T(4,128)S(1)} %get-tuple-element.311), channel_id=1, source_target_pairs={{0,1},{1,2},{2,3},{3,4},{4,5},{5,6},{6,7},{8,9},{9,10},{10,11},{11... | collective-permute-start | bytes 786440 | tf_op jit(solution)/shard_map/while/body/eval_jaxpr/ppermute | solution.py:16
  262.1 16.7 %collective-permute-start.1 = (f32[4,64,256]{1,0,2:T(4,128)S(1)}, f32[4,64,256]{1,0,2:T(4,128)S(1)}, u32[]{:S(2)}, u32[]{:S(2)}) collective-permute-start(f32[4,64,256]{1,0,2:T(4,128)S(1)} %get-tuple-element.312), channel_id=1, source_target_pairs={{1,0},{2,1},{3,2},{4,3},{5,4},{6,5},{7,6},{9,8},{10,9},{11,10},{12... | collective-permute-start | bytes 786440 | tf_op jit(solution)/shard_map/while/body/eval_jaxpr/ppermute | solution.py:17
  264.0 16.9 %collective-permute-start = (f32[4,64,256]{1,0,2:T(4,128)S(1)}, f32[4,64,256]{1,0,2:T(4,128)}, u32[]{:S(2)}, u32[]{:S(2)}) collective-permute-start(f32[4,64,256]{1,0,2:T(4,128)S(1)} %get-tuple-element.311), channel_id=1, source_target_pairs={{0,1},{1,2},{2,3},{3,4},{4,5},{5,6},{6,7},{8,9},{9,10},{10,11},{11... | collective-permute-start | bytes 786440 | tf_op jit(solution)/shard_map/while/body/eval_jaxpr/ppermute | solution.py:16
  299.9 16.7 %collective-permute-start.1 = (f32[4,64,256]{1,0,2:T(4,128)S(1)}, f32[4,64,256]{1,0,2:T(4,128)S(1)}, u32[]{:S(2)}, u32[]{:S(2)}) collective-permute-start(f32[4,64,256]{1,0,2:T(4,128)S(1)} %get-tuple-element.312), channel_id=1, source_target_pairs={{1,0},{2,1},{3,2},{4,3},{5,4},{6,5},{7,6},{9,8},{10,9},{11,10},{12... | collective-permute-start | bytes 786440 | tf_op jit(solution)/shard_map/while/body/eval_jaxpr/ppermute | solution.py:17
  301.8 16.9 %collective-permute-start = (f32[4,64,256]{1,0,2:T(4,128)S(1)}, f32[4,64,256]{1,0,2:T(4,128)}, u32[]{:S(2)}, u32[]{:S(2)}) collective-permute-start(f32[4,64,256]{1,0,2:T(4,128)S(1)} %get-tuple-element.311), channel_id=1, source_target_pairs={{0,1},{1,2},{2,3},{3,4},{4,5},{5,6},{6,7},{8,9},{9,10},{10,11},{11... | collective-permute-start | bytes 786440 | tf_op jit(solution)/shard_map/while/body/eval_jaxpr/ppermute | solution.py:16
  337.8 16.7 %collective-permute-start.1 = (f32[4,64,256]{1,0,2:T(4,128)S(1)}, f32[4,64,256]{1,0,2:T(4,128)S(1)}, u32[]{:S(2)}, u32[]{:S(2)}) collective-permute-start(f32[4,64,256]{1,0,2:T(4,128)S(1)} %get-tuple-element.312), channel_id=1, source_target_pairs={{1,0},{2,1},{3,2},{4,3},{5,4},{6,5},{7,6},{9,8},{10,9},{11,10},{12... | collective-permute-start | bytes 786440 | tf_op jit(solution)/shard_map/while/body/eval_jaxpr/ppermute | solution.py:17
  339.7 16.9 %collective-permute-start = (f32[4,64,256]{1,0,2:T(4,128)S(1)}, f32[4,64,256]{1,0,2:T(4,128)}, u32[]{:S(2)}, u32[]{:S(2)}) collective-permute-start(f32[4,64,256]{1,0,2:T(4,128)S(1)} %get-tuple-element.311), channel_id=1, source_target_pairs={{0,1},{1,2},{2,3},{3,4},{4,5},{5,6},{6,7},{8,9},{9,10},{10,11},{11... | collective-permute-start | bytes 786440 | tf_op jit(solution)/shard_map/while/body/eval_jaxpr/ppermute | solution.py:16
  375.6 16.7 %collective-permute-start.1 = (f32[4,64,256]{1,0,2:T(4,128)S(1)}, f32[4,64,256]{1,0,2:T(4,128)S(1)}, u32[]{:S(2)}, u32[]{:S(2)}) collective-permute-start(f32[4,64,256]{1,0,2:T(4,128)S(1)} %get-tuple-element.312), channel_id=1, source_target_pairs={{1,0},{2,1},{3,2},{4,3},{5,4},{6,5},{7,6},{9,8},{10,9},{11,10},{12... | collective-permute-start | bytes 786440 | tf_op jit(solution)/shard_map/while/body/eval_jaxpr/ppermute | solution.py:17
  377.5 16.9 %collective-permute-start = (f32[4,64,256]{1,0,2:T(4,128)S(1)}, f32[4,64,256]{1,0,2:T(4,128)}, u32[]{:S(2)}, u32[]{:S(2)}) collective-permute-start(f32[4,64,256]{1,0,2:T(4,128)S(1)} %get-tuple-element.311), channel_id=1, source_target_pairs={{0,1},{1,2},{2,3},{3,4},{4,5},{5,6},{6,7},{8,9},{9,10},{10,11},{11... | collective-permute-start | bytes 786440 | tf_op jit(solution)/shard_map/while/body/eval_jaxpr/ppermute | solution.py:16
  413.4 16.7 %collective-permute-start.1 = (f32[4,64,256]{1,0,2:T(4,128)S(1)}, f32[4,64,256]{1,0,2:T(4,128)S(1)}, u32[]{:S(2)}, u32[]{:S(2)}) collective-permute-start(f32[4,64,256]{1,0,2:T(4,128)S(1)} %get-tuple-element.312), channel_id=1, source_target_pairs={{1,0},{2,1},{3,2},{4,3},{5,4},{6,5},{7,6},{9,8},{10,9},{11,10},{12... | collective-permute-start | bytes 786440 | tf_op jit(solution)/shard_map/while/body/eval_jaxpr/ppermute | solution.py:17
  415.4 16.9 %collective-permute-start = (f32[4,64,256]{1,0,2:T(4,128)S(1)}, f32[4,64,256]{1,0,2:T(4,128)}, u32[]{:S(2)}, u32[]{:S(2)}) collective-permute-start(f32[4,64,256]{1,0,2:T(4,128)S(1)} %get-tuple-element.311), channel_id=1, source_target_pairs={{0,1},{1,2},{2,3},{3,4},{4,5},{5,6},{6,7},{8,9},{9,10},{10,11},{11... | collective-permute-start | bytes 786440 | tf_op jit(solution)/shard_map/while/body/eval_jaxpr/ppermute | solution.py:16
  451.3 16.7 %collective-permute-start.1 = (f32[4,64,256]{1,0,2:T(4,128)S(1)}, f32[4,64,256]{1,0,2:T(4,128)S(1)}, u32[]{:S(2)}, u32[]{:S(2)}) collective-permute-start(f32[4,64,256]{1,0,2:T(4,128)S(1)} %get-tuple-element.312), channel_id=1, source_target_pairs={{1,0},{2,1},{3,2},{4,3},{5,4},{6,5},{7,6},{9,8},{10,9},{11,10},{12... | collective-permute-start | bytes 786440 | tf_op jit(solution)/shard_map/while/body/eval_jaxpr/ppermute | solution.py:17
  453.2 16.9 %collective-permute-start = (f32[4,64,256]{1,0,2:T(4,128)S(1)}, f32[4,64,256]{1,0,2:T(4,128)}, u32[]{:S(2)}, u32[]{:S(2)}) collective-permute-start(f32[4,64,256]{1,0,2:T(4,128)S(1)} %get-tuple-element.311), channel_id=1, source_target_pairs={{0,1},{1,2},{2,3},{3,4},{4,5},{5,6},{6,7},{8,9},{9,10},{10,11},{11... | collective-permute-start | bytes 786440 | tf_op jit(solution)/shard_map/while/body/eval_jaxpr/ppermute | solution.py:16
  489.1 16.7 %collective-permute-start.1 = (f32[4,64,256]{1,0,2:T(4,128)S(1)}, f32[4,64,256]{1,0,2:T(4,128)S(1)}, u32[]{:S(2)}, u32[]{:S(2)}) collective-permute-start(f32[4,64,256]{1,0,2:T(4,128)S(1)} %get-tuple-element.312), channel_id=1, source_target_pairs={{1,0},{2,1},{3,2},{4,3},{5,4},{6,5},{7,6},{9,8},{10,9},{11,10},{12... | collective-permute-start | bytes 786440 | tf_op jit(solution)/shard_map/while/body/eval_jaxpr/ppermute | solution.py:17
  491.0 16.9 %collective-permute-start = (f32[4,64,256]{1,0,2:T(4,128)S(1)}, f32[4,64,256]{1,0,2:T(4,128)}, u32[]{:S(2)}, u32[]{:S(2)}) collective-permute-start(f32[4,64,256]{1,0,2:T(4,128)S(1)} %get-tuple-element.311), channel_id=1, source_target_pairs={{0,1},{1,2},{2,3},{3,4},{4,5},{5,6},{6,7},{8,9},{9,10},{10,11},{11... | collective-permute-start | bytes 786440 | tf_op jit(solution)/shard_map/while/body/eval_jaxpr/ppermute | solution.py:16
  (63 other events, 174.3 us)
Sparse Core Ops, SparseCore 0:
  529.3 21.5 reduce-scatter.1
where the time goes:
time: 562 us; the launch traced here: 558 us
  other arithmetic  184 us (33%)
  waiting for transfers between devices  149 us (27%)
  local copies, waits for them, and re-layouts  85.5 us (15%)
  starting transfers between devices  70.2 us (12%)
  blocking collectives  51.9 us (9%)
  between operations  14.8 us (3%)
    ppermute x12, waiting for transfers between devices, extended_2(): after = lax.ppermute(leading, axis, down)  129 us
    add x12, other arithmetic, advance(): fresh = 2.0 * current - later + courant_sq * laplace_rim(extended)  122 us
    while x156, local copies, waits for them, and re-layouts  67.3 us
    ppermute x12, starting transfers between devices, extended_2(): before = lax.ppermute(last, axis, up)  44.7 us
    concatenate x12, other arithmetic, extended_2(): shard = jnp.concatenate([before, shard, after], axis=dim)  28.2 us
    ppermute x12, starting transfers between devices, extended_2(): after = lax.ppermute(leading, axis, down)  25.4 us
    reduce_scatter x1, waiting for transfers between devices, shards(): lax.psum_scatter(gradient, 'shot', scatter_dimension=1, tiled=True)  20.5 us
    all_gather x1, blocking collectives, shards(): piece_traces = lax.all_gather(traces, 'space', axis=1, tiled=True)  19.3 us
  transfers between devices with their start and end apart: 25, of which 13 were waited for; matrix products, arithmetic and copies ran while one was open for 1% of the time, Pallas kernels for 0%

commit v1 on v0

v1 whole, which is shorter than its diff:
```python
import functools

import jax
import jax.numpy as jnp
from jax import lax
from jax.experimental import pallas as pl
from jax.experimental.pallas import tpu as pltpu
from jax.sharding import PartitionSpec as P

SCALE = 5040.0
TAPS = (8064.0, -1008.0, 128.0, -9.0)
CENTRE = 3.0 * (-205.0 / 72.0)

LIMIT = 40 * 1024 * 1024
VM = pltpu.VMEM
F32 = jnp.float32
BF16 = jnp.bfloat16


def vmem(x):
    return pltpu.with_memory_space_constraint(x, VM)


def band(rows, cols, block):
    r = lax.broadcasted_iota(jnp.int32, (rows, cols), 0)
    c = lax.broadcasted_iota(jnp.int32, (rows, cols), 1)
    r = r % cols
    c = c % rows
    gap = jnp.abs(r - c)
    out = jnp.zeros((rows, cols), F32)
    for j, w in enumerate(TAPS):
        out = jnp.where(gap == j + 1, w, out)
    return jnp.where(r // block == c // block, out, 0.0).astype(BF16)


def advance(src, so, prev, po, dst, do, a_ref, c_ref, q_ref, wz_ref, wy_ref, start, groups, k, extra=None):
    ny, nz = src.shape[1], src.shape[2]
    half = q_ref.shape[2]
    lane = lax.broadcasted_iota(jnp.int32, (ny, half), 1)
    for g in range(groups):
        t = start + 4 * g
        v = src[t + so : t + so + 4].reshape(4 * ny, nz)
        hi = v.astype(BF16)
        lo = (v - hi.astype(F32)).astype(BF16)
        s = jnp.dot(jnp.concatenate([hi, lo], 1), wz_ref[...], preferred_element_type=F32)
        s = s + jnp.dot(wy_ref[...], jnp.concatenate([hi, lo], 0), preferred_element_type=F32)
        for i in range(4):
            p = t + i
            total = s[i * ny : (i + 1) * ny]
            for j, w in enumerate(TAPS):
                total = total + w * (src[p + so + j + 1] + src[p + so - j - 1])
            fresh = a_ref[p + 4] * src[p + so] - prev[p + po] + c_ref[p + 4] * total
            x = p + 4
            shift = (2 - ((x % 8) * 16 + k)) % half
            q = q_ref[x // 8]
            q = jnp.where(lane == 2, pltpu.roll(q, shift, 1), 0.0)
            fresh = jnp.concatenate([fresh[:, :half] + q, fresh[:, half:]], 1)
            dst[p + do] = fresh
            if extra is not None:
                extra[p - start] = fresh


def local_of(scal_ref, y, p, length):
    g = y * length + p
    odd = scal_ref[1]
    return jnp.where(odd == 1, 2 * length - 1 - g, g)


def q_kernel(scal_ref, gathered_ref, q_ref, *, steps, length):
    n, rows, width = gathered_ref.shape
    across = q_ref.shape[1]
    level, odd = scal_ref[0], scal_ref[1]
    x_iota = lax.broadcasted_iota(jnp.int32, (8, 16, width), 0)
    y_iota = lax.broadcasted_iota(jnp.int32, (across, width), 0)

    def body(b, acc):
        block = gathered_ref[b]
        code = block[steps : steps + 1].astype(jnp.int32)
        gx = code // across
        y = code - gx * across
        gx = gx - level * (2 * length)
        x = jnp.where(odd == 1, 2 * length - 1 - gx, gx) + 4
        one_y = jnp.where(y_iota == y, 1.0, 0.0).astype(BF16)
        out = []
        for j in range(3):
            t = jnp.where(x_iota + 8 * j == x[None], block[None], 0.0).reshape(8 * 16, width)
            hi = t.astype(BF16)
            lo = (t - hi.astype(F32)).astype(BF16)
            dims = (((1,), (1,)), ((), ()))
            o = lax.dot_general(one_y, hi, dims, preferred_element_type=F32)
            o = o + lax.dot_general(one_y, lo, dims, preferred_element_type=F32)
            out.append(acc[j] + o)
        return tuple(out)

    zero = jnp.zeros(q_ref.shape[1:], F32)
    acc = lax.fori_loop(0, n, body, (zero, zero, zero))
    for j in range(3):
        q_ref[j] = acc[j]


def init_kernel(scal_ref, cur_own, cur_oth, lat_own, lat_oth, c_own, c_oth,
                e_ref, o_ref, a_ref, c_ref, wz_ref, wy_ref, send_a, send_b):
    length, ny, nz = cur_own.shape
    y = scal_ref[2]
    for p in range(length):
        for who, cur, lat, cou in ((y, cur_own, lat_own, c_own), (1 - y, cur_oth, lat_oth, c_oth)):
            j = local_of(scal_ref, who, p, length)
            e_ref[j + 8] = cur[p]
            o_ref[j + 4] = lat[p]
            cv = cou[p]
            c_ref[j + 4] = cv * (1.0 / SCALE)
            a_ref[j + 4] = 2.0 + CENTRE * cv
    send_a[0:8] = e_ref[16:24]
    send_a[8:12] = o_ref[16:20]
    send_a[12:16] = c_ref[16:20]
    send_b[0:8] = e_ref[8:16]
    send_b[8:12] = o_ref[4:8]
    send_b[12:16] = c_ref[4:8]
    wz_ref[...] = band(2 * nz, nz, nz)
    wy_ref[...] = band(4 * ny, 8 * ny, ny)


def inner_kernel(scal_ref, e_ref, o_in, a_ref, c_ref, q_ref, wz_ref, wy_ref, f_ref, g_in, o_ref, g_ref, *, r, length):
    y = scal_ref[2]
    if r > 0:
        for p in range(length):
            j = local_of(scal_ref, y, p, length)
            add = o_ref[j + 4] * f_ref[2 * r - 2, p].astype(F32) + e_ref[j + 8] * f_ref[2 * r - 1, p].astype(F32)
            g_ref[p] = add if r == 1 else g_ref[p] + add
    advance(e_ref, 8, o_ref, 4, o_ref, 4, a_ref, c_ref, q_ref, wz_ref, wy_ref, 4, 2, 2 * r)


def side_kernel(recv, e_in, o_in, a_in, c_in, q_ref, wz_ref, wy_ref, *outs, r, side, first):
    if first:
        e_ref, o_ref, a_ref, c_ref, new = outs
    else:
        e_ref, o_ref, new = outs
        a_ref, c_ref = a_in, c_in
    for i in range(8):
        if side == "a":
            e_ref[24 + i] = recv[7 - i]
        else:
            e_ref[7 - i] = recv[i]
    if first:
        for i in range(4):
            if side == "a":
                to, at = 20 + i, 3 - i
            else:
                to, at = 3 - i, i
            o_ref[to] = recv[8 + at]
            cv = recv[12 + at]
            c_ref[to] = cv
            a_ref[to] = 2.0 + (CENTRE * SCALE) * cv
    args = (a_ref, c_ref, q_ref, wz_ref, wy_ref)
    advance(e_ref, 8, o_ref, 4, o_ref, 4, *args, 12 if side == "a" else -4, 2, 2 * r)
    advance(o_ref, 4, e_ref, 8, e_ref, 8, *args, 8 if side == "a" else 0, 2, 2 * r + 1, extra=new)


def final_kernel(scal_ref, e_ref, o_ref, f_ref, g_in, field_ref, g_ref, *, steps):
    length = field_ref.shape[0]
    y = scal_ref[2]
    for p in range(length):
        j = local_of(scal_ref, y, p, length)
        last = e_ref[j + 8]
        field_ref[p] = last
        g_ref[p] = g_in[p] + o_ref[j + 4] * f_ref[steps - 2, p].astype(F32) + last * f_ref[steps - 1, p].astype(F32)


def call(kernel, out_shapes, args, aliases=None, flops=0, name=None):
    smem = pl.BlockSpec(memory_space=pltpu.SMEM)
    vm = pl.BlockSpec(memory_space=VM)
    specs = [smem if a.dtype == jnp.int32 and a.ndim == 1 else vm for a in args]
    args = [a if s is smem else vmem(a) for a, s in zip(args, specs)]
    return pl.pallas_call(
        kernel,
        out_shape=out_shapes,
        in_specs=specs,
        out_specs=jax.tree.map(lambda _: vm, out_shapes),
        input_output_aliases=aliases or {},
        compiler_params=pltpu.CompilerParams(vmem_limit_bytes=LIMIT),
        cost_estimate=pl.CostEstimate(flops=flops, bytes_accessed=1 << 20, transcendentals=0),
        name=name,
    )(*args)


def shards(residual_traces, owners, surface_cells, trace_counts, start_current, start_later, forward_accel, courant_sq):
    traces = residual_traces[0]
    forward = forward_accel[0]
    cur, later = start_current[0], start_later[0]
    length, ny, nz = courant_sq.shape
    steps, width = traces.shape
    n = lax.axis_size("space")
    levels = n // 2
    me = lax.axis_index("space")
    level = me // 2
    scal = jnp.stack([level, level % 2, me % 2, me * 0]).astype(jnp.int32)

    def pairs(low_levels):
        out = []
        for lv in low_levels:
            for y in range(2):
                lo, hi = 2 * lv + y, 2 * lv + 2 + y
                out += [(lo, hi), (hi, lo)]
        return out

    swap_y = [(i, i ^ 1) for i in range(n)]
    swap_a = pairs(range(0, levels - 1, 2))
    swap_b = pairs(range(1, levels - 1, 2))

    number = me * width + jnp.arange(width, dtype=jnp.int32)
    live = jnp.where(number < trace_counts[0], 1.0, 0.0)
    code = (owners[0, :, 0] * (length * ny) + surface_cells[0]).astype(F32)
    payload = jnp.concatenate([traces * live[None], code[None], jnp.zeros((16 - steps - 1, width), F32)], 0)
    gathered = lax.all_gather(payload, "space", axis=0)

    cur_oth = lax.ppermute(cur, "space", swap_y)
    lat_oth = lax.ppermute(later, "space", swap_y)
    c_oth = lax.ppermute(courant_sq, "space", swap_y)

    plane = lambda k: VM((k, ny, nz), F32)
    e, o, a, c, wz, wy, send_a, send_b = call(
        init_kernel,
        [plane(32), plane(24), plane(24), plane(24), VM((2 * nz, nz), BF16), VM((4 * ny, 8 * ny), BF16),
         plane(16), plane(16)],
        [scal, cur, cur_oth, later, lat_oth, courant_sq, c_oth],
        name="init",
    )
    q = call(
        functools.partial(q_kernel, steps=steps, length=length),
        VM((3, ny, 128), F32),
        [scal, gathered],
        name="receivers",
    )
    g = None
    work = 2 * 16 * ny * nz * 60
    for r in range(steps // 2):
        recv_a = lax.ppermute(send_a, "space", swap_a)
        recv_b = lax.ppermute(send_b, "space", swap_b)
        if g is None:
            g = jnp.zeros((length, ny, nz), F32)
        o, g = call(
            functools.partial(inner_kernel, r=r, length=length),
            [plane(24), plane(length)],
            [scal, e, o, a, c, q, wz, wy, forward, g],
            {2: 0, 9: 1},
            flops=work,
            name=f"inner{r}",
        )
        for side in "ab":
            recv = recv_a if side == "a" else recv_b
            first = r == 0
            kern = functools.partial(side_kernel, r=r, side=side, first=first)
            if first:
                e, o, a, c, new = call(
                    kern, [plane(32), plane(24), plane(24), plane(24), plane(8)],
                    [recv, e, o, a, c, q, wz, wy], {1: 0, 2: 1, 3: 2, 4: 3}, flops=work, name=f"side_{side}{r}")
            else:
                e, o, new = call(
                    kern, [plane(32), plane(24), plane(8)],
                    [recv, e, o, a, c, q, wz, wy], {1: 0, 2: 1}, flops=work, name=f"side_{side}{r}")
            if side == "a":
                send_a = new
            else:
                send_b = new

    field, g = call(
        functools.partial(final_kernel, steps=steps),
        [plane(length), plane(length)],
        [scal, e, o, forward, g],
        name="final",
    )
    shot = lax.axis_index("shot")
    sx, sc = shot // 2, shot % 2
    part = ny // 4
    quarters = g.reshape(length, 2, 2, part, nz)
    give = lax.dynamic_index_in_dim(quarters, 1 - sc, 2, keepdims=False)
    keep = lax.dynamic_index_in_dim(quarters, sc, 2, keepdims=False)
    keep = keep + lax.ppermute(give, "shot", [(0, 1), (1, 0), (2, 3), (3, 2)])
    give = lax.dynamic_index_in_dim(keep, 1 - sx, 1, keepdims=False)
    mine = lax.dynamic_index_in_dim(keep, sx, 1, keepdims=False)
    grad = mine + lax.ppermute(give, "shot", [(0, 2), (2, 0), (1, 3), (3, 1)])
    return field[None], grad


def solution(mesh):
    placed = (
        P("shot", None, "space"),
        P("shot", "space", None),
        P("shot", "space"),
        P("shot"),
        P("shot", "space", None, None),
        P("shot", "space", None, None),
        P("shot", None, "space", None, None),
        P("space", None, None),
    )
    return jax.shard_map(
        shards,
        mesh=mesh,
        in_specs=placed,
        out_specs=(P("shot", "space", None, None), P("space", "shot", None)),
        check_vma=False,
    )
```

time: 562 us -> 212 us (0.38)
  other arithmetic: 184 us -> 1.83 us
  waiting for transfers between devices: 149 us -> 56.2 us
  local copies, waits for them, and re-layouts: 85.5 us -> 25.6 us
  Pallas kernels: 0 us -> 41.7 us
  starting transfers between devices: 70.2 us -> 41.4 us
  between operations: 14.8 us -> 1.64 us
  blocking collectives: 51.9 us -> 42.4 us
    add x24 -> x2, other arithmetic: 140 us -> 1.66 us  [the longest x1 0.99 us: shards(): keep = keep + lax.ppermute(give, 'shot', [(0, 1), (1, 0), (2, 3), (3, 2)])]
    ppermute x24 -> x17, waiting for transfers between devices: 129 us -> 56.2 us  [the longest x1 11.4 us: shards(): cur_oth = lax.ppermute(cur, 'space', swap_y)]
    while x158 -> x0, local copies, waits for them, and re-layouts: 70.8 us -> none
    pallas_call x0 -> x21, Pallas kernels: none -> 41.7 us  [call(): pl.pallas_call(kernel, out_shape=out_shapes, in_specs=specs, out_specs=ja...]
    ppermute x24 -> x17, starting transfers between devices: 70.1 us -> 41.4 us  [the longest x6 23.4 us: shards(): recv_b = lax.ppermute(send_b, 'space', swap_b)]
    concatenate x12 -> x1, other arithmetic: 28.2 us -> 0.07 us  [shards(): jnp.concatenate([traces * live[None], code[None], jnp.zeros((16 - steps -...]
    reduce_scatter x1 -> x0, waiting for transfers between devices: 20.5 us -> none  [shards(): lax.psum_scatter(gradient, 'shot', scatter_dimension=1, tiled=True)]
    scatter-add x12 -> x0, other arithmetic: 15.1 us -> none  [advance(): fresh.at[:, :, 2]]
  transfers between devices with their start and end apart: 25 -> 17, of which waited for: 13 -> 13; matrix products, arithmetic and copies ran while one was open for 1% -> 1% of each run, Pallas kernels for 0% -> 16%
where the time goes in v1:
time: 212 us; the launch traced here: 211 us
  waiting for transfers between devices  56.2 us (27%)
  blocking collectives  42.4 us (20%)
  Pallas kernels  41.7 us (20%)
  starting transfers between devices  41.4 us (20%)
  local copies, waits for them, and re-layouts  25.6 us (12%)
    all_gather x1, blocking collectives, shards(): gathered = lax.all_gather(payload, 'space', axis=0)  42.4 us
    pallas_call x21, Pallas kernels, call(): pl.pallas_call(kernel, out_shape=out_shapes, in_specs=specs, out_specs=ja...  41.7 us
    unnamed x53, local copies, waits for them, and re-layouts  24.5 us
    ppermute x6, starting transfers between devices, shards(): recv_b = lax.ppermute(send_b, 'space', swap_b)  23.4 us
    ppermute x6, starting transfers between devices, shards(): recv_a = lax.ppermute(send_a, 'space', swap_a)  12.8 us
    ppermute x1, waiting for transfers between devices, shards(): cur_oth = lax.ppermute(cur, 'space', swap_y)  11.4 us
    ppermute x1, waiting for transfers between devices, shards(): lat_oth = lax.ppermute(later, 'space', swap_y)  11.2 us
    ppermute x6, waiting for transfers between devices, shards(): recv_a = lax.ppermute(send_a, 'space', swap_a)  10.5 us
  transfers between devices with their start and end apart: 17, of which 13 were waited for; matrix products, arithmetic and copies ran while one was open for 1% of the time, Pallas kernels for 16%

profile of v1, /device:TPU:16, one launch (start us, length us, event | category | flops | bytes accessed | tf_op | source)
XLA Modules:
  0.0 210.7 jit_solution(9294505866834910908)
XLA Ops:
  4.3 11.4 %collective-permute-done.cur_oth = f32[8,64,256]{2,1,0:T(8,128)S(1)} collective-permute-done((f32[8,64,256]{2,1,0:T(8,128)}, f32[8,64,256]{2,1,0:T(8,128)S(1)}, u32[]{:S(2)}, u32[]{:S(2)}) %collective-permute-start) | collective-permute-done | bytes 524320 | tf_op jit(solution)/shard_map/ppermute | solution.py:216
  15.7 11.2 %collective-permute-done.1.lat_oth = f32[8,64,256]{2,1,0:T(8,128)S(1)} collective-permute-done((f32[8,64,256]{2,1,0:T(8,128)}, f32[8,64,256]{2,1,0:T(8,128)S(1)}, u32[]{:S(2)}, u32[]{:S(2)}) %collective-permute-start.1) | collective-permute-done | bytes 524320 | tf_op jit(solution)/shard_map/ppermute | solution.py:217
  27.7 9.3 %collective-permute-done.2.c_oth = f32[8,64,256]{2,1,0:T(8,128)S(1)} collective-permute-done((f32[8,64,256]{2,1,0:T(8,128)}, f32[8,64,256]{2,1,0:T(8,128)S(1)}, u32[]{:S(2)}, u32[]{:S(2)}) %collective-permute-start.2) | collective-permute-done | bytes 524320 | tf_op jit(solution)/shard_map/ppermute | solution.py:218
  43.1 2.3 %init.1 = (f32[32,64,256]{2,1,0:T(8,128)S(1)}, f32[24,64,256]{2,1,0:T(8,128)S(1)}, f32[24,64,256]{2,1,0:T(8,128)S(1)}, f32[24,64,256]{2,1,0:T(8,128)S(1)}, bf16[...) custom-call(s32[4]{0:T(128)S(1)} %pad_add_fusion.scal_ref, ...), custom_call_target="tpu_custom_call" | custom-call | bytes 1048576 | tf_op jit(solution)/shard_map/init/pallas_call | solution.py:174
  53.2 42.4 %all-gather = f32[128,256]{1,0:T(8,128)S(1)} all-gather(f32[16,256]{1,0:T(8,128)S(1)} %maximum_maximum_fusion), channel_id=2, replica_groups=mesh['shot'=4,'space'=8] {'space'}, dimensions={0}, use_global_device_ids=true | all-gather | bytes 147456 | tf_op jit(solution)/shard_map/all_gather | solution.py:214
  95.7 2.8 %receivers.1.q_ref = f32[3,64,128]{2,1,0:T(8,128)S(1)} custom-call(s32[4]{0:T(128)S(1)} %pad_add_fusion.scal_ref, f32[8,16,256]{2,1,0:T(8,128)S(1)} %bitcast.37), custom_call_target="tpu_custom_call" | custom-call | bytes 1048576 | tf_op jit(solution)/shard_map/receivers/pallas_call | solution.py:174
  105.9 2.7 %side_a0.1 = (f32[32,64,256]{2,1,0:T(8,128)S(1)}, f32[24,64,256]{2,1,0:T(8,128)S(1)}, f32[24,64,256]{2,1,0:T(8,128)S(1)}, f32[24,64,256]{2,1,0:T(8,128)S(1)}, f32[8,64,256]{2,1,0:T(8,128)S(1)}) custom-call(f32[16,64,256]{2,1,0:T(8,128)} %collective-permute-done.4.recv, ...), custom_call_target="tpu_custom_call", output_to_operand_aliasing={{0}: (1, {}), {1}: (2, {}), {2}: (3, {}), {3}: (4, {})} | custom-call | flops 31457280 | bytes 1048576 | tf_op jit(solution)/shard_map/side_a0/pallas_call | solution.py:174
  108.7 3.1 %collective-permute-start.6 = (f32[8,64,256]{2,1,0:T(8,128)S(1)}, f32[8,64,256]{2,1,0:T(8,128)S(1)}, u32[]{:S(2)}, u32[]{:S(2)}) collective-permute-start(f32[8,64,256]{2,1,0:T(8,128)S(1)} %get-tuple-element.76), channel_id=1, source_target_pairs={{0,2},{2,0},{1,3},{3,1},{4,6},{6,4},{5,7},{7,5},{8,10},{10,8},{9,1... | collective-permute-start | bytes 1572872 | tf_op jit(solution)/shard_map/ppermute | solution.py:237
  111.8 2.9 %side_b0.1 = (f32[32,64,256]{2,1,0:T(8,128)S(1)}, f32[24,64,256]{2,1,0:T(8,128)S(1)}, f32[24,64,256]{2,1,0:T(8,128)S(1)}, f32[24,64,256]{2,1,0:T(8,128)S(1)}, f32[8,64,256]{2,1,0:T(8,128)S(1)}) custom-call(f32[16,64,256]{2,1,0:T(8,128)} %collective-permute-done.3.recv, ...), custom_call_target="tpu_custom_call", output_to_operand_aliasing={{0}: (1, {}), {1}: (2, {}), {2}: (3, {}), {3}: (4, {})} | custom-call | flops 31457280 | bytes 1048576 | tf_op jit(solution)/shard_map/side_b0/pallas_call | solution.py:174
  114.7 4.3 %collective-permute-start.5 = (f32[8,64,256]{2,1,0:T(8,128)S(1)}, f32[8,64,256]{2,1,0:T(8,128)S(1)}, u32[]{:S(2)}, u32[]{:S(2)}) collective-permute-start(f32[8,64,256]{2,1,0:T(8,128)S(1)} %get-tuple-element.75), channel_id=1, source_target_pairs={{2,4},{4,2},{3,5},{5,3},{10,12},{12,10},{11,13},{13,11},{18,20},{2... | collective-permute-start | bytes 1572872 | tf_op jit(solution)/shard_map/ppermute | solution.py:238
  124.1 2.5 %collective-permute-start.8 = (f32[8,64,256]{2,1,0:T(8,128)S(1)}, f32[8,64,256]{2,1,0:T(8,128)S(1)}, u32[]{:S(2)}, u32[]{:S(2)}) collective-permute-start(f32[8,64,256]{2,1,0:T(8,128)S(1)} %get-tuple-element.86), channel_id=1, source_target_pairs={{0,2},{2,0},{1,3},{3,1},{4,6},{6,4},{5,7},{7,5},{8,10},{10,8},{9,1... | collective-permute-start | bytes 1572872 | tf_op jit(solution)/shard_map/ppermute | solution.py:237
  130.0 4.4 %collective-permute-start.7 = (f32[8,64,256]{2,1,0:T(8,128)S(1)}, f32[8,64,256]{2,1,0:T(8,128)S(1)}, u32[]{:S(2)}, u32[]{:S(2)}) collective-permute-start(f32[8,64,256]{2,1,0:T(8,128)S(1)} %get-tuple-element.85), channel_id=1, source_target_pairs={{2,4},{4,2},{3,5},{5,3},{10,12},{12,10},{11,13},{13,11},{18,20},{2... | collective-permute-start | bytes 1572872 | tf_op jit(solution)/shard_map/ppermute | solution.py:238
  135.9 2.9 %collective-permute-done.8.recv = f32[8,64,256]{2,1,0:T(8,128)S(1)} collective-permute-done((f32[8,64,256]{2,1,0:T(8,128)S(1)}, f32[8,64,256]{2,1,0:T(8,128)S(1)}, u32[]{:S(2)}, u32[]{:S(2)}) %collective-permute-start.8) | collective-permute-done | bytes 524320 | tf_op jit(solution)/shard_map/ppermute | solution.py:237
  140.4 2.4 %collective-permute-start.10 = (f32[8,64,256]{2,1,0:T(8,128)S(1)}, f32[8,64,256]{2,1,0:T(8,128)S(1)}, u32[]{:S(2)}, u32[]{:S(2)}) collective-permute-start(f32[8,64,256]{2,1,0:T(8,128)S(1)} %get-tuple-element.94), channel_id=1, source_target_pairs={{0,2},{2,0},{1,3},{3,1},{4,6},{6,4},{5,7},{7,5},{8,10},{10,8},{9,1... | collective-permute-start | bytes 1572872 | tf_op jit(solution)/shard_map/ppermute | solution.py:237
  146.1 4.2 %collective-permute-start.9 = (f32[8,64,256]{2,1,0:T(8,128)S(1)}, f32[8,64,256]{2,1,0:T(8,128)S(1)}, u32[]{:S(2)}, u32[]{:S(2)}) collective-permute-start(f32[8,64,256]{2,1,0:T(8,128)S(1)} %get-tuple-element.93), channel_id=1, source_target_pairs={{2,4},{4,2},{3,5},{5,3},{10,12},{12,10},{11,13},{13,11},{18,20},{2... | collective-permute-start | bytes 1572872 | tf_op jit(solution)/shard_map/ppermute | solution.py:238
  151.8 3.2 %collective-permute-done.10.recv = f32[8,64,256]{2,1,0:T(8,128)S(1)} collective-permute-done((f32[8,64,256]{2,1,0:T(8,128)S(1)}, f32[8,64,256]{2,1,0:T(8,128)S(1)}, u32[]{:S(2)}, u32[]{:S(2)}) %collective-permute-start.10) | collective-permute-done | bytes 524320 | tf_op jit(solution)/shard_map/ppermute | solution.py:237
  158.3 3.1 %collective-permute-done.9.recv = f32[8,64,256]{2,1,0:T(8,128)S(1)} collective-permute-done((f32[8,64,256]{2,1,0:T(8,128)S(1)}, f32[8,64,256]{2,1,0:T(8,128)S(1)}, u32[]{:S(2)}, u32[]{:S(2)}) %collective-permute-start.9) | collective-permute-done | bytes 524320 | tf_op jit(solution)/shard_map/ppermute | solution.py:238
  162.9 4.2 %collective-permute-start.11 = (f32[8,64,256]{2,1,0:T(8,128)S(1)}, f32[8,64,256]{2,1,0:T(8,128)S(1)}, u32[]{:S(2)}, u32[]{:S(2)}) collective-permute-start(f32[8,64,256]{2,1,0:T(8,128)S(1)} %get-tuple-element.101), channel_id=1, source_target_pairs={{2,4},{4,2},{3,5},{5,3},{10,12},{12,10},{11,13},{13,11},{18,20},{2... | collective-permute-start | bytes 1572872 | tf_op jit(solution)/shard_map/ppermute | solution.py:238
  171.0 2.3 %side_a4.1 = (f32[32,64,256]{2,1,0:T(8,128)S(1)}, f32[24,64,256]{2,1,0:T(8,128)S(1)}, f32[8,64,256]{2,1,0:T(8,128)}) custom-call(f32[8,64,256]{2,1,0:T(8,128)S(1)} %collective-permute-done.12.recv, f32[32,64,256]{2,1,0:T(8,128)S(1)} %get-tuple-element.103.e_ref.e_in, ...), custom_call_target="tpu_custom_call", output_to_operand_aliasing={{0}: (1, {}), {1}: (2, {})} | custom-call | flops 31457280 | bytes 1048576 | tf_op jit(solution)/shard_map/side_a4/pallas_call | solution.py:174
  177.0 2.3 %side_b4.1 = (f32[32,64,256]{2,1,0:T(8,128)S(1)}, f32[24,64,256]{2,1,0:T(8,128)S(1)}, f32[8,64,256]{2,1,0:T(8,128)}) custom-call(f32[8,64,256]{2,1,0:T(8,128)S(1)} %collective-permute-done.11.recv, f32[32,64,256]{2,1,0:T(8,128)S(1)} %get-tuple-element.107.e_in, ...), custom_call_target="tpu_custom_call", output_to_operand_aliasing={{0}: (1, {}), {1}: (2, {})} | custom-call | flops 31457280 | bytes 1048576 | tf_op jit(solution)/shard_map/side_b4/pallas_call | solution.py:174
  180.4 4.4 %collective-permute-start.13 = (f32[8,64,256]{2,1,0:T(8,128)}, f32[8,64,256]{2,1,0:T(8,128)}, u32[]{:S(2)}, u32[]{:S(2)}) collective-permute-start(f32[8,64,256]{2,1,0:T(8,128)} %get-tuple-element.109), channel_id=1, source_target_pairs={{2,4},{4,2},{3,5},{5,3},{10,12},{12,10},{11,13},{13,11},{18,20},{2... | collective-permute-start | bytes 1572872 | tf_op jit(solution)/shard_map/ppermute | solution.py:238
  192.5 3.4 %side_a5.1 = (f32[32,64,256]{2,1,0:T(8,128)S(1)}, f32[24,64,256]{2,1,0:T(8,128)S(1)}, f32[8,64,256]{2,1,0:T(8,128)}) custom-call(f32[8,64,256]{2,1,0:T(8,128)} %collective-permute-done.14.recv, f32[32,64,256]{2,1,0:T(8,128)S(1)} %get-tuple-element.111.e_ref.e_in, ...), custom_call_target="tpu_custom_call", output_to_operand_aliasing={{0}: (1, {}), {1}: (2, {})} | custom-call | flops 31457280 | bytes 1048576 | tf_op jit(solution)/shard_map/side_a5/pallas_call | solution.py:174
  195.9 3.5 %side_b5.1 = (f32[32,64,256]{2,1,0:T(8,128)S(1)}, f32[24,64,256]{2,1,0:T(8,128)S(1)}, f32[8,64,256]{2,1,0:T(8,128)}) custom-call(f32[8,64,256]{2,1,0:T(8,128)} %collective-permute-done.13.recv, f32[32,64,256]{2,1,0:T(8,128)S(1)} %get-tuple-element.115.e_in, ...), custom_call_target="tpu_custom_call", output_to_operand_aliasing={{0}: (1, {}), {1}: (2, {})} | custom-call | flops 31457280 | bytes 1048576 | tf_op jit(solution)/shard_map/side_b5/pallas_call | solution.py:174
  206.7 3.3 %collective-permute-done.16 = f32[8,16,256]{2,1,0:T(8,128)S(1)} collective-permute-done((f32[8,16,256]{2,1,0:T(8,128)S(1)}, f32[8,16,256]{2,1,0:T(8,128)S(1)}, u32[]{:S(2)}, u32[]{:S(2)}) %collective-permute-start.16) | collective-permute-done | bytes 131104 | tf_op jit(solution)/shard_map/ppermute | solution.py:281
  (97 shorter events, 70.4 us)
Async XLA Ops:
  0.6 15.1 %collective-permute-start = (f32[8,64,256]{2,1,0:T(8,128)}, f32[8,64,256]{2,1,0:T(8,128)S(1)}, u32[]{:S(2)}, u32[]{:S(2)}) collective-permute-start(f32[8,64,256]{2,1,0:T(8,128)} %bitcast.38), channel_id=1, source_target_pairs={{0,1},{1,0},{2,3},{3,2},{4,5},{5,4},{6,7},{7,6},{8,9},{9,8},{10,11... | collective-permute-start | bytes 1572872 | tf_op jit(solution)/shard_map/ppermute | solution.py:216
  2.2 24.7 %collective-permute-start.1 = (f32[8,64,256]{2,1,0:T(8,128)}, f32[8,64,256]{2,1,0:T(8,128)S(1)}, u32[]{:S(2)}, u32[]{:S(2)}) collective-permute-start(f32[8,64,256]{2,1,0:T(8,128)} %bitcast.40), channel_id=1, source_target_pairs={{0,1},{1,0},{2,3},{3,2},{4,5},{5,4},{6,7},{7,6},{8,9},{9,8},{10,11... | collective-permute-start | bytes 1572872 | tf_op jit(solution)/shard_map/ppermute | solution.py:217
  2.7 34.3 %collective-permute-start.2 = (f32[8,64,256]{2,1,0:T(8,128)}, f32[8,64,256]{2,1,0:T(8,128)S(1)}, u32[]{:S(2)}, u32[]{:S(2)}) collective-permute-start(f32[8,64,256]{2,1,0:T(8,128)} %c_own.1), channel_id=1, source_target_pairs={{0,1},{1,0},{2,3},{3,2},{4,5},{5,4},{6,7},{7,6},{8,9},{9,8},{10,11... | collective-permute-start | bytes 1572872 | tf_op jit(solution)/shard_map/ppermute | solution.py:218
  4.2 48.9 %copy-start.24 = (s32[1,256]{1,0:T(1,128)S(1)}, s32[1,256]{1,0:T(1,128)}, u32[]{:S(2)}) copy-start(s32[1,256]{1,0:T(1,128)} %param.10) | copy-start | bytes 3076
  4.2 48.9 %copy-start.25 = (s32[1,256,1]{1,2,0:T(1,128)S(1)}, s32[1,256,1]{1,2,0:T(1,128)}, u32[]{:S(2)}) copy-start(s32[1,256,1]{1,2,0:T(1,128)} %param.9) | copy-start | bytes 3076
  43.1 10.1 %copy-start.23 = (f32[1,12,256]{2,0,1:T(1,128)S(1)}, f32[1,12,256]{2,0,1:T(1,128)}, u32[]{:S(2)}) copy-start(f32[1,12,256]{2,0,1:T(1,128)} %param.8) | copy-start | bytes 36868
  48.9 57.0 %collective-permute-start.4 = (f32[16,64,256]{2,1,0:T(8,128)}, f32[16,64,256]{2,1,0:T(8,128)}, u32[]{:S(2)}, u32[]{:S(2)}) collective-permute-start(f32[16,64,256]{2,1,0:T(8,128)} %get-tuple-element.63), channel_id=1, source_target_pairs={{0,2},{2,0},{1,3},{3,1},{4,6},{6,4},{5,7},{7,5},{8,10},{10,8},{9,1... | collective-permute-start | bytes 3145736 | tf_op jit(solution)/shard_map/ppermute | solution.py:237
  50.5 61.3 %collective-permute-start.3 = (f32[16,64,256]{2,1,0:T(8,128)}, f32[16,64,256]{2,1,0:T(8,128)}, u32[]{:S(2)}, u32[]{:S(2)}) collective-permute-start(f32[16,64,256]{2,1,0:T(8,128)} %get-tuple-element.62), channel_id=1, source_target_pairs={{2,4},{4,2},{3,5},{5,3},{10,12},{12,10},{11,13},{13,11},{18,20},{2... | collective-permute-start | bytes 3145736 | tf_op jit(solution)/shard_map/ppermute | solution.py:238
  108.7 13.9 %collective-permute-start.6 = (f32[8,64,256]{2,1,0:T(8,128)S(1)}, f32[8,64,256]{2,1,0:T(8,128)S(1)}, u32[]{:S(2)}, u32[]{:S(2)}) collective-permute-start(f32[8,64,256]{2,1,0:T(8,128)S(1)} %get-tuple-element.76), channel_id=1, source_target_pairs={{0,2},{2,0},{1,3},{3,1},{4,6},{6,4},{5,7},{7,5},{8,10},{10,8},{9,1... | collective-permute-start | bytes 1572872 | tf_op jit(solution)/shard_map/ppermute | solution.py:237
  111.8 7.2 %copy-start.13 = (bf16[1,12,8,64,256]{4,3,2,1,0:T(8,128)(2,1)S(1)}, bf16[1,12,8,64,256]{4,3,2,1,0:T(8,128)(2,1)}, u32[]{:S(2)}) copy-start(bf16[1,12,8,64,256]{4,3,2,1,0:T(8,128)(2,1)} %param.14) | copy-start | bytes 9437188
  114.7 62.3 %copy-start.6 = (f32[24,64,256]{2,1,0:T(8,128)}, f32[24,64,256]{2,1,0:T(8,128)S(1)}, u32[]{:S(2)}) copy-start(f32[24,64,256]{2,1,0:T(8,128)S(1)} %get-tuple-element.79.a_ref.a_in) | copy-start | bytes 4718596
  114.7 62.3 %copy-start.10 = (f32[24,64,256]{2,1,0:T(8,128)}, f32[24,64,256]{2,1,0:T(8,128)S(1)}, u32[]{:S(2)}) copy-start(f32[24,64,256]{2,1,0:T(8,128)S(1)} %get-tuple-element.80.c_ref.c_in) | copy-start | bytes 4718596
  114.7 13.8 %collective-permute-start.5 = (f32[8,64,256]{2,1,0:T(8,128)S(1)}, f32[8,64,256]{2,1,0:T(8,128)S(1)}, u32[]{:S(2)}, u32[]{:S(2)}) collective-permute-start(f32[8,64,256]{2,1,0:T(8,128)S(1)} %get-tuple-element.75), channel_id=1, source_target_pairs={{2,4},{4,2},{3,5},{5,3},{10,12},{12,10},{11,13},{13,11},{18,20},{2... | collective-permute-start | bytes 1572872 | tf_op jit(solution)/shard_map/ppermute | solution.py:238
  124.1 14.7 %collective-permute-start.8 = (f32[8,64,256]{2,1,0:T(8,128)S(1)}, f32[8,64,256]{2,1,0:T(8,128)S(1)}, u32[]{:S(2)}, u32[]{:S(2)}) collective-permute-start(f32[8,64,256]{2,1,0:T(8,128)S(1)} %get-tuple-element.86), channel_id=1, source_target_pairs={{0,2},{2,0},{1,3},{3,1},{4,6},{6,4},{5,7},{7,5},{8,10},{10,8},{9,1... | collective-permute-start | bytes 1572872 | tf_op jit(solution)/shard_map/ppermute | solution.py:237
  130.0 14.5 %collective-permute-start.7 = (f32[8,64,256]{2,1,0:T(8,128)S(1)}, f32[8,64,256]{2,1,0:T(8,128)S(1)}, u32[]{:S(2)}, u32[]{:S(2)}) collective-permute-start(f32[8,64,256]{2,1,0:T(8,128)S(1)} %get-tuple-element.85), channel_id=1, source_target_pairs={{2,4},{4,2},{3,5},{5,3},{10,12},{12,10},{11,13},{13,11},{18,20},{2... | collective-permute-start | bytes 1572872 | tf_op jit(solution)/shard_map/ppermute | solution.py:238
  140.4 14.6 %collective-permute-start.10 = (f32[8,64,256]{2,1,0:T(8,128)S(1)}, f32[8,64,256]{2,1,0:T(8,128)S(1)}, u32[]{:S(2)}, u32[]{:S(2)}) collective-permute-start(f32[8,64,256]{2,1,0:T(8,128)S(1)} %get-tuple-element.94), channel_id=1, source_target_pairs={{0,2},{2,0},{1,3},{3,1},{4,6},{6,4},{5,7},{7,5},{8,10},{10,8},{9,1... | collective-permute-start | bytes 1572872 | tf_op jit(solution)/shard_map/ppermute | solution.py:237
  146.1 15.3 %collective-permute-start.9 = (f32[8,64,256]{2,1,0:T(8,128)S(1)}, f32[8,64,256]{2,1,0:T(8,128)S(1)}, u32[]{:S(2)}, u32[]{:S(2)}) collective-permute-start(f32[8,64,256]{2,1,0:T(8,128)S(1)} %get-tuple-element.93), channel_id=1, source_target_pairs={{2,4},{4,2},{3,5},{5,3},{10,12},{12,10},{11,13},{13,11},{18,20},{2... | collective-permute-start | bytes 1572872 | tf_op jit(solution)/shard_map/ppermute | solution.py:238
  156.5 14.4 %collective-permute-start.12 = (f32[8,64,256]{2,1,0:T(8,128)S(1)}, f32[8,64,256]{2,1,0:T(8,128)S(1)}, u32[]{:S(2)}, u32[]{:S(2)}) collective-permute-start(f32[8,64,256]{2,1,0:T(8,128)S(1)} %get-tuple-element.102), channel_id=1, source_target_pairs={{0,2},{2,0},{1,3},{3,1},{4,6},{6,4},{5,7},{7,5},{8,10},{10,8},{9,1... | collective-permute-start | bytes 1572872 | tf_op jit(solution)/shard_map/ppermute | solution.py:237
  162.9 14.0 %collective-permute-start.11 = (f32[8,64,256]{2,1,0:T(8,128)S(1)}, f32[8,64,256]{2,1,0:T(8,128)S(1)}, u32[]{:S(2)}, u32[]{:S(2)}) collective-permute-start(f32[8,64,256]{2,1,0:T(8,128)S(1)} %get-tuple-element.101), channel_id=1, source_target_pairs={{2,4},{4,2},{3,5},{5,3},{10,12},{12,10},{11,13},{13,11},{18,20},{2... | collective-permute-start | bytes 1572872 | tf_op jit(solution)/shard_map/ppermute | solution.py:238
  173.3 19.2 %collective-permute-start.14 = (f32[8,64,256]{2,1,0:T(8,128)}, f32[8,64,256]{2,1,0:T(8,128)}, u32[]{:S(2)}, u32[]{:S(2)}) collective-permute-start(f32[8,64,256]{2,1,0:T(8,128)} %get-tuple-element.110), channel_id=1, source_target_pairs={{0,2},{2,0},{1,3},{3,1},{4,6},{6,4},{5,7},{7,5},{8,10},{10,8},{9,1... | collective-permute-start | bytes 1572872 | tf_op jit(solution)/shard_map/ppermute | solution.py:237
  180.4 15.4 %collective-permute-start.13 = (f32[8,64,256]{2,1,0:T(8,128)}, f32[8,64,256]{2,1,0:T(8,128)}, u32[]{:S(2)}, u32[]{:S(2)}) collective-permute-start(f32[8,64,256]{2,1,0:T(8,128)} %get-tuple-element.109), channel_id=1, source_target_pairs={{2,4},{4,2},{3,5},{5,3},{10,12},{12,10},{11,13},{13,11},{18,20},{2... | collective-permute-start | bytes 1572872 | tf_op jit(solution)/shard_map/ppermute | solution.py:238
  195.9 3.5 %copy-start.15 = (bf16[1,12,8,64,256]{4,3,2,1,0:T(8,128)(2,1)S(1)}, bf16[1,12,8,64,256]{4,3,2,1,0:T(8,128)(2,1)}, u32[]{:S(2)}) copy-start(bf16[1,12,8,64,256]{4,3,2,1,0:T(8,128)(2,1)} %param.14) | copy-start | bytes 9437188
  201.8 1.6 collective-permute-start.15
  204.5 5.6 %collective-permute-start.16 = (f32[8,16,256]{2,1,0:T(8,128)S(1)}, f32[8,16,256]{2,1,0:T(8,128)S(1)}, u32[]{:S(2)}, u32[]{:S(2)}) collective-permute-start(f32[8,16,256]{2,1,0:T(8,128)S(1)} %dynamic-slice_bitcast_fusion.1), channel_id=1, source_target_pairs={{0,16},{16,0},{8,24},{24,8},{1,17},{17,1},{9,25},{25,9},{2,18},{18... | collective-permute-start | bytes 393224 | tf_op jit(solution)/shard_map/ppermute | solution.py:281
  (19 other events, 23.7 us)

commit v2 on v1

v2 whole, which is shorter than its diff:
```python
import functools

import jax
import jax.numpy as jnp
from jax import lax
from jax.experimental import pallas as pl
from jax.experimental.pallas import tpu as pltpu
from jax.sharding import PartitionSpec as P

SCALE = 5040.0
TAPS = (8064.0, -1008.0, 128.0, -9.0)
CENTRE = 3.0 * (-205.0 / 72.0)

LIMIT = 8 * 1024 * 1024
VM = pltpu.VMEM
F32 = jnp.float32
BF16 = jnp.bfloat16


def vmem(x):
    return pltpu.with_memory_space_constraint(x, VM)


def band(rows, cols, block):
    r = lax.broadcasted_iota(jnp.int32, (rows, cols), 0)
    c = lax.broadcasted_iota(jnp.int32, (rows, cols), 1)
    r = r % cols
    c = c % rows
    gap = jnp.abs(r - c)
    out = jnp.zeros((rows, cols), F32)
    for j, w in enumerate(TAPS):
        out = jnp.where(gap == j + 1, w, out)
    return jnp.where(r // block == c // block, out, 0.0).astype(BF16)


def advance(src, so, prev, po, dst, do, a_ref, c_ref, q_ref, wz_ref, wy_ref, start, groups, k, extra=None):
    ny, nz = src.shape[1], src.shape[2]
    half = q_ref.shape[2]
    lane = lax.broadcasted_iota(jnp.int32, (ny, half), 1)
    for g in range(groups):
        t = start + 4 * g
        v = src[t + so : t + so + 4].reshape(4 * ny, nz)
        hi = v.astype(BF16)
        lo = (v - hi.astype(F32)).astype(BF16)
        s = jnp.dot(jnp.concatenate([hi, lo], 1), wz_ref[...], preferred_element_type=F32)
        s = s + jnp.dot(wy_ref[...], jnp.concatenate([hi, lo], 0), preferred_element_type=F32)
        for i in range(4):
            p = t + i
            total = s[i * ny : (i + 1) * ny]
            for j, w in enumerate(TAPS):
                total = total + w * (src[p + so + j + 1] + src[p + so - j - 1])
            fresh = a_ref[p + 4] * src[p + so] - prev[p + po] + c_ref[p + 4] * total
            x = p + 4
            shift = (2 - ((x % 8) * 16 + k)) % half
            q = q_ref[x // 8]
            q = jnp.where(lane == 2, pltpu.roll(q, shift, 1), 0.0)
            fresh = jnp.concatenate([fresh[:, :half] + q, fresh[:, half:]], 1)
            dst[p + do] = fresh
            if extra is not None:
                extra[p - start] = fresh


def local_of(scal_ref, g, length):
    return jnp.where(scal_ref[1] == 1, 2 * length - 1 - g, g)


def q_kernel(scal_ref, gathered_ref, q_ref, *, steps, length):
    n, rows, width = gathered_ref.shape
    across = q_ref.shape[1]
    level, odd = scal_ref[0], scal_ref[1]
    x_iota = lax.broadcasted_iota(jnp.int32, (8, 16, width), 0)
    y_iota = lax.broadcasted_iota(jnp.int32, (across, width), 0)

    def body(b, acc):
        block = gathered_ref[b]
        code = block[steps : steps + 1].astype(jnp.int32)
        gx = code // across
        y = code - gx * across
        gx = gx - level * (2 * length)
        x = jnp.where(odd == 1, 2 * length - 1 - gx, gx) + 4
        one_y = jnp.where(y_iota == y, 1.0, 0.0).astype(BF16)
        out = []
        for j in range(3):
            t = jnp.where(x_iota + 8 * j == x[None], block[None], 0.0).reshape(8 * 16, width)
            hi = t.astype(BF16)
            lo = (t - hi.astype(F32)).astype(BF16)
            dims = (((1,), (1,)), ((), ()))
            o = lax.dot_general(one_y, hi, dims, preferred_element_type=F32)
            o = o + lax.dot_general(one_y, lo, dims, preferred_element_type=F32)
            out.append(acc[j] + o)
        return tuple(out)

    zero = jnp.zeros(q_ref.shape[1:], F32)
    acc = lax.fori_loop(0, n, body, (zero, zero, zero))
    for j in range(3):
        q_ref[j] = acc[j]


def field_kernel(scal_ref, cur_own, cur_oth, lat_own, lat_edge, lat_rest, e_ref, o_ref, wz_ref, wy_ref):
    length, ny, nz = cur_own.shape
    half = length // 2
    y = scal_ref[2]
    for p in range(length):
        j = local_of(scal_ref, y * length + p, length)
        e_ref[j + 8] = cur_own[p]
        o_ref[j + 4] = lat_own[p]
        j = local_of(scal_ref, (1 - y) * length + p, length)
        e_ref[j + 8] = cur_oth[p]
    for p in range(half):
        j = local_of(scal_ref, (1 - y) * length + half * (1 - y) + p, length)
        o_ref[j + 4] = lat_edge[p]
        j = local_of(scal_ref, (1 - y) * length + half * y + p, length)
        o_ref[j + 4] = lat_rest[p]
    wz_ref[...] = band(2 * nz, nz, nz)
    wy_ref[...] = band(4 * ny, 8 * ny, ny)


def halo_at(scal_ref, upper, p, depth, length):
    g = jnp.where(upper == 1, 2 * length + p, p - depth)
    return local_of(scal_ref, g, length)


def model_kernel(scal_ref, c_own, c_oth, c_core, d_cur, d_edge, r_c, e_in, o_in, a_ref, c_ref, e_ref, o_ref):
    length = c_own.shape[0]
    half, two = length // 2, length // 4
    y, core = scal_ref[2], scal_ref[3]

    def put(j, cv):
        c_ref[j + 4] = cv * (1.0 / SCALE)
        a_ref[j + 4] = 2.0 + CENTRE * cv

    for p in range(length):
        put(local_of(scal_ref, y * length + p, length), c_own[p])
    base = (1 - y) * length
    for p in range(two):
        for who, piece, at in ((core, c_oth, 0), (1 - core, c_core, 0)):
            put(local_of(scal_ref, base + half * (1 - y) + two * who + p, length), piece[at + p])
            put(local_of(scal_ref, base + half * y + two * who + p, length), piece[at + two + p])
        put(halo_at(scal_ref, 1 - y, two * core + p, half, length), d_edge[half + p])
        put(halo_at(scal_ref, 1 - y, two * (1 - core) + p, half, length), c_core[half + p])
        put(halo_at(scal_ref, y, two * core + p, half, length), r_c[p])
        put(halo_at(scal_ref, y, two * (1 - core) + p, half, length), c_core[half + two + p])
    for p in range(length):
        e_ref[halo_at(scal_ref, 1 - y, p, length, length) + 8] = d_cur[p]
    for p in range(half):
        o_ref[halo_at(scal_ref, 1 - y, p, half, length) + 4] = d_edge[p]


def inner_kernel(scal_ref, e_ref, o_in, a_ref, c_ref, q_ref, wz_ref, wy_ref, f_ref, g_in, o_ref, g_ref, *, r, length):
    y = scal_ref[2]
    if r > 0:
        for p in range(length):
            j = local_of(scal_ref, y * length + p, length)
            add = o_ref[j + 4] * f_ref[2 * r - 2, p].astype(F32) + e_ref[j + 8] * f_ref[2 * r - 1, p].astype(F32)
            g_ref[p] = add if r == 1 else g_ref[p] + add
    advance(e_ref, 8, o_ref, 4, o_ref, 4, a_ref, c_ref, q_ref, wz_ref, wy_ref, 4, 2, 2 * r)


def side_steps(side, r, e_ref, o_ref, args, new):
    advance(e_ref, 8, o_ref, 4, o_ref, 4, *args, 12 if side == "a" else -4, 2, 2 * r)
    advance(o_ref, 4, e_ref, 8, e_ref, 8, *args, 8 if side == "a" else 0, 2, 2 * r + 1, extra=new)


def first_kernel(scal_ref, r_cur, r_lat, e_in, o_in, a_ref, c_ref, q_ref, wz_ref, wy_ref, e_ref, o_ref, new):
    length = r_cur.shape[0]
    y = scal_ref[2]
    for p in range(length):
        e_ref[halo_at(scal_ref, y, p, length, length) + 8] = r_cur[p]
    for p in range(length // 2):
        o_ref[halo_at(scal_ref, y, p, length // 2, length) + 4] = r_lat[p]
    side_steps("a", 0, e_ref, o_ref, (a_ref, c_ref, q_ref, wz_ref, wy_ref), new)


def side_kernel(scal_ref, *refs, r, side, recv, last):
    if recv:
        refs, recv_ref = refs[1:], refs[0]
    e_in, o_in, a_ref, c_ref, q_ref, wz_ref, wy_ref, e_ref, o_ref = refs[:9]
    new = None if last else refs[9]

    def work():
        if recv:
            for i in range(8):
                if side == "a":
                    e_ref[24 + i] = recv_ref[7 - i]
                else:
                    e_ref[7 - i] = recv_ref[i]
        side_steps(side, r, e_ref, o_ref, (a_ref, c_ref, q_ref, wz_ref, wy_ref), new)

    if last:
        own_a = (scal_ref[1] + scal_ref[2]) % 2
        pl.when(own_a == (1 if side == "a" else 0))(work)
    else:
        work()


def final_kernel(scal_ref, e_ref, o_ref, f_ref, g_in, field_ref, give_ref, keep_ref, *, steps):
    length, ny, _ = field_ref.shape
    y, core = scal_ref[2], scal_ref[3]
    part = ny // 4
    for p in range(length):
        j = local_of(scal_ref, y * length + p, length)
        last = e_ref[j + 8]
        field_ref[p] = last
        g = g_in[p] + o_ref[j + 4] * f_ref[steps - 2, p].astype(F32) + last * f_ref[steps - 1, p].astype(F32)
        for x in range(2):
            zero, one = g[2 * x * part : (2 * x + 1) * part], g[(2 * x + 1) * part : (2 * x + 2) * part]
            give_ref[p, x * part : (x + 1) * part] = jnp.where(core == 1, zero, one)
            keep_ref[p, x * part : (x + 1) * part] = jnp.where(core == 1, one, zero)


def pair_kernel(scal_ref, keep_ref, recv_ref, give_ref, mine_ref):
    x = scal_ref[4]
    part = give_ref.shape[1]
    for p in range(keep_ref.shape[0]):
        low = keep_ref[p, :part] + recv_ref[p, :part]
        high = keep_ref[p, part:] + recv_ref[p, part:]
        give_ref[p] = jnp.where(x == 1, low, high)
        mine_ref[p] = jnp.where(x == 1, high, low)


def call(kernel, out_shapes, args, aliases=None, free=(), flops=0, name=None):
    smem = pl.BlockSpec(memory_space=pltpu.SMEM)
    vm = pl.BlockSpec(memory_space=VM)
    specs = [smem if a.dtype == jnp.int32 and a.ndim == 1 else vm for a in args]
    args = [a if s is smem or i in free else vmem(a) for i, (a, s) in enumerate(zip(args, specs))]
    return pl.pallas_call(
        kernel,
        out_shape=out_shapes,
        in_specs=specs,
        out_specs=jax.tree.map(lambda _: vm, out_shapes),
        input_output_aliases=aliases or {},
        compiler_params=pltpu.CompilerParams(vmem_limit_bytes=LIMIT),
        cost_estimate=pl.CostEstimate(flops=flops, bytes_accessed=1 << 20, transcendentals=0),
        name=name,
    )(*args)


def shards(residual_traces, owners, surface_cells, trace_counts, start_current, start_later, forward_accel, courant_sq):
    traces = residual_traces[0]
    forward = forward_accel[0]
    cur, later = start_current[0], start_later[0]
    length, ny, nz = courant_sq.shape
    steps, width = traces.shape
    n, shots = lax.axis_size("space"), lax.axis_size("shot")
    levels = n // 2
    me, shot = lax.axis_index("space"), lax.axis_index("shot")
    level, y, core = me // 2, me % 2, shot % 2
    scal = jnp.stack([level, (level + core) % 2, y, core, shot // 2]).astype(jnp.int32)

    def move(x, pairs):
        return lax.ppermute(x, ("shot", "space"), pairs)

    def everywhere(space_pairs):
        return [(s * n + i, s * n + j) for s in range(shots) for i, j in space_pairs]

    def level_swap(parity):
        out = []
        for s in range(shots):
            for lv in range(levels - 1):
                if (lv + s) % 2 == parity:
                    for i in range(2):
                        lo = s * n + 2 * lv + i
                        out += [(lo, lo + 2), (lo + 2, lo)]
        return out

    swap_y = everywhere([(i, i ^ 1) for i in range(n)])
    down = [(2 * lv, 2 * lv - 2) for lv in range(1, levels)]
    up = [(2 * lv + 1, 2 * lv + 3) for lv in range(levels - 1)]
    direct = everywhere(down + up)
    relay = everywhere([(2 * lv, 2 * lv + 2) for lv in range(levels - 1)] + [(2 * lv + 1, 2 * lv - 1) for lv in range(1, levels)])
    swap_core = [(s * n + i, (s ^ 1) * n + i) for s in range(shots) for i in range(n)]
    swap_x = [(s * n + i, (s ^ 2) * n + i) for s in range(shots) for i in range(n)]
    swap_a, swap_b = level_swap(0), level_swap(1)

    half, two = length // 2, length // 4
    cut = lambda x, at, size: lax.dynamic_slice_in_dim(x, at, size, 0)
    y_cur = move(cur, swap_y)
    d_cur = move(cur, direct)
    c_edge = cut(courant_sq, half * y + two * core, two)
    c_rest = cut(courant_sq, half * (1 - y) + two * core, two)
    l_edge = cut(later, half * y, half)
    l_rest = cut(later, half * (1 - y), half)
    y_c = move(jnp.concatenate([c_edge, c_rest], 0), swap_y)
    d_edge = move(jnp.concatenate([l_edge, c_edge], 0), direct)
    y_edge = move(l_edge, swap_y)
    y_rest = move(l_rest, swap_y)

    number = me * width + jnp.arange(width, dtype=jnp.int32)
    live = jnp.where(number < trace_counts[0], 1.0, 0.0)
    code = (owners[0, :, 0] * (length * ny) + surface_cells[0]).astype(F32)
    gathered = jnp.concatenate([traces * live[None], code[None], jnp.zeros((16 - steps - 1, width), F32)], 0)[None]
    reach = 1
    while reach < n:
        gathered = jnp.concatenate([gathered, move(gathered, everywhere([(i, i ^ reach) for i in range(n)]))], 0)
        reach *= 2

    r_cur = move(y_cur, relay)
    r_c = move(y_c[:two], relay)
    r_lat = move(y_edge, relay)
    x_c = move(jnp.concatenate([y_c, d_edge[half:], r_c], 0), swap_core)

    plane = lambda k: VM((k, ny, nz), F32)
    e, o, wz, wy = call(
        field_kernel,
        [plane(32), plane(24), VM((2 * nz, nz), BF16), VM((4 * ny, 8 * ny), BF16)],
        [scal, cur, y_cur, later, y_edge, y_rest],
        free=(1, 3),
        name="fields",
    )
    q = call(
        functools.partial(q_kernel, steps=steps, length=length),
        VM((3, ny, 128), F32),
        [scal, gathered],
        name="receivers",
    )
    a, c, e, o = call(
        model_kernel,
        [plane(24), plane(24), plane(32), plane(24)],
        [scal, courant_sq, y_c, x_c, d_cur, d_edge, r_c, e, o],
        {7: 2, 8: 3},
        free=(1,),
        name="model",
    )
    g = jnp.zeros((length, ny, nz), F32)
    work = 2 * 16 * ny * nz * 60
    rounds = steps // 2
    send_a = send_b = None
    for r in range(rounds):
        if r:
            recv_a = move(send_a, swap_a)
            recv_b = move(send_b, swap_b)
        o, g = call(
            functools.partial(inner_kernel, r=r, length=length),
            [plane(24), plane(length)],
            [scal, e, o, a, c, q, wz, wy, forward, g],
            {2: 0, 9: 1},
            flops=work,
            name=f"inner{r}",
        )
        last = r == rounds - 1
        outs = [plane(32), plane(24)] + ([] if last else [plane(8)])
        model = [a, c, q, wz, wy]
        if r == 0:
            e, o, send_a = call(first_kernel, outs, [scal, r_cur, r_lat, e, o] + model, {3: 0, 4: 1}, flops=work, name="first")
            kern = functools.partial(side_kernel, r=r, side="b", recv=False, last=False)
            e, o, send_b = call(kern, outs, [scal, e, o] + model, {1: 0, 2: 1}, flops=work, name="side_b0")
            continue
        sent = []
        for side, recv in (("a", recv_a), ("b", recv_b)):
            kern = functools.partial(side_kernel, r=r, side=side, recv=True, last=last)
            e, o, *new = call(kern, outs, [scal, recv, e, o] + model, {2: 0, 3: 1}, flops=work, name=f"side_{side}{r}")
            sent += new
        if not last:
            send_a, send_b = sent

    part = ny // 4
    field, give, keep = call(
        functools.partial(final_kernel, steps=steps),
        [jax.ShapeDtypeStruct((length, ny, nz), F32), VM((length, 2 * part, nz), F32), VM((length, 2 * part, nz), F32)],
        [scal, e, o, forward, g],
        name="final",
    )
    give, mine = call(
        pair_kernel,
        [VM((length, part, nz), F32)] * 2,
        [scal, keep, move(give, swap_core)],
        name="pair",
    )
    return field[None], mine + move(give, swap_x)


def solution(mesh):
    placed = (
        P("shot", None, "space"),
        P("shot", "space", None),
        P("shot", "space"),
        P("shot"),
        P("shot", "space", None, None),
        P("shot", "space", None, None),
        P("shot", None, "space", None, None),
        P("space", None, None),
    )
    return jax.shard_map(
        shards,
        mesh=mesh,
        in_specs=placed,
        out_specs=(P("shot", "space", None, None), P("space", "shot", None)),
        check_vma=False,
    )
```

time: 212 us -> 172 us (0.81)
  blocking collectives: 42.4 us -> 0 us
  local copies, waits for them, and re-layouts: 25.6 us -> 3.53 us
  waiting for transfers between devices: 56.2 us -> 71 us
  starting transfers between devices: 41.4 us -> 53.4 us
  Pallas kernels: 41.7 us -> 39.1 us
    all_gather x1 -> x0, blocking collectives: 42.4 us -> none  [shards(): gathered = lax.all_gather(payload, 'space', axis=0)]
    unnamed x53 -> x14, local copies, waits for them, and re-layouts: 24.5 us -> 0.46 us
    ppermute x17 -> x25, waiting for transfers between devices: 56.2 us -> 71 us  [move(): return lax.ppermute(x, ('shot', 'space'), pairs)]
    ppermute x17 -> x25, starting transfers between devices: 41.4 us -> 53.4 us  [move(): return lax.ppermute(x, ('shot', 'space'), pairs)]
    dynamic_slice x0 -> x2, local copies, waits for them, and re-layouts: none -> 2.85 us  [shards(): cut = lambda x, at, size: lax.dynamic_slice_in_dim(x, at, size, 0)]
    pallas_call x21 -> x23, Pallas kernels: 41.7 us -> 39.1 us  [call(): pl.pallas_call(kernel, out_shape=out_shapes, in_specs=specs, out_specs=ja...]
  transfers between devices with their start and end apart: 17 -> 25, of which waited for: 13 -> 16; matrix products, arithmetic and copies ran while one was open for 1% -> 3% of each run, Pallas kernels for 16% -> 19%
where the time goes in v2:
time: 172 us; the launch traced here: 171 us
  waiting for transfers between devices  71 us (41%)
  starting transfers between devices  53.4 us (31%)
  Pallas kernels  39.1 us (23%)
  local copies, waits for them, and re-layouts  3.53 us (2%)
  other arithmetic  2.61 us (2%)
  between operations  1.83 us (1%)
    ppermute x25, waiting for transfers between devices, move(): return lax.ppermute(x, ('shot', 'space'), pairs)  71 us
    ppermute x25, starting transfers between devices, move(): return lax.ppermute(x, ('shot', 'space'), pairs)  53.4 us
    pallas_call x23, Pallas kernels, call(): pl.pallas_call(kernel, out_shape=out_shapes, in_specs=specs, out_specs=ja...  39.1 us
  transfers between devices with their start and end apart: 25, of which 16 were waited for; matrix products, arithmetic and copies ran while one was open for 3% of the time, Pallas kernels for 19%

profile of v2, /device:TPU:16, one launch (start us, length us, event | category | flops | bytes accessed | tf_op | source)
XLA Modules:
  0.0 171.4 jit_solution(11941122522501595184)
XLA Ops:
  2.2 2.3 %collective-permute-start.8 = (f32[8,64,256]{2,1,0:T(8,128)}, f32[8,64,256]{2,1,0:T(8,128)S(1)}, u32[]{:S(2)}, u32[]{:S(2)}) collective-permute-start(f32[8,64,256]{2,1,0:T(8,128)} %bitcast.32), channel_id=1, source_target_pairs={{2,0},{4,2},{6,4},{1,3},{3,5},{5,7},{10,8},{12,10},{14,12},{9,11},... | collective-permute-start | bytes 1572872 | tf_op jit(solution)/shard_map/ppermute | solution.py:251
  10.1 2.5 %collective-permute-start.5 = (f32[6,64,256]{2,1,0:T(8,128)S(1)}, f32[6,64,256]{2,1,0:T(8,128)S(1)}, u32[]{:S(2)}, u32[]{:S(2)}) collective-permute-start(f32[6,64,256]{2,1,0:T(8,128)S(1)} %pad_maximum_fusion.1), channel_id=1, source_target_pairs={{2,0},{4,2},{6,4},{1,3},{3,5},{5,7},{10,8},{12,10},{14,12},{9,11},... | collective-permute-start | bytes 1179656 | tf_op jit(solution)/shard_map/ppermute | solution.py:251
  15.0 10.8 %collective-permute-done.4.c_oth = f32[4,64,256]{2,1,0:T(8,128)S(1)} collective-permute-done((f32[4,64,256]{2,1,0:T(8,128)S(1)}, f32[4,64,256]{2,1,0:T(8,128)S(1)}, u32[]{:S(2)}, u32[]{:S(2)}) %collective-permute-start.4) | collective-permute-done | bytes 262176 | tf_op jit(solution)/shard_map/ppermute | solution.py:251
  25.8 3.5 %collective-permute-start.6 = (f32[2,64,256]{2,1,0:T(8,128)S(1)}, f32[2,64,256]{2,1,0:T(8,128)S(1)}, u32[]{:S(2)}, u32[]{:S(2)}) collective-permute-start(f32[2,64,256]{2,1,0:T(8,128)S(1)} %slice.9), channel_id=1, source_target_pairs={{0,2},{2,4},{4,6},{3,1},{5,3},{7,5},{8,10},{10,12},{12,14},{11,9},... | collective-permute-start | bytes 393224 | tf_op jit(solution)/shard_map/ppermute | solution.py:251
  29.8 2.9 %collective-permute-done.6.r_c = f32[2,64,256]{2,1,0:T(8,128)S(1)} collective-permute-done((f32[2,64,256]{2,1,0:T(8,128)S(1)}, f32[2,64,256]{2,1,0:T(8,128)S(1)}, u32[]{:S(2)}, u32[]{:S(2)}) %collective-permute-start.6) | collective-permute-done | bytes 131104 | tf_op jit(solution)/shard_map/ppermute | solution.py:251
  33.6 3.6 %collective-permute-start.1 = (f32[8,64,256]{2,1,0:T(8,128)S(1)}, f32[8,64,256]{2,1,0:T(8,128)}, u32[]{:S(2)}, u32[]{:S(2)}) collective-permute-start(f32[8,64,256]{2,1,0:T(8,128)S(1)} %collective-permute-done.cur_oth), channel_id=1, source_target_pairs={{0,2},{2,4},{4,6},{3,1},{5,3},{7,5},{8,10},{10,12},{12,14},{11,9},... | collective-permute-start | bytes 1572872 | tf_op jit(solution)/shard_map/ppermute | solution.py:251
  37.3 12.3 %collective-permute-done.11 = f32[2,16,256]{2,1,0:T(8,128)S(1)} collective-permute-done((f32[2,16,256]{2,1,0:T(8,128)S(1)}, f32[2,16,256]{2,1,0:T(8,128)S(1)}, u32[]{:S(2)}, u32[]{:S(2)}) %collective-permute-start.11) | collective-permute-done | bytes 32800 | tf_op jit(solution)/shard_map/ppermute | solution.py:251
  49.9 4.9 %collective-permute-done.12 = f32[4,16,256]{2,1,0:T(8,128)S(1)} collective-permute-done((f32[4,16,256]{2,1,0:T(8,128)S(1)}, f32[4,16,256]{2,1,0:T(8,128)S(1)}, u32[]{:S(2)}, u32[]{:S(2)}) %collective-permute-start.12) | collective-permute-done | bytes 65568 | tf_op jit(solution)/shard_map/ppermute | solution.py:251
  54.8 2.3 %collective-permute-start.9 = (f32[4,64,256]{2,1,0:T(8,128)}, f32[4,64,256]{2,1,0:T(8,128)}, u32[]{:S(2)}, u32[]{:S(2)}) collective-permute-start(f32[4,64,256]{2,1,0:T(8,128)} %get-tuple-element.120), channel_id=1, source_target_pairs={{0,1},{1,0},{2,3},{3,2},{4,5},{5,4},{6,7},{7,6},{8,9},{9,8},{10,11... | collective-permute-start | bytes 786440 | tf_op jit(solution)/shard_map/ppermute | solution.py:251
  59.5 2.8 %receivers.1.q_ref.refs_4_.refs_5_ = f32[3,64,128]{2,1,0:T(8,128)S(1)} custom-call(s32[5]{0:T(128)S(1)} %stack.23.scal_ref, f32[8,16,256]{2,1,0:T(8,128)S(1)} %pad_maximum_fusion.3.gathered_ref), custom_call_target="tpu_custom_call" | custom-call | bytes 1048576 | tf_op jit(solution)/shard_map/receivers/pallas_call | solution.py:226
  67.4 2.7 %first.1 = (f32[32,64,256]{2,1,0:T(8,128)S(1)}, f32[24,64,256]{2,1,0:T(8,128)S(1)}, f32[8,64,256]{2,1,0:T(8,128)S(1)}) custom-call(s32[5]{0:T(128)S(1)} %stack.23.scal_ref, f32[8,64,256]{2,1,0:T(8,128)} %collective-permute-done.1.r_cur, f32[4,64,256]{2,1,0:T(8,128)} %collective-permute-done.3.r_lat, ...), custom_call_target="tpu_custom_call", output_to_operand_aliasing={{0}: (3, {}), {1}: (4, {})} | custom-call | flops 31457280 | bytes 1048576 | tf_op jit(solution)/shard_map/first/pallas_call | solution.py:226
  70.1 4.6 %collective-permute-start.14 = (f32[8,64,256]{2,1,0:T(8,128)S(1)}, f32[8,64,256]{2,1,0:T(8,128)S(1)}, u32[]{:S(2)}, u32[]{:S(2)}) collective-permute-start(f32[8,64,256]{2,1,0:T(8,128)S(1)} %get-tuple-element.73), channel_id=1, source_target_pairs={{0,2},{2,0},{1,3},{3,1},{4,6},{6,4},{5,7},{7,5},{10,12},{12,10},{1... | collective-permute-start | bytes 1572872 | tf_op jit(solution)/shard_map/ppermute | solution.py:251
  80.0 6.8 %collective-permute-done.14.refs_0_ = f32[8,64,256]{2,1,0:T(8,128)S(1)} collective-permute-done((f32[8,64,256]{2,1,0:T(8,128)S(1)}, f32[8,64,256]{2,1,0:T(8,128)S(1)}, u32[]{:S(2)}, u32[]{:S(2)}) %collective-permute-start.14) | collective-permute-done | bytes 524320 | tf_op jit(solution)/shard_map/ppermute | solution.py:251
  88.8 4.4 %collective-permute-start.16 = (f32[8,64,256]{2,1,0:T(8,128)S(1)}, f32[8,64,256]{2,1,0:T(8,128)S(1)}, u32[]{:S(2)}, u32[]{:S(2)}) collective-permute-start(f32[8,64,256]{2,1,0:T(8,128)S(1)} %get-tuple-element.81), channel_id=1, source_target_pairs={{0,2},{2,0},{1,3},{3,1},{4,6},{6,4},{5,7},{7,5},{10,12},{12,10},{1... | collective-permute-start | bytes 1572872 | tf_op jit(solution)/shard_map/ppermute | solution.py:251
  98.5 6.8 %collective-permute-done.16.refs_0_ = f32[8,64,256]{2,1,0:T(8,128)S(1)} collective-permute-done((f32[8,64,256]{2,1,0:T(8,128)S(1)}, f32[8,64,256]{2,1,0:T(8,128)S(1)}, u32[]{:S(2)}, u32[]{:S(2)}) %collective-permute-start.16) | collective-permute-done | bytes 524320 | tf_op jit(solution)/shard_map/ppermute | solution.py:251
  107.4 3.8 %collective-permute-start.18 = (f32[8,64,256]{2,1,0:T(8,128)S(1)}, f32[8,64,256]{2,1,0:T(8,128)S(1)}, u32[]{:S(2)}, u32[]{:S(2)}) collective-permute-start(f32[8,64,256]{2,1,0:T(8,128)S(1)} %get-tuple-element.89), channel_id=1, source_target_pairs={{0,2},{2,0},{1,3},{3,1},{4,6},{6,4},{5,7},{7,5},{10,12},{12,10},{1... | collective-permute-start | bytes 1572872 | tf_op jit(solution)/shard_map/ppermute | solution.py:251
  116.9 5.8 %collective-permute-done.18.refs_0_ = f32[8,64,256]{2,1,0:T(8,128)S(1)} collective-permute-done((f32[8,64,256]{2,1,0:T(8,128)S(1)}, f32[8,64,256]{2,1,0:T(8,128)S(1)}, u32[]{:S(2)}, u32[]{:S(2)}) %collective-permute-start.18) | collective-permute-done | bytes 524320 | tf_op jit(solution)/shard_map/ppermute | solution.py:251
  124.7 3.3 %collective-permute-start.20 = (f32[8,64,256]{2,1,0:T(8,128)S(1)}, f32[8,64,256]{2,1,0:T(8,128)S(1)}, u32[]{:S(2)}, u32[]{:S(2)}) collective-permute-start(f32[8,64,256]{2,1,0:T(8,128)S(1)} %get-tuple-element.97), channel_id=1, source_target_pairs={{0,2},{2,0},{1,3},{3,1},{4,6},{6,4},{5,7},{7,5},{10,12},{12,10},{1... | collective-permute-start | bytes 1572872 | tf_op jit(solution)/shard_map/ppermute | solution.py:251
  135.1 3.9 %collective-permute-done.20.refs_0_ = f32[8,64,256]{2,1,0:T(8,128)S(1)} collective-permute-done((f32[8,64,256]{2,1,0:T(8,128)S(1)}, f32[8,64,256]{2,1,0:T(8,128)S(1)}, u32[]{:S(2)}, u32[]{:S(2)}) %collective-permute-start.20) | collective-permute-done | bytes 524320 | tf_op jit(solution)/shard_map/ppermute | solution.py:251
  140.9 3.0 %collective-permute-start.22 = (f32[8,64,256]{2,1,0:T(8,128)S(1)}, f32[8,64,256]{2,1,0:T(8,128)S(1)}, u32[]{:S(2)}, u32[]{:S(2)}) collective-permute-start(f32[8,64,256]{2,1,0:T(8,128)S(1)} %get-tuple-element.105), channel_id=1, source_target_pairs={{0,2},{2,0},{1,3},{3,1},{4,6},{6,4},{5,7},{7,5},{10,12},{12,10},{1... | collective-permute-start | bytes 1572872 | tf_op jit(solution)/shard_map/ppermute | solution.py:251
  143.9 2.5 %collective-permute-done.19.refs_0_ = f32[8,64,256]{2,1,0:T(8,128)S(1)} collective-permute-done((f32[8,64,256]{2,1,0:T(8,128)S(1)}, f32[8,64,256]{2,1,0:T(8,128)S(1)}, u32[]{:S(2)}, u32[]{:S(2)}) %collective-permute-start.19) | collective-permute-done | bytes 524320 | tf_op jit(solution)/shard_map/ppermute | solution.py:251
  148.5 2.6 %collective-permute-start.21 = (f32[8,64,256]{2,1,0:T(8,128)S(1)}, f32[8,64,256]{2,1,0:T(8,128)S(1)}, u32[]{:S(2)}, u32[]{:S(2)}) collective-permute-start(f32[8,64,256]{2,1,0:T(8,128)S(1)} %get-tuple-element.104), channel_id=1, source_target_pairs={{2,4},{4,2},{3,5},{5,3},{8,10},{10,8},{9,11},{11,9},{12,14},{14,12... | collective-permute-start | bytes 1572872 | tf_op jit(solution)/shard_map/ppermute | solution.py:251
  154.8 4.7 %collective-permute-done.21.refs_0_ = f32[8,64,256]{2,1,0:T(8,128)S(1)} collective-permute-done((f32[8,64,256]{2,1,0:T(8,128)S(1)}, f32[8,64,256]{2,1,0:T(8,128)S(1)}, u32[]{:S(2)}, u32[]{:S(2)}) %collective-permute-start.21) | collective-permute-done | bytes 524320 | tf_op jit(solution)/shard_map/ppermute | solution.py:251
  166.7 4.0 %collective-permute-done.24 = f32[8,16,256]{2,1,0:T(8,128)S(1)} collective-permute-done((f32[8,16,256]{2,1,0:T(8,128)S(1)}, f32[8,16,256]{2,1,0:T(8,128)S(1)}, u32[]{:S(2)}, u32[]{:S(2)}) %collective-permute-start.24) | collective-permute-done | bytes 131104 | tf_op jit(solution)/shard_map/ppermute | solution.py:251
  (82 shorter events, 62.7 us)
Async XLA Ops:
  0.7 32.9 %collective-permute-start = (f32[8,64,256]{2,1,0:T(8,128)}, f32[8,64,256]{2,1,0:T(8,128)S(1)}, u32[]{:S(2)}, u32[]{:S(2)}) collective-permute-start(f32[8,64,256]{2,1,0:T(8,128)} %bitcast.31), channel_id=1, source_target_pairs={{0,1},{1,0},{2,3},{3,2},{4,5},{5,4},{6,7},{7,6},{8,9},{9,8},{10,11... | collective-permute-start | bytes 1572872 | tf_op jit(solution)/shard_map/ppermute | solution.py:251
  2.2 61.8 %collective-permute-start.8 = (f32[8,64,256]{2,1,0:T(8,128)}, f32[8,64,256]{2,1,0:T(8,128)S(1)}, u32[]{:S(2)}, u32[]{:S(2)}) collective-permute-start(f32[8,64,256]{2,1,0:T(8,128)} %bitcast.32), channel_id=1, source_target_pairs={{2,0},{4,2},{6,4},{1,3},{3,5},{5,7},{10,8},{12,10},{14,12},{9,11},... | collective-permute-start | bytes 1572872 | tf_op jit(solution)/shard_map/ppermute | solution.py:251
  6.5 50.7 %collective-permute-start.2 = (f32[4,64,256]{2,1,0:T(8,128)}, f32[4,64,256]{2,1,0:T(8,128)}, u32[]{:S(2)}, u32[]{:S(2)}) collective-permute-start(f32[4,64,256]{2,1,0:T(8,128)} %get-tuple-element.121), channel_id=1, source_target_pairs={{0,1},{1,0},{2,3},{3,2},{4,5},{5,4},{6,7},{7,6},{8,9},{9,8},{10,11... | collective-permute-start | bytes 786440 | tf_op jit(solution)/shard_map/ppermute | solution.py:251
  10.1 19.3 %collective-permute-start.5 = (f32[6,64,256]{2,1,0:T(8,128)S(1)}, f32[6,64,256]{2,1,0:T(8,128)S(1)}, u32[]{:S(2)}, u32[]{:S(2)}) collective-permute-start(f32[6,64,256]{2,1,0:T(8,128)S(1)} %pad_maximum_fusion.1), channel_id=1, source_target_pairs={{2,0},{4,2},{6,4},{1,3},{3,5},{5,7},{10,8},{12,10},{14,12},{9,11},... | collective-permute-start | bytes 1179656 | tf_op jit(solution)/shard_map/ppermute | solution.py:251
  12.6 13.2 %collective-permute-start.4 = (f32[4,64,256]{2,1,0:T(8,128)S(1)}, f32[4,64,256]{2,1,0:T(8,128)S(1)}, u32[]{:S(2)}, u32[]{:S(2)}) collective-permute-start(f32[4,64,256]{2,1,0:T(8,128)S(1)} %pad_maximum_fusion.2), channel_id=1, source_target_pairs={{0,1},{1,0},{2,3},{3,2},{4,5},{5,4},{6,7},{7,6},{8,9},{9,8},{10,11... | collective-permute-start | bytes 786440 | tf_op jit(solution)/shard_map/ppermute | solution.py:251
  25.8 6.9 %collective-permute-start.6 = (f32[2,64,256]{2,1,0:T(8,128)S(1)}, f32[2,64,256]{2,1,0:T(8,128)S(1)}, u32[]{:S(2)}, u32[]{:S(2)}) collective-permute-start(f32[2,64,256]{2,1,0:T(8,128)S(1)} %slice.9), channel_id=1, source_target_pairs={{0,2},{2,4},{4,6},{3,1},{5,3},{7,5},{8,10},{10,12},{12,14},{11,9},... | collective-permute-start | bytes 393224 | tf_op jit(solution)/shard_map/ppermute | solution.py:251
  29.4 7.8 %collective-permute-start.10 = (f32[1,16,256]{2,1,0:T(8,128)S(1)}, f32[1,16,256]{2,1,0:T(8,128)S(1)}, u32[]{:S(2)}, u32[]{:S(2)}) collective-permute-start(f32[1,16,256]{2,1,0:T(8,128)S(1)} %maximum_bitcast_fusion), channel_id=1, source_target_pairs={{0,1},{1,0},{2,3},{3,2},{4,5},{5,4},{6,7},{7,6},{8,9},{9,8},{10,11... | collective-permute-start | bytes 49160 | tf_op jit(solution)/shard_map/ppermute | solution.py:251
  33.5 30.5 %collective-permute-start.7 = (f32[8,64,256]{2,1,0:T(8,128)}, f32[8,64,256]{2,1,0:T(8,128)}, u32[]{:S(2)}, u32[]{:S(2)}) collective-permute-start(f32[8,64,256]{2,1,0:T(8,128)} %pad_maximum_fusion), channel_id=1, source_target_pairs={{0,8},{1,9},{2,10},{3,11},{4,12},{5,13},{6,14},{7,15},{8,0},{9,1},... | collective-permute-start | bytes 1572872 | tf_op jit(solution)/shard_map/ppermute | solution.py:251
  33.6 33.8 %collective-permute-start.1 = (f32[8,64,256]{2,1,0:T(8,128)S(1)}, f32[8,64,256]{2,1,0:T(8,128)}, u32[]{:S(2)}, u32[]{:S(2)}) collective-permute-start(f32[8,64,256]{2,1,0:T(8,128)S(1)} %collective-permute-done.cur_oth), channel_id=1, source_target_pairs={{0,2},{2,4},{4,6},{3,1},{5,3},{7,5},{8,10},{10,12},{12,14},{11,9},... | collective-permute-start | bytes 1572872 | tf_op jit(solution)/shard_map/ppermute | solution.py:251
  37.2 12.4 %collective-permute-start.11 = (f32[2,16,256]{2,1,0:T(8,128)S(1)}, f32[2,16,256]{2,1,0:T(8,128)S(1)}, u32[]{:S(2)}, u32[]{:S(2)}) collective-permute-start(f32[2,16,256]{2,1,0:T(8,128)S(1)} %pad_maximum_fusion.5), channel_id=1, source_target_pairs={{0,2},{1,3},{2,0},{3,1},{4,6},{5,7},{6,4},{7,5},{8,10},{9,11},{10,... | collective-permute-start | bytes 98312 | tf_op jit(solution)/shard_map/ppermute | solution.py:251
  49.6 5.3 %collective-permute-start.12 = (f32[4,16,256]{2,1,0:T(8,128)S(1)}, f32[4,16,256]{2,1,0:T(8,128)S(1)}, u32[]{:S(2)}, u32[]{:S(2)}) collective-permute-start(f32[4,16,256]{2,1,0:T(8,128)S(1)} %pad_maximum_fusion.4), channel_id=1, source_target_pairs={{0,4},{1,5},{2,6},{3,7},{4,0},{5,1},{6,2},{7,3},{8,12},{9,13},{10,... | collective-permute-start | bytes 196616 | tf_op jit(solution)/shard_map/ppermute | solution.py:251
  54.8 7.7 %collective-permute-start.9 = (f32[4,64,256]{2,1,0:T(8,128)}, f32[4,64,256]{2,1,0:T(8,128)}, u32[]{:S(2)}, u32[]{:S(2)}) collective-permute-start(f32[4,64,256]{2,1,0:T(8,128)} %get-tuple-element.120), channel_id=1, source_target_pairs={{0,1},{1,0},{2,3},{3,2},{4,5},{5,4},{6,7},{7,6},{8,9},{9,8},{10,11... | collective-permute-start | bytes 786440 | tf_op jit(solution)/shard_map/ppermute | solution.py:251
  57.2 10.2 %collective-permute-start.3 = (f32[4,64,256]{2,1,0:T(8,128)}, f32[4,64,256]{2,1,0:T(8,128)}, u32[]{:S(2)}, u32[]{:S(2)}) collective-permute-start(f32[4,64,256]{2,1,0:T(8,128)} %collective-permute-done.2.lat_edge), channel_id=1, source_target_pairs={{0,2},{2,4},{4,6},{3,1},{5,3},{7,5},{8,10},{10,12},{12,14},{11,9},... | collective-permute-start | bytes 786440 | tf_op jit(solution)/shard_map/ppermute | solution.py:251
  70.1 16.7 %collective-permute-start.14 = (f32[8,64,256]{2,1,0:T(8,128)S(1)}, f32[8,64,256]{2,1,0:T(8,128)S(1)}, u32[]{:S(2)}, u32[]{:S(2)}) collective-permute-start(f32[8,64,256]{2,1,0:T(8,128)S(1)} %get-tuple-element.73), channel_id=1, source_target_pairs={{0,2},{2,0},{1,3},{3,1},{4,6},{6,4},{5,7},{7,5},{10,12},{12,10},{1... | collective-permute-start | bytes 1572872 | tf_op jit(solution)/shard_map/ppermute | solution.py:251
  76.7 16.5 %collective-permute-start.13 = (f32[8,64,256]{2,1,0:T(8,128)S(1)}, f32[8,64,256]{2,1,0:T(8,128)S(1)}, u32[]{:S(2)}, u32[]{:S(2)}) collective-permute-start(f32[8,64,256]{2,1,0:T(8,128)S(1)} %get-tuple-element.72), channel_id=1, source_target_pairs={{2,4},{4,2},{3,5},{5,3},{8,10},{10,8},{9,11},{11,9},{12,14},{14,12... | collective-permute-start | bytes 1572872 | tf_op jit(solution)/shard_map/ppermute | solution.py:251
  88.8 16.6 %collective-permute-start.16 = (f32[8,64,256]{2,1,0:T(8,128)S(1)}, f32[8,64,256]{2,1,0:T(8,128)S(1)}, u32[]{:S(2)}, u32[]{:S(2)}) collective-permute-start(f32[8,64,256]{2,1,0:T(8,128)S(1)} %get-tuple-element.81), channel_id=1, source_target_pairs={{0,2},{2,0},{1,3},{3,1},{4,6},{6,4},{5,7},{7,5},{10,12},{12,10},{1... | collective-permute-start | bytes 1572872 | tf_op jit(solution)/shard_map/ppermute | solution.py:251
  95.2 16.3 %collective-permute-start.15 = (f32[8,64,256]{2,1,0:T(8,128)S(1)}, f32[8,64,256]{2,1,0:T(8,128)S(1)}, u32[]{:S(2)}, u32[]{:S(2)}) collective-permute-start(f32[8,64,256]{2,1,0:T(8,128)S(1)} %get-tuple-element.80), channel_id=1, source_target_pairs={{2,4},{4,2},{3,5},{5,3},{8,10},{10,8},{9,11},{11,9},{12,14},{14,12... | collective-permute-start | bytes 1572872 | tf_op jit(solution)/shard_map/ppermute | solution.py:251
  107.4 15.3 %collective-permute-start.18 = (f32[8,64,256]{2,1,0:T(8,128)S(1)}, f32[8,64,256]{2,1,0:T(8,128)S(1)}, u32[]{:S(2)}, u32[]{:S(2)}) collective-permute-start(f32[8,64,256]{2,1,0:T(8,128)S(1)} %get-tuple-element.89), channel_id=1, source_target_pairs={{0,2},{2,0},{1,3},{3,1},{4,6},{6,4},{5,7},{7,5},{10,12},{12,10},{1... | collective-permute-start | bytes 1572872 | tf_op jit(solution)/shard_map/ppermute | solution.py:251
  113.5 15.9 %collective-permute-start.17 = (f32[8,64,256]{2,1,0:T(8,128)S(1)}, f32[8,64,256]{2,1,0:T(8,128)S(1)}, u32[]{:S(2)}, u32[]{:S(2)}) collective-permute-start(f32[8,64,256]{2,1,0:T(8,128)S(1)} %get-tuple-element.88), channel_id=1, source_target_pairs={{2,4},{4,2},{3,5},{5,3},{8,10},{10,8},{9,11},{11,9},{12,14},{14,12... | collective-permute-start | bytes 1572872 | tf_op jit(solution)/shard_map/ppermute | solution.py:251
  124.7 14.3 %collective-permute-start.20 = (f32[8,64,256]{2,1,0:T(8,128)S(1)}, f32[8,64,256]{2,1,0:T(8,128)S(1)}, u32[]{:S(2)}, u32[]{:S(2)}) collective-permute-start(f32[8,64,256]{2,1,0:T(8,128)S(1)} %get-tuple-element.97), channel_id=1, source_target_pairs={{0,2},{2,0},{1,3},{3,1},{4,6},{6,4},{5,7},{7,5},{10,12},{12,10},{1... | collective-permute-start | bytes 1572872 | tf_op jit(solution)/shard_map/ppermute | solution.py:251
  131.4 15.0 %collective-permute-start.19 = (f32[8,64,256]{2,1,0:T(8,128)S(1)}, f32[8,64,256]{2,1,0:T(8,128)S(1)}, u32[]{:S(2)}, u32[]{:S(2)}) collective-permute-start(f32[8,64,256]{2,1,0:T(8,128)S(1)} %get-tuple-element.96), channel_id=1, source_target_pairs={{2,4},{4,2},{3,5},{5,3},{8,10},{10,8},{9,11},{11,9},{12,14},{14,12... | collective-permute-start | bytes 1572872 | tf_op jit(solution)/shard_map/ppermute | solution.py:251
  140.9 13.3 %collective-permute-start.22 = (f32[8,64,256]{2,1,0:T(8,128)S(1)}, f32[8,64,256]{2,1,0:T(8,128)S(1)}, u32[]{:S(2)}, u32[]{:S(2)}) collective-permute-start(f32[8,64,256]{2,1,0:T(8,128)S(1)} %get-tuple-element.105), channel_id=1, source_target_pairs={{0,2},{2,0},{1,3},{3,1},{4,6},{6,4},{5,7},{7,5},{10,12},{12,10},{1... | collective-permute-start | bytes 1572872 | tf_op jit(solution)/shard_map/ppermute | solution.py:251
  148.5 11.1 %collective-permute-start.21 = (f32[8,64,256]{2,1,0:T(8,128)S(1)}, f32[8,64,256]{2,1,0:T(8,128)S(1)}, u32[]{:S(2)}, u32[]{:S(2)}) collective-permute-start(f32[8,64,256]{2,1,0:T(8,128)S(1)} %get-tuple-element.104), channel_id=1, source_target_pairs={{2,4},{4,2},{3,5},{5,3},{8,10},{10,8},{9,11},{11,9},{12,14},{14,12... | collective-permute-start | bytes 1572872 | tf_op jit(solution)/shard_map/ppermute | solution.py:251
  165.2 5.6 %collective-permute-start.24 = (f32[8,16,256]{2,1,0:T(8,128)S(1)}, f32[8,16,256]{2,1,0:T(8,128)S(1)}, u32[]{:S(2)}, u32[]{:S(2)}) collective-permute-start(f32[8,16,256]{2,1,0:T(8,128)S(1)} %get-tuple-element.119), channel_id=1, source_target_pairs={{0,16},{1,17},{2,18},{3,19},{4,20},{5,21},{6,22},{7,23},{8,24},{9,... | collective-permute-start | bytes 393224 | tf_op jit(solution)/shard_map/ppermute | solution.py:251
  (8 other events, 182.1 us)

commit v3 on v2

--- a/solution.py
+++ b/solution.py
@@ -11,7 +11,7 @@
 TAPS = (8064.0, -1008.0, 128.0, -9.0)
 CENTRE = 3.0 * (-205.0 / 72.0)
 
-LIMIT = 8 * 1024 * 1024
+LIMIT = 16 * 1024 * 1024
 VM = pltpu.VMEM
 F32 = jnp.float32
 BF16 = jnp.bfloat16
@@ -96,6 +96,10 @@
         q_ref[j] = acc[j]
 
 
+def keep_if(flag, x):
+    return jnp.where(flag == 1, x, 0.0)
+
+
 def field_kernel(scal_ref, cur_own, cur_oth, lat_own, lat_edge, lat_rest, e_ref, o_ref, wz_ref, wy_ref):
     length, ny, nz = cur_own.shape
     half = length // 2
@@ -124,6 +128,7 @@
     length = c_own.shape[0]
     half, two = length // 2, length // 4
     y, core = scal_ref[2], scal_ref[3]
+    near, far = scal_ref[6 - y], scal_ref[5 + y]
 
     def put(j, cv):
         c_ref[j + 4] = cv * (1.0 / SCALE)
@@ -136,14 +141,14 @@
         for who, piece, at in ((core, c_oth, 0), (1 - core, c_core, 0)):
             put(local_of(scal_ref, base + half * (1 - y) + two * who + p, length), piece[at + p])
             put(local_of(scal_ref, base + half * y + two * who + p, length), piece[at + two + p])
-        put(halo_at(scal_ref, 1 - y, two * core + p, half, length), d_edge[half + p])
-        put(halo_at(scal_ref, 1 - y, two * (1 - core) + p, half, length), c_core[half + p])
-        put(halo_at(scal_ref, y, two * core + p, half, length), r_c[p])
-        put(halo_at(scal_ref, y, two * (1 - core) + p, half, length), c_core[half + two + p])
+        put(halo_at(scal_ref, 1 - y, two * core + p, half, length), keep_if(near, d_edge[half + p]))
+        put(halo_at(scal_ref, 1 - y, two * (1 - core) + p, half, length), keep_if(near, c_core[half + p]))
+        put(halo_at(scal_ref, y, two * core + p, half, length), keep_if(far, r_c[p]))
+        put(halo_at(scal_ref, y, two * (1 - core) + p, half, length), keep_if(far, c_core[half + two + p]))
     for p in range(length):
-        e_ref[halo_at(scal_ref, 1 - y, p, length, length) + 8] = d_cur[p]
+        e_ref[halo_at(scal_ref, 1 - y, p, length, length) + 8] = keep_if(near, d_cur[p])
     for p in range(half):
-        o_ref[halo_at(scal_ref, 1 - y, p, half, length) + 4] = d_edge[p]
+        o_ref[halo_at(scal_ref, 1 - y, p, half, length) + 4] = keep_if(near, d_edge[p])
 
 
 def inner_kernel(scal_ref, e_ref, o_in, a_ref, c_ref, q_ref, wz_ref, wy_ref, f_ref, g_in, o_ref, g_ref, *, r, length):
@@ -164,10 +169,11 @@
 def first_kernel(scal_ref, r_cur, r_lat, e_in, o_in, a_ref, c_ref, q_ref, wz_ref, wy_ref, e_ref, o_ref, new):
     length = r_cur.shape[0]
     y = scal_ref[2]
+    far = scal_ref[5 + y]
     for p in range(length):
-        e_ref[halo_at(scal_ref, y, p, length, length) + 8] = r_cur[p]
+        e_ref[halo_at(scal_ref, y, p, length, length) + 8] = keep_if(far, r_cur[p])
     for p in range(length // 2):
-        o_ref[halo_at(scal_ref, y, p, length // 2, length) + 4] = r_lat[p]
+        o_ref[halo_at(scal_ref, y, p, length // 2, length) + 4] = keep_if(far, r_lat[p])
     side_steps("a", 0, e_ref, o_ref, (a_ref, c_ref, q_ref, wz_ref, wy_ref), new)
 
 
@@ -179,11 +185,13 @@
 
     def work():
         if recv:
+            odd = scal_ref[1]
+            inside = scal_ref[6 - odd] if side == "a" else scal_ref[5 + odd]
             for i in range(8):
                 if side == "a":
-                    e_ref[24 + i] = recv_ref[7 - i]
+                    e_ref[24 + i] = keep_if(inside, recv_ref[7 - i])
                 else:
-                    e_ref[7 - i] = recv_ref[i]
+                    e_ref[7 - i] = keep_if(inside, recv_ref[i])
         side_steps(side, r, e_ref, o_ref, (a_ref, c_ref, q_ref, wz_ref, wy_ref), new)
 
     if last:
@@ -245,7 +253,9 @@
     levels = n // 2
     me, shot = lax.axis_index("space"), lax.axis_index("shot")
     level, y, core = me // 2, me % 2, shot % 2
-    scal = jnp.stack([level, (level + core) % 2, y, core, shot // 2]).astype(jnp.int32)
+    has_low = jnp.where(level > 0, 1, 0)
+    has_high = jnp.where(level < levels - 1, 1, 0)
+    scal = jnp.stack([level, level % 2, y, core, shot // 2, has_low, has_high]).astype(jnp.int32)
 
     def move(x, pairs):
         return lax.ppermute(x, ("shot", "space"), pairs)
@@ -256,34 +266,27 @@
     def level_swap(parity):
         out = []
         for s in range(shots):
-            for lv in range(levels - 1):
-                if (lv + s) % 2 == parity:
-                    for i in range(2):
-                        lo = s * n + 2 * lv + i
-                        out += [(lo, lo + 2), (lo + 2, lo)]
+            for lv in range(levels):
+                up = lv % 2 == parity
+                to = lv + 1 if up else lv - 1
+                for i in range(2):
+                    out.append((s * n + 2 * lv + i, s * n + (2 * to + i if 0 <= to < levels else 2 * lv + 1 - i)))
         return out
 
     swap_y = everywhere([(i, i ^ 1) for i in range(n)])
-    down = [(2 * lv, 2 * lv - 2) for lv in range(1, levels)]
-    up = [(2 * lv + 1, 2 * lv + 3) for lv in range(levels - 1)]
-    direct = everywhere(down + up)
-    relay = everywhere([(2 * lv, 2 * lv + 2) for lv in range(levels - 1)] + [(2 * lv + 1, 2 * lv - 1) for lv in range(1, levels)])
+    hops = [(2 * lv, 2 * lv + 2) for lv in range(levels - 1)] + [(2 * lv + 1, 2 * lv - 1) for lv in range(1, levels)]
+    relay = everywhere(hops)
+    direct = [(j, i) for i, j in relay]
     swap_core = [(s * n + i, (s ^ 1) * n + i) for s in range(shots) for i in range(n)]
     swap_x = [(s * n + i, (s ^ 2) * n + i) for s in range(shots) for i in range(n)]
     swap_a, swap_b = level_swap(0), level_swap(1)
 
+    def after(x, *others):
+        return lax.optimization_barrier((x, *others))[0]
+
     half, two = length // 2, length // 4
     cut = lambda x, at, size: lax.dynamic_slice_in_dim(x, at, size, 0)
     y_cur = move(cur, swap_y)
-    d_cur = move(cur, direct)
-    c_edge = cut(courant_sq, half * y + two * core, two)
-    c_rest = cut(courant_sq, half * (1 - y) + two * core, two)
-    l_edge = cut(later, half * y, half)
-    l_rest = cut(later, half * (1 - y), half)
-    y_c = move(jnp.concatenate([c_edge, c_rest], 0), swap_y)
-    d_edge = move(jnp.concatenate([l_edge, c_edge], 0), direct)
-    y_edge = move(l_edge, swap_y)
-    y_rest = move(l_rest, swap_y)
 
     number = me * width + jnp.arange(width, dtype=jnp.int32)
     live = jnp.where(number < trace_counts[0], 1.0, 0.0)
@@ -292,8 +295,23 @@
     reach = 1
     while reach < n:
         gathered = jnp.concatenate([gathered, move(gathered, everywhere([(i, i ^ reach) for i in range(n)]))], 0)
+        if reach == 1:
+            early = gathered
         reach *= 2
 
+    c_edge = cut(courant_sq, half * y + two * core, two)
+    c_rest = cut(courant_sq, half * (1 - y) + two * core, two)
+    l_edge = cut(later, half * y, half)
+    l_rest = cut(later, half * (1 - y), half)
+    d_cur = move(cur, direct)
+    y_c = move(after(jnp.concatenate([c_edge, c_rest], 0), early), swap_y)
+    y_edge = move(after(l_edge, early), swap_y)
+    y_rest = move(after(l_rest, early), swap_y)
+    d_edge = move(after(jnp.concatenate([l_edge, c_edge], 0), gathered), direct)
+
+    y_c = after(y_c, y_cur)
+    y_edge = after(y_edge, y_c)
+    y_rest = after(y_rest, y_edge)
     r_cur = move(y_cur, relay)
     r_c = move(y_c[:two], relay)
     r_lat = move(y_edge, relay)

time: 172 us -> 138 us (0.80)
  starting transfers between devices: 53.4 us -> 32 us
  waiting for transfers between devices: 71 us -> 58.8 us
    ppermute x25, starting transfers between devices: 53.4 us -> 32 us  [move(): return lax.ppermute(x, ('shot', 'space'), pairs)]
    ppermute x25, waiting for transfers between devices: 71 us -> 58.8 us  [move(): return lax.ppermute(x, ('shot', 'space'), pairs)]
  transfers between devices with their start and end apart: 25 -> 25, of which waited for: 16 -> 14; matrix products, arithmetic and copies ran while one was open for 3% -> 3% of each run, Pallas kernels for 19% -> 23%
where the time goes in v3:
time: 138 us
  waiting for transfers between devices  58.8 us (43%)
  Pallas kernels  38.6 us (28%)
  starting transfers between devices  32 us (23%)
  local copies, waits for them, and re-layouts  3.47 us (3%)
  other arithmetic  3.08 us (2%)
  between operations  1.71 us (1%)
    ppermute x25, waiting for transfers between devices, move(): return lax.ppermute(x, ('shot', 'space'), pairs)  58.8 us
    pallas_call x23, Pallas kernels, call(): pl.pallas_call(kernel, out_shape=out_shapes, in_specs=specs, out_specs=ja...  38.6 us
    ppermute x25, starting transfers between devices, move(): return lax.ppermute(x, ('shot', 'space'), pairs)  32 us
    dynamic_slice x2, local copies, waits for them, and re-layouts, shards(): cut = lambda x, at, size: lax.dynamic_slice_in_dim(x, at, size, 0)  2.81 us
  transfers between devices with their start and end apart: 25, of which 14 were waited for; matrix products, arithmetic and copies ran while one was open for 3% of the time, Pallas kernels for 23%

profile of v3, /device:TPU:16, one launch (start us, length us, event | category | flops | bytes accessed | tf_op | source)
XLA Modules:
  0.0 137.7 jit_solution(13200453371393087155)
XLA Ops:
  9.4 2.3 %collective-permute-done.6 = f32[2,16,256]{2,1,0:T(8,128)S(1)} collective-permute-done((f32[2,16,256]{2,1,0:T(8,128)S(1)}, f32[2,16,256]{2,1,0:T(8,128)S(1)}, u32[]{:S(2)}, u32[]{:S(2)}) %collective-permute-start.6) | collective-permute-done | bytes 32800 | tf_op jit(solution)/shard_map/ppermute | solution.py:261
  13.7 3.3 %collective-permute-done.7 = f32[4,16,256]{2,1,0:T(8,128)S(1)} collective-permute-done((f32[4,16,256]{2,1,0:T(8,128)S(1)}, f32[4,16,256]{2,1,0:T(8,128)S(1)}, u32[]{:S(2)}, u32[]{:S(2)}) %collective-permute-start.7) | collective-permute-done | bytes 65568 | tf_op jit(solution)/shard_map/ppermute | solution.py:261
  17.0 2.3 %collective-permute-start.8 = (f32[6,64,256]{2,1,0:T(8,128)S(1)}, f32[6,64,256]{2,1,0:T(8,128)S(1)}, u32[]{:S(2)}, u32[]{:S(2)}) collective-permute-start(f32[6,64,256]{2,1,0:T(8,128)S(1)} %pad_maximum_fusion.1), channel_id=1, source_target_pairs={{2,0},{4,2},{6,4},{1,3},{3,5},{5,7},{10,8},{12,10},{14,12},{9,11},... | collective-permute-start | bytes 1179656 | tf_op jit(solution)/shard_map/ppermute | solution.py:261
  19.3 4.3 %collective-permute-done.4.c_oth = f32[4,64,256]{2,1,0:T(8,128)S(1)} collective-permute-done((f32[4,64,256]{2,1,0:T(8,128)S(1)}, f32[4,64,256]{2,1,0:T(8,128)S(1)}, u32[]{:S(2)}, u32[]{:S(2)}) %collective-permute-start.4) | collective-permute-done | bytes 262176 | tf_op jit(solution)/shard_map/ppermute | solution.py:261
  23.6 3.5 %collective-permute-start.9 = (f32[2,64,256]{2,1,0:T(8,128)S(1)}, f32[2,64,256]{2,1,0:T(8,128)S(1)}, u32[]{:S(2)}, u32[]{:S(2)}) collective-permute-start(f32[2,64,256]{2,1,0:T(8,128)S(1)} %slice.7), channel_id=1, source_target_pairs={{0,2},{2,4},{4,6},{3,1},{5,3},{7,5},{8,10},{10,12},{12,14},{11,9},... | collective-permute-start | bytes 393224 | tf_op jit(solution)/shard_map/ppermute | solution.py:261
  27.1 2.4 %collective-permute-start.11 = (f32[8,64,256]{2,1,0:T(8,128)S(1)}, f32[8,64,256]{2,1,0:T(8,128)}, u32[]{:S(2)}, u32[]{:S(2)}) collective-permute-start(f32[8,64,256]{2,1,0:T(8,128)S(1)} %bitcast.34), channel_id=1, source_target_pairs={{2,0},{4,2},{6,4},{1,3},{3,5},{5,7},{10,8},{12,10},{14,12},{9,11},... | collective-permute-start | bytes 1572872 | tf_op jit(solution)/shard_map/ppermute | solution.py:261
  32.0 2.8 %collective-permute-start.1 = (f32[8,64,256]{2,1,0:T(8,128)S(1)}, f32[8,64,256]{2,1,0:T(8,128)S(1)}, u32[]{:S(2)}, u32[]{:S(2)}) collective-permute-start(f32[8,64,256]{2,1,0:T(8,128)S(1)} %collective-permute-done.cur_oth), channel_id=1, source_target_pairs={{0,2},{2,4},{4,6},{3,1},{5,3},{7,5},{8,10},{10,12},{12,14},{11,9},... | collective-permute-start | bytes 1572872 | tf_op jit(solution)/shard_map/ppermute | solution.py:261
  35.8 4.8 %collective-permute-done.3.lat_edge = f32[4,64,256]{2,1,0:T(8,128)} collective-permute-done((f32[4,64,256]{2,1,0:T(8,128)S(1)}, f32[4,64,256]{2,1,0:T(8,128)}, u32[]{:S(2)}, u32[]{:S(2)}) %collective-permute-start.3) | collective-permute-done | bytes 262176 | tf_op jit(solution)/shard_map/ppermute | solution.py:261
  40.5 3.5 %collective-permute-start.5 = (f32[4,64,256]{2,1,0:T(8,128)}, f32[4,64,256]{2,1,0:T(8,128)}, u32[]{:S(2)}, u32[]{:S(2)}) collective-permute-start(f32[4,64,256]{2,1,0:T(8,128)} %collective-permute-done.3.lat_edge), channel_id=1, source_target_pairs={{0,2},{2,4},{4,6},{3,1},{5,3},{7,5},{8,10},{10,12},{12,14},{11,9},... | collective-permute-start | bytes 786440 | tf_op jit(solution)/shard_map/ppermute | solution.py:261
  44.2 2.8 %receivers.1.q_ref.refs_4_.refs_5_ = f32[3,64,128]{2,1,0:T(8,128)S(1)} custom-call(s32[7]{0:T(128)S(1)} %stack.31.scal_ref, f32[8,16,256]{2,1,0:T(8,128)S(1)} %pad_maximum_fusion.3.gathered_ref), custom_call_target="tpu_custom_call" | custom-call | bytes 1048576 | tf_op jit(solution)/shard_map/receivers/pallas_call | solution.py:234
  53.7 2.5 %first.1 = (f32[32,64,256]{2,1,0:T(8,128)S(1)}, f32[24,64,256]{2,1,0:T(8,128)S(1)}, f32[8,64,256]{2,1,0:T(8,128)S(1)}) custom-call(s32[7]{0:T(128)S(1)} %stack.31.scal_ref, f32[8,64,256]{2,1,0:T(8,128)S(1)} %collective-permute-done.1.r_cur, f32[4,64,256]{2,1,0:T(8,128)} %collective-permute-done.5.r_lat, ...), custom_call_target="tpu_custom_call", output_to_operand_aliasing={{0}: (3, {}), {1}: (4, {})} | custom-call | flops 31457280 | bytes 1048576 | tf_op jit(solution)/shard_map/first/pallas_call | solution.py:234
  57.4 1.9 %side_b0.1 = (f32[32,64,256]{2,1,0:T(8,128)S(1)}, f32[24,64,256]{2,1,0:T(8,128)S(1)}, f32[8,64,256]{2,1,0:T(8,128)S(1)}) custom-call(s32[7]{0:T(128)S(1)} %stack.31.scal_ref, f32[32,64,256]{2,1,0:T(8,128)S(1)} %get-tuple-element.84.refs_0_, f32[24,64,256]{2,1,0:T(8,128)S(1)} %get-tuple-element.85.refs_1_, ...), custom_call_target="tpu_custom_call", output_to_operand_aliasing={{0}: (1, {}), {1}: (2, {})} | custom-call | flops 31457280 | bytes 1048576 | tf_op jit(solution)/shard_map/side_b0/pallas_call | solution.py:234
  60.9 8.6 %collective-permute-done.14.refs_0_ = f32[8,64,256]{2,1,0:T(8,128)S(1)} collective-permute-done((f32[8,64,256]{2,1,0:T(8,128)S(1)}, f32[8,64,256]{2,1,0:T(8,128)S(1)}, u32[]{:S(2)}, u32[]{:S(2)}) %collective-permute-start.14) | collective-permute-done | bytes 524320 | tf_op jit(solution)/shard_map/ppermute | solution.py:261
  76.4 7.5 %collective-permute-done.16.refs_0_ = f32[8,64,256]{2,1,0:T(8,128)S(1)} collective-permute-done((f32[8,64,256]{2,1,0:T(8,128)S(1)}, f32[8,64,256]{2,1,0:T(8,128)S(1)}, u32[]{:S(2)}, u32[]{:S(2)}) %collective-permute-start.16) | collective-permute-done | bytes 524320 | tf_op jit(solution)/shard_map/ppermute | solution.py:261
  87.6 2.0 %side_b2.1 = (f32[32,64,256]{2,1,0:T(8,128)S(1)}, f32[24,64,256]{2,1,0:T(8,128)S(1)}, f32[8,64,256]{2,1,0:T(8,128)S(1)}) custom-call(s32[7]{0:T(128)S(1)} %stack.31.scal_ref, f32[8,64,256]{2,1,0:T(8,128)S(1)} %collective-permute-done.15.refs_0_, f32[32,64,256]{2,1,0:T(8,128)S(1)} %get-tuple-element.100.refs_1_, ...), custom_call_target="tpu_custom_call", output_to_operand_aliasing={{0}: (2, {}), {1}: (3, {})} | custom-call | flops 31457280 | bytes 1048576 | tf_op jit(solution)/shard_map/side_b2/pallas_call | solution.py:234
  91.1 6.5 %collective-permute-done.18.refs_0_ = f32[8,64,256]{2,1,0:T(8,128)S(1)} collective-permute-done((f32[8,64,256]{2,1,0:T(8,128)S(1)}, f32[8,64,256]{2,1,0:T(8,128)S(1)}, u32[]{:S(2)}, u32[]{:S(2)}) %collective-permute-start.18) | collective-permute-done | bytes 524320 | tf_op jit(solution)/shard_map/ppermute | solution.py:261
  97.6 2.1 %side_a3.1 = (f32[32,64,256]{2,1,0:T(8,128)S(1)}, f32[24,64,256]{2,1,0:T(8,128)S(1)}, f32[8,64,256]{2,1,0:T(8,128)S(1)}) custom-call(s32[7]{0:T(128)S(1)} %stack.31.scal_ref, f32[8,64,256]{2,1,0:T(8,128)S(1)} %collective-permute-done.18.refs_0_, f32[32,64,256]{2,1,0:T(8,128)S(1)} %get-tuple-element.104.e_ref.refs_1_, ...), custom_call_target="tpu_custom_call", output_to_operand_aliasing={{0}: (2, {}), {1}: (3, {})} | custom-call | flops 31457280 | bytes 1048576 | tf_op jit(solution)/shard_map/side_a3/pallas_call | solution.py:234
  101.5 2.0 %side_b3.1 = (f32[32,64,256]{2,1,0:T(8,128)S(1)}, f32[24,64,256]{2,1,0:T(8,128)S(1)}, f32[8,64,256]{2,1,0:T(8,128)S(1)}) custom-call(s32[7]{0:T(128)S(1)} %stack.31.scal_ref, f32[8,64,256]{2,1,0:T(8,128)S(1)} %collective-permute-done.17.refs_0_, f32[32,64,256]{2,1,0:T(8,128)S(1)} %get-tuple-element.108.refs_1_, ...), custom_call_target="tpu_custom_call", output_to_operand_aliasing={{0}: (2, {}), {1}: (3, {})} | custom-call | flops 31457280 | bytes 1048576 | tf_op jit(solution)/shard_map/side_b3/pallas_call | solution.py:234
  104.9 5.6 %collective-permute-done.20.refs_0_ = f32[8,64,256]{2,1,0:T(8,128)S(1)} collective-permute-done((f32[8,64,256]{2,1,0:T(8,128)S(1)}, f32[8,64,256]{2,1,0:T(8,128)S(1)}, u32[]{:S(2)}, u32[]{:S(2)}) %collective-permute-start.20) | collective-permute-done | bytes 524320 | tf_op jit(solution)/shard_map/ppermute | solution.py:261
  114.3 2.0 %side_b4.1 = (f32[32,64,256]{2,1,0:T(8,128)S(1)}, f32[24,64,256]{2,1,0:T(8,128)S(1)}, f32[8,64,256]{2,1,0:T(8,128)S(1)}) custom-call(s32[7]{0:T(128)S(1)} %stack.31.scal_ref, f32[8,64,256]{2,1,0:T(8,128)S(1)} %collective-permute-done.19.refs_0_, f32[32,64,256]{2,1,0:T(8,128)S(1)} %get-tuple-element.116.refs_1_, ...), custom_call_target="tpu_custom_call", output_to_operand_aliasing={{0}: (2, {}), {1}: (3, {})} | custom-call | flops 31457280 | bytes 1048576 | tf_op jit(solution)/shard_map/side_b4/pallas_call | solution.py:234
  117.8 4.7 %collective-permute-done.22.refs_0_ = f32[8,64,256]{2,1,0:T(8,128)S(1)} collective-permute-done((f32[8,64,256]{2,1,0:T(8,128)S(1)}, f32[8,64,256]{2,1,0:T(8,128)S(1)}, u32[]{:S(2)}, u32[]{:S(2)}) %collective-permute-start.22) | collective-permute-done | bytes 524320 | tf_op jit(solution)/shard_map/ppermute | solution.py:261
  123.0 2.9 %collective-permute-done.21.refs_0_ = f32[8,64,256]{2,1,0:T(8,128)S(1)} collective-permute-done((f32[8,64,256]{2,1,0:T(8,128)S(1)}, f32[8,64,256]{2,1,0:T(8,128)S(1)}, u32[]{:S(2)}, u32[]{:S(2)}) %collective-permute-start.21) | collective-permute-done | bytes 524320 | tf_op jit(solution)/shard_map/ppermute | solution.py:261
  125.9 2.0 %side_b5.1 = (f32[32,64,256]{2,1,0:T(8,128)S(1)}, f32[24,64,256]{2,1,0:T(8,128)S(1)}) custom-call(s32[7]{0:T(128)S(1)} %stack.31.scal_ref, f32[8,64,256]{2,1,0:T(8,128)S(1)} %collective-permute-done.21.refs_0_, f32[32,64,256]{2,1,0:T(8,128)S(1)} %get-tuple-element.124.refs_1_, ...), custom_call_target="tpu_custom_call", output_to_operand_aliasing={{0}: (2, {}), {1}: (3, {})} | custom-call | flops 31457280 | bytes 1048576 | tf_op jit(solution)/shard_map/side_b5/pallas_call | solution.py:234
  133.0 4.0 %collective-permute-done.24 = f32[8,16,256]{2,1,0:T(8,128)S(1)} collective-permute-done((f32[8,16,256]{2,1,0:T(8,128)S(1)}, f32[8,16,256]{2,1,0:T(8,128)S(1)}, u32[]{:S(2)}, u32[]{:S(2)}) %collective-permute-start.24) | collective-permute-done | bytes 131104 | tf_op jit(solution)/shard_map/ppermute | solution.py:261
  (76 shorter events, 50.0 us)
Async XLA Ops:
  2.9 4.8 %collective-permute-start.2 = (f32[1,16,256]{2,1,0:T(8,128)S(1)}, f32[1,16,256]{2,1,0:T(8,128)S(1)}, u32[]{:S(2)}, u32[]{:S(2)}) collective-permute-start(f32[1,16,256]{2,1,0:T(8,128)S(1)} %maximum_bitcast_fusion), channel_id=1, source_target_pairs={{0,1},{1,0},{2,3},{3,2},{4,5},{5,4},{6,7},{7,6},{8,9},{9,8},{10,11... | collective-permute-start | bytes 49160 | tf_op jit(solution)/shard_map/ppermute | solution.py:261
  4.4 19.2 %collective-permute-start = (f32[8,64,256]{2,1,0:T(8,128)}, f32[8,64,256]{2,1,0:T(8,128)S(1)}, u32[]{:S(2)}, u32[]{:S(2)}) collective-permute-start(f32[8,64,256]{2,1,0:T(8,128)} %bitcast.33), channel_id=1, source_target_pairs={{0,1},{1,0},{2,3},{3,2},{4,5},{5,4},{6,7},{7,6},{8,9},{9,8},{10,11... | collective-permute-start | bytes 1572872 | tf_op jit(solution)/shard_map/ppermute | solution.py:261
  7.7 4.0 %collective-permute-start.6 = (f32[2,16,256]{2,1,0:T(8,128)S(1)}, f32[2,16,256]{2,1,0:T(8,128)S(1)}, u32[]{:S(2)}, u32[]{:S(2)}) collective-permute-start(f32[2,16,256]{2,1,0:T(8,128)S(1)} %pad_maximum_fusion.5), channel_id=1, source_target_pairs={{0,2},{1,3},{2,0},{3,1},{4,6},{5,7},{6,4},{7,5},{8,10},{9,11},{10,... | collective-permute-start | bytes 98312 | tf_op jit(solution)/shard_map/ppermute | solution.py:261
  11.7 5.2 %collective-permute-start.7 = (f32[4,16,256]{2,1,0:T(8,128)S(1)}, f32[4,16,256]{2,1,0:T(8,128)S(1)}, u32[]{:S(2)}, u32[]{:S(2)}) collective-permute-start(f32[4,16,256]{2,1,0:T(8,128)S(1)} %pad_maximum_fusion.4), channel_id=1, source_target_pairs={{0,4},{1,5},{2,6},{3,7},{4,0},{5,1},{6,2},{7,3},{8,12},{9,13},{10,... | collective-permute-start | bytes 196616 | tf_op jit(solution)/shard_map/ppermute | solution.py:261
  11.8 11.8 %collective-permute-start.4 = (f32[4,64,256]{2,1,0:T(8,128)S(1)}, f32[4,64,256]{2,1,0:T(8,128)S(1)}, u32[]{:S(2)}, u32[]{:S(2)}) collective-permute-start(f32[4,64,256]{2,1,0:T(8,128)S(1)} %pad_maximum_fusion.2), channel_id=1, source_target_pairs={{0,1},{1,0},{2,3},{3,2},{4,5},{5,4},{6,7},{7,6},{8,9},{9,8},{10,11... | collective-permute-start | bytes 786440 | tf_op jit(solution)/shard_map/ppermute | solution.py:261
  17.0 12.5 %collective-permute-start.8 = (f32[6,64,256]{2,1,0:T(8,128)S(1)}, f32[6,64,256]{2,1,0:T(8,128)S(1)}, u32[]{:S(2)}, u32[]{:S(2)}) collective-permute-start(f32[6,64,256]{2,1,0:T(8,128)S(1)} %pad_maximum_fusion.1), channel_id=1, source_target_pairs={{2,0},{4,2},{6,4},{1,3},{3,5},{5,7},{10,8},{12,10},{14,12},{9,11},... | collective-permute-start | bytes 1179656 | tf_op jit(solution)/shard_map/ppermute | solution.py:261
  23.6 6.9 %collective-permute-start.9 = (f32[2,64,256]{2,1,0:T(8,128)S(1)}, f32[2,64,256]{2,1,0:T(8,128)S(1)}, u32[]{:S(2)}, u32[]{:S(2)}) collective-permute-start(f32[2,64,256]{2,1,0:T(8,128)S(1)} %slice.7), channel_id=1, source_target_pairs={{0,2},{2,4},{4,6},{3,1},{5,3},{7,5},{8,10},{10,12},{12,14},{11,9},... | collective-permute-start | bytes 393224 | tf_op jit(solution)/shard_map/ppermute | solution.py:261
  27.1 21.3 %collective-permute-start.11 = (f32[8,64,256]{2,1,0:T(8,128)S(1)}, f32[8,64,256]{2,1,0:T(8,128)}, u32[]{:S(2)}, u32[]{:S(2)}) collective-permute-start(f32[8,64,256]{2,1,0:T(8,128)S(1)} %bitcast.34), channel_id=1, source_target_pairs={{2,0},{4,2},{6,4},{1,3},{3,5},{5,7},{10,8},{12,10},{14,12},{9,11},... | collective-permute-start | bytes 1572872 | tf_op jit(solution)/shard_map/ppermute | solution.py:261
  31.3 17.1 %collective-permute-start.10 = (f32[8,64,256]{2,1,0:T(8,128)}, f32[8,64,256]{2,1,0:T(8,128)}, u32[]{:S(2)}, u32[]{:S(2)}) collective-permute-start(f32[8,64,256]{2,1,0:T(8,128)} %pad_maximum_fusion), channel_id=1, source_target_pairs={{0,8},{1,9},{2,10},{3,11},{4,12},{5,13},{6,14},{7,15},{8,0},{9,1},... | collective-permute-start | bytes 1572872 | tf_op jit(solution)/shard_map/ppermute | solution.py:261
  31.3 9.2 %collective-permute-start.3 = (f32[4,64,256]{2,1,0:T(8,128)S(1)}, f32[4,64,256]{2,1,0:T(8,128)}, u32[]{:S(2)}, u32[]{:S(2)}) collective-permute-start(f32[4,64,256]{2,1,0:T(8,128)S(1)} %get-tuple-element.68), channel_id=1, source_target_pairs={{0,1},{1,0},{2,3},{3,2},{4,5},{5,4},{6,7},{7,6},{8,9},{9,8},{10,11... | collective-permute-start | bytes 786440 | tf_op jit(solution)/shard_map/ppermute | solution.py:261
  32.0 21.7 %collective-permute-start.1 = (f32[8,64,256]{2,1,0:T(8,128)S(1)}, f32[8,64,256]{2,1,0:T(8,128)S(1)}, u32[]{:S(2)}, u32[]{:S(2)}) collective-permute-start(f32[8,64,256]{2,1,0:T(8,128)S(1)} %collective-permute-done.cur_oth), channel_id=1, source_target_pairs={{0,2},{2,4},{4,6},{3,1},{5,3},{7,5},{8,10},{10,12},{12,14},{11,9},... | collective-permute-start | bytes 1572872 | tf_op jit(solution)/shard_map/ppermute | solution.py:261
  34.8 12.1 %collective-permute-start.12 = (f32[4,64,256]{2,1,0:T(8,128)}, f32[4,64,256]{2,1,0:T(8,128)}, u32[]{:S(2)}, u32[]{:S(2)}) collective-permute-start(f32[4,64,256]{2,1,0:T(8,128)} %get-tuple-element.73), channel_id=1, source_target_pairs={{0,1},{1,0},{2,3},{3,2},{4,5},{5,4},{6,7},{7,6},{8,9},{9,8},{10,11... | collective-permute-start | bytes 786440 | tf_op jit(solution)/shard_map/ppermute | solution.py:261
  40.5 13.1 %collective-permute-start.5 = (f32[4,64,256]{2,1,0:T(8,128)}, f32[4,64,256]{2,1,0:T(8,128)}, u32[]{:S(2)}, u32[]{:S(2)}) collective-permute-start(f32[4,64,256]{2,1,0:T(8,128)} %collective-permute-done.3.lat_edge), channel_id=1, source_target_pairs={{0,2},{2,4},{4,6},{3,1},{5,3},{7,5},{8,10},{10,12},{12,14},{11,9},... | collective-permute-start | bytes 786440 | tf_op jit(solution)/shard_map/ppermute | solution.py:261
  56.2 13.3 %collective-permute-start.14 = (f32[8,64,256]{2,1,0:T(8,128)S(1)}, f32[8,64,256]{2,1,0:T(8,128)S(1)}, u32[]{:S(2)}, u32[]{:S(2)}) collective-permute-start(f32[8,64,256]{2,1,0:T(8,128)S(1)} %get-tuple-element.87), channel_id=1, source_target_pairs={{0,2},{1,3},{2,0},{3,1},{4,6},{5,7},{6,4},{7,5},{8,10},{9,11},{10,... | collective-permute-start | bytes 1572872 | tf_op jit(solution)/shard_map/ppermute | solution.py:261
  59.4 13.6 %collective-permute-start.13 = (f32[8,64,256]{2,1,0:T(8,128)S(1)}, f32[8,64,256]{2,1,0:T(8,128)S(1)}, u32[]{:S(2)}, u32[]{:S(2)}) collective-permute-start(f32[8,64,256]{2,1,0:T(8,128)S(1)} %get-tuple-element.86), channel_id=1, source_target_pairs={{0,1},{1,0},{2,4},{3,5},{4,2},{5,3},{6,7},{7,6},{8,9},{9,8},{10,12... | collective-permute-start | bytes 1572872 | tf_op jit(solution)/shard_map/ppermute | solution.py:261
  71.4 12.5 %collective-permute-start.16 = (f32[8,64,256]{2,1,0:T(8,128)S(1)}, f32[8,64,256]{2,1,0:T(8,128)S(1)}, u32[]{:S(2)}, u32[]{:S(2)}) collective-permute-start(f32[8,64,256]{2,1,0:T(8,128)S(1)} %get-tuple-element.95), channel_id=1, source_target_pairs={{0,2},{1,3},{2,0},{3,1},{4,6},{5,7},{6,4},{7,5},{8,10},{9,11},{10,... | collective-permute-start | bytes 1572872 | tf_op jit(solution)/shard_map/ppermute | solution.py:261
  74.9 12.7 %collective-permute-start.15 = (f32[8,64,256]{2,1,0:T(8,128)S(1)}, f32[8,64,256]{2,1,0:T(8,128)S(1)}, u32[]{:S(2)}, u32[]{:S(2)}) collective-permute-start(f32[8,64,256]{2,1,0:T(8,128)S(1)} %get-tuple-element.94), channel_id=1, source_target_pairs={{0,1},{1,0},{2,4},{3,5},{4,2},{5,3},{6,7},{7,6},{8,9},{9,8},{10,12... | collective-permute-start | bytes 1572872 | tf_op jit(solution)/shard_map/ppermute | solution.py:261
  85.8 11.8 %collective-permute-start.18 = (f32[8,64,256]{2,1,0:T(8,128)S(1)}, f32[8,64,256]{2,1,0:T(8,128)S(1)}, u32[]{:S(2)}, u32[]{:S(2)}) collective-permute-start(f32[8,64,256]{2,1,0:T(8,128)S(1)} %get-tuple-element.103), channel_id=1, source_target_pairs={{0,2},{1,3},{2,0},{3,1},{4,6},{5,7},{6,4},{7,5},{8,10},{9,11},{10,... | collective-permute-start | bytes 1572872 | tf_op jit(solution)/shard_map/ppermute | solution.py:261
  89.6 11.9 %collective-permute-start.17 = (f32[8,64,256]{2,1,0:T(8,128)S(1)}, f32[8,64,256]{2,1,0:T(8,128)S(1)}, u32[]{:S(2)}, u32[]{:S(2)}) collective-permute-start(f32[8,64,256]{2,1,0:T(8,128)S(1)} %get-tuple-element.102), channel_id=1, source_target_pairs={{0,1},{1,0},{2,4},{3,5},{4,2},{5,3},{6,7},{7,6},{8,9},{9,8},{10,12... | collective-permute-start | bytes 1572872 | tf_op jit(solution)/shard_map/ppermute | solution.py:261
  99.7 10.9 %collective-permute-start.20 = (f32[8,64,256]{2,1,0:T(8,128)S(1)}, f32[8,64,256]{2,1,0:T(8,128)S(1)}, u32[]{:S(2)}, u32[]{:S(2)}) collective-permute-start(f32[8,64,256]{2,1,0:T(8,128)S(1)} %get-tuple-element.111), channel_id=1, source_target_pairs={{0,2},{1,3},{2,0},{3,1},{4,6},{5,7},{6,4},{7,5},{8,10},{9,11},{10,... | collective-permute-start | bytes 1572872 | tf_op jit(solution)/shard_map/ppermute | solution.py:261
  103.4 10.8 %collective-permute-start.19 = (f32[8,64,256]{2,1,0:T(8,128)S(1)}, f32[8,64,256]{2,1,0:T(8,128)S(1)}, u32[]{:S(2)}, u32[]{:S(2)}) collective-permute-start(f32[8,64,256]{2,1,0:T(8,128)S(1)} %get-tuple-element.110), channel_id=1, source_target_pairs={{0,1},{1,0},{2,4},{3,5},{4,2},{5,3},{6,7},{7,6},{8,9},{9,8},{10,12... | collective-permute-start | bytes 1572872 | tf_op jit(solution)/shard_map/ppermute | solution.py:261
  112.5 10.0 %collective-permute-start.22 = (f32[8,64,256]{2,1,0:T(8,128)S(1)}, f32[8,64,256]{2,1,0:T(8,128)S(1)}, u32[]{:S(2)}, u32[]{:S(2)}) collective-permute-start(f32[8,64,256]{2,1,0:T(8,128)S(1)} %get-tuple-element.119), channel_id=1, source_target_pairs={{0,2},{1,3},{2,0},{3,1},{4,6},{5,7},{6,4},{7,5},{8,10},{9,11},{10,... | collective-permute-start | bytes 1572872 | tf_op jit(solution)/shard_map/ppermute | solution.py:261
  116.2 9.7 %collective-permute-start.21 = (f32[8,64,256]{2,1,0:T(8,128)S(1)}, f32[8,64,256]{2,1,0:T(8,128)S(1)}, u32[]{:S(2)}, u32[]{:S(2)}) collective-permute-start(f32[8,64,256]{2,1,0:T(8,128)S(1)} %get-tuple-element.118), channel_id=1, source_target_pairs={{0,1},{1,0},{2,4},{3,5},{4,2},{5,3},{6,7},{7,6},{8,9},{9,8},{10,12... | collective-permute-start | bytes 1572872 | tf_op jit(solution)/shard_map/ppermute | solution.py:261
  131.4 5.6 %collective-permute-start.24 = (f32[8,16,256]{2,1,0:T(8,128)S(1)}, f32[8,16,256]{2,1,0:T(8,128)S(1)}, u32[]{:S(2)}, u32[]{:S(2)}) collective-permute-start(f32[8,16,256]{2,1,0:T(8,128)S(1)} %get-tuple-element.133), channel_id=1, source_target_pairs={{0,16},{1,17},{2,18},{3,19},{4,20},{5,21},{6,22},{7,23},{8,24},{9,... | collective-permute-start | bytes 393224 | tf_op jit(solution)/shard_map/ppermute | solution.py:261
  (5 other events, 82.4 us)

commit v4 on v3

--- a/solution.py
+++ b/solution.py
@@ -100,6 +100,23 @@
     return jnp.where(flag == 1, x, 0.0)
 
 
+def pack_kernel(scal_ref, later_ref, c_ref, edge_ref, rest_ref, sems):
+    half = rest_ref.shape[0]
+    two = half // 2
+    y, core = scal_ref[2], scal_ref[3]
+    copies = [
+        (later_ref.at[pl.ds(half * y, half)], edge_ref.at[0:half]),
+        (c_ref.at[pl.ds(half * y + two * core, two)], edge_ref.at[half : half + two]),
+        (c_ref.at[pl.ds(half * (1 - y) + two * core, two)], edge_ref.at[half + two : 2 * half]),
+        (later_ref.at[pl.ds(half * (1 - y), half)], rest_ref),
+    ]
+    copies = [pltpu.make_async_copy(src, dst, sems.at[i]) for i, (src, dst) in enumerate(copies)]
+    for copy in copies:
+        copy.start()
+    for copy in copies:
+        copy.wait()
+
+
 def field_kernel(scal_ref, cur_own, cur_oth, lat_own, lat_edge, lat_rest, e_ref, o_ref, wz_ref, wy_ref):
     length, ny, nz = cur_own.shape
     half = length // 2
@@ -124,7 +141,7 @@
     return local_of(scal_ref, g, length)
 
 
-def model_kernel(scal_ref, c_own, c_oth, c_core, d_cur, d_edge, r_c, e_in, o_in, a_ref, c_ref, e_ref, o_ref):
+def model_kernel(scal_ref, c_own, m_oth, c_core, d_cur, d_edge, r_edge, e_in, o_in, a_ref, c_ref, e_ref, o_ref):
     length = c_own.shape[0]
     half, two = length // 2, length // 4
     y, core = scal_ref[2], scal_ref[3]
@@ -138,17 +155,18 @@
         put(local_of(scal_ref, y * length + p, length), c_own[p])
     base = (1 - y) * length
     for p in range(two):
-        for who, piece, at in ((core, c_oth, 0), (1 - core, c_core, 0)):
+        for who, piece, at in ((core, m_oth, half), (1 - core, c_core, 0)):
             put(local_of(scal_ref, base + half * (1 - y) + two * who + p, length), piece[at + p])
             put(local_of(scal_ref, base + half * y + two * who + p, length), piece[at + two + p])
         put(halo_at(scal_ref, 1 - y, two * core + p, half, length), keep_if(near, d_edge[half + p]))
         put(halo_at(scal_ref, 1 - y, two * (1 - core) + p, half, length), keep_if(near, c_core[half + p]))
-        put(halo_at(scal_ref, y, two * core + p, half, length), keep_if(far, r_c[p]))
+        put(halo_at(scal_ref, y, two * core + p, half, length), keep_if(far, r_edge[half + p]))
         put(halo_at(scal_ref, y, two * (1 - core) + p, half, length), keep_if(far, c_core[half + two + p]))
     for p in range(length):
         e_ref[halo_at(scal_ref, 1 - y, p, length, length) + 8] = keep_if(near, d_cur[p])
     for p in range(half):
         o_ref[halo_at(scal_ref, 1 - y, p, half, length) + 4] = keep_if(near, d_edge[p])
+        o_ref[halo_at(scal_ref, y, p, half, length) + 4] = keep_if(far, r_edge[p])
 
 
 def inner_kernel(scal_ref, e_ref, o_in, a_ref, c_ref, q_ref, wz_ref, wy_ref, f_ref, g_in, o_ref, g_ref, *, r, length):
@@ -166,14 +184,12 @@
     advance(o_ref, 4, e_ref, 8, e_ref, 8, *args, 8 if side == "a" else 0, 2, 2 * r + 1, extra=new)
 
 
-def first_kernel(scal_ref, r_cur, r_lat, e_in, o_in, a_ref, c_ref, q_ref, wz_ref, wy_ref, e_ref, o_ref, new):
+def first_kernel(scal_ref, r_cur, e_in, o_in, a_ref, c_ref, q_ref, wz_ref, wy_ref, e_ref, o_ref, new):
     length = r_cur.shape[0]
     y = scal_ref[2]
     far = scal_ref[5 + y]
     for p in range(length):
         e_ref[halo_at(scal_ref, y, p, length, length) + 8] = keep_if(far, r_cur[p])
-    for p in range(length // 2):
-        o_ref[halo_at(scal_ref, y, p, length // 2, length) + 4] = keep_if(far, r_lat[p])
     side_steps("a", 0, e_ref, o_ref, (a_ref, c_ref, q_ref, wz_ref, wy_ref), new)
 
 
@@ -284,40 +300,36 @@
     def after(x, *others):
         return lax.optimization_barrier((x, *others))[0]
 
-    half, two = length // 2, length // 4
-    cut = lambda x, at, size: lax.dynamic_slice_in_dim(x, at, size, 0)
-    y_cur = move(cur, swap_y)
-
     number = me * width + jnp.arange(width, dtype=jnp.int32)
     live = jnp.where(number < trace_counts[0], 1.0, 0.0)
     code = (owners[0, :, 0] * (length * ny) + surface_cells[0]).astype(F32)
     gathered = jnp.concatenate([traces * live[None], code[None], jnp.zeros((16 - steps - 1, width), F32)], 0)[None]
-    reach = 1
+    reach = 2
     while reach < n:
         gathered = jnp.concatenate([gathered, move(gathered, everywhere([(i, i ^ reach) for i in range(n)]))], 0)
-        if reach == 1:
-            early = gathered
         reach *= 2
 
-    c_edge = cut(courant_sq, half * y + two * core, two)
-    c_rest = cut(courant_sq, half * (1 - y) + two * core, two)
-    l_edge = cut(later, half * y, half)
-    l_rest = cut(later, half * (1 - y), half)
-    d_cur = move(cur, direct)
-    y_c = move(after(jnp.concatenate([c_edge, c_rest], 0), early), swap_y)
-    y_edge = move(after(l_edge, early), swap_y)
-    y_rest = move(after(l_rest, early), swap_y)
-    d_edge = move(after(jnp.concatenate([l_edge, c_edge], 0), gathered), direct)
-
-    y_c = after(y_c, y_cur)
-    y_edge = after(y_edge, y_c)
-    y_rest = after(y_rest, y_edge)
-    r_cur = move(y_cur, relay)
-    r_c = move(y_c[:two], relay)
-    r_lat = move(y_edge, relay)
-    x_c = move(jnp.concatenate([y_c, d_edge[half:], r_c], 0), swap_core)
-
+    half, two = length // 2, length // 4
     plane = lambda k: VM((k, ny, nz), F32)
+    edge, rest = pl.pallas_call(
+        pack_kernel,
+        out_shape=[plane(length), plane(half)],
+        in_specs=[pl.BlockSpec(memory_space=pltpu.SMEM)] + [pl.BlockSpec(memory_space=pl.ANY)] * 2,
+        out_specs=[pl.BlockSpec(memory_space=VM)] * 2,
+        scratch_shapes=[pltpu.SemaphoreType.DMA((4,))],
+        compiler_params=pltpu.CompilerParams(vmem_limit_bytes=LIMIT),
+        name="pack",
+    )(scal, *[pltpu.with_memory_space_constraint(x, pltpu.HBM) for x in (later, courant_sq)])
+    y_edge = move(edge, swap_y)
+    y_cur = move(after(cur, edge), swap_y)
+    y_rest = move(after(rest, y_edge), swap_y)
+    d_edge = move(after(edge, gathered), direct)
+    d_cur = move(after(cur, gathered), direct)
+    gathered = jnp.concatenate([gathered, move(gathered, swap_y)], 0)
+    r_edge = move(y_edge, relay)
+    r_cur = move(after(y_cur, gathered), relay)
+    x_c = move(jnp.concatenate([y_edge[half:], d_edge[half : half + two], r_edge[half : half + two]], 0), swap_core)
+
     e, o, wz, wy = call(
         field_kernel,
         [plane(32), plane(24), VM((2 * nz, nz), BF16), VM((4 * ny, 8 * ny), BF16)],
@@ -334,7 +346,7 @@
     a, c, e, o = call(
         model_kernel,
         [plane(24), plane(24), plane(32), plane(24)],
-        [scal, courant_sq, y_c, x_c, d_cur, d_edge, r_c, e, o],
+        [scal, courant_sq, y_edge, x_c, d_cur, d_edge, r_edge, e, o],
         {7: 2, 8: 3},
         free=(1,),
         name="model",
@@ -359,7 +371,7 @@
         outs = [plane(32), plane(24)] + ([] if last else [plane(8)])
         model = [a, c, q, wz, wy]
         if r == 0:
-            e, o, send_a = call(first_kernel, outs, [scal, r_cur, r_lat, e, o] + model, {3: 0, 4: 1}, flops=work, name="first")
+            e, o, send_a = call(first_kernel, outs, [scal, r_cur, e, o] + model, {2: 0, 3: 1}, flops=work, name="first")
             kern = functools.partial(side_kernel, r=r, side="b", recv=False, last=False)
             e, o, send_b = call(kern, outs, [scal, e, o] + model, {1: 0, 2: 1}, flops=work, name="side_b0")
             continue

time: 138 us -> 127 us (0.920)
  starting transfers between devices: 32 us -> 26.4 us
  waiting for transfers between devices: 58.8 us -> 55.2 us
  local copies, waits for them, and re-layouts: 3.47 us -> 1.12 us
    ppermute x25 -> x23, starting transfers between devices: 32 us -> 26.4 us  [move(): return lax.ppermute(x, ('shot', 'space'), pairs)]
    ppermute x25 -> x23, waiting for transfers between devices: 58.8 us -> 55.2 us  [move(): return lax.ppermute(x, ('shot', 'space'), pairs)]
    dynamic_slice x2 -> x0, local copies, waits for them, and re-layouts: 2.81 us -> none  [shards(): cut = lambda x, at, size: lax.dynamic_slice_in_dim(x, at, size, 0)]
    pallas_call x23, Pallas kernels: 38.6 us -> 36.9 us  [call(): pl.pallas_call(kernel, out_shape=out_shapes, in_specs=specs, out_specs=ja...]
    pallas_call x0 -> x1, Pallas kernels: none -> 1.73 us  [shards(): pl.pallas_call(pack_kernel, out_shape=[plane(length), plane(half)], in_sp...]
  transfers between devices with their start and end apart: 25 -> 23, of which waited for: 14 -> 14; matrix products, arithmetic and copies ran while one was open for 3% -> 1% of each run, Pallas kernels for 23% -> 25%
where the time goes in v4:
time: 127 us; the launch traced here: 125 us
  waiting for transfers between devices  55.2 us (43%)
  Pallas kernels  38.6 us (30%)
  starting transfers between devices  26.4 us (21%)
  other arithmetic  2.22 us (2%)
  between operations  1.69 us (1%)
    ppermute x23, waiting for transfers between devices, move(): return lax.ppermute(x, ('shot', 'space'), pairs)  55.2 us
    pallas_call x23, Pallas kernels, call(): pl.pallas_call(kernel, out_shape=out_shapes, in_specs=specs, out_specs=ja...  36.9 us
    ppermute x23, starting transfers between devices, move(): return lax.ppermute(x, ('shot', 'space'), pairs)  26.4 us
  transfers between devices with their start and end apart: 23, of which 14 were waited for; matrix products, arithmetic and copies ran while one was open for 1% of the time, Pallas kernels for 25%

profile of v4, /device:TPU:16, one launch (start us, length us, event | category | flops | bytes accessed | tf_op | source)
XLA Modules:
  0.0 125.3 jit_solution(1984879964685277414)
XLA Ops:
  7.9 2.2 %collective-permute-done.1 = f32[1,16,256]{2,1,0:T(8,128)S(1)} collective-permute-done((f32[1,16,256]{2,1,0:T(8,128)S(1)}, f32[1,16,256]{2,1,0:T(8,128)S(1)}, u32[]{:S(2)}, u32[]{:S(2)}) %collective-permute-start.1) | collective-permute-done | bytes 16416 | tf_op jit(solution)/shard_map/ppermute | solution.py:277
  10.4 4.5 %collective-permute-done.2 = f32[2,16,256]{2,1,0:T(8,128)S(1)} collective-permute-done((f32[2,16,256]{2,1,0:T(8,128)S(1)}, f32[2,16,256]{2,1,0:T(8,128)S(1)}, u32[]{:S(2)}, u32[]{:S(2)}) %collective-permute-start.2) | collective-permute-done | bytes 32800 | tf_op jit(solution)/shard_map/ppermute | solution.py:277
  14.9 2.3 %collective-permute-start.6 = (f32[8,64,256]{2,1,0:T(8,128)S(1)}, f32[8,64,256]{2,1,0:T(8,128)S(1)}, u32[]{:S(2)}, u32[]{:S(2)}) collective-permute-start(f32[8,64,256]{2,1,0:T(8,128)S(1)} %get-tuple-element.71), channel_id=1, source_target_pairs={{2,0},{4,2},{6,4},{1,3},{3,5},{5,7},{10,8},{12,10},{14,12},{9,11},... | collective-permute-start | bytes 1572872 | tf_op jit(solution)/shard_map/ppermute | solution.py:277
  17.3 3.5 %collective-permute-start.7 = (f32[8,64,256]{2,1,0:T(8,128)S(1)}, f32[8,64,256]{2,1,0:T(8,128)S(1)}, u32[]{:S(2)}, u32[]{:S(2)}) collective-permute-start(f32[8,64,256]{2,1,0:T(8,128)S(1)} %collective-permute-done.5.lat_edge.m_oth), channel_id=1, source_target_pairs={{0,2},{2,4},{4,6},{3,1},{5,3},{7,5},{8,10},{10,12},{12,14},{11,9},... | collective-permute-start | bytes 1572872 | tf_op jit(solution)/shard_map/ppermute | solution.py:277
  22.9 2.3 %collective-permute-start.9 = (f32[8,64,256]{2,1,0:T(8,128)}, f32[8,64,256]{2,1,0:T(8,128)S(1)}, u32[]{:S(2)}, u32[]{:S(2)}) collective-permute-start(f32[8,64,256]{2,1,0:T(8,128)} %bitcast.31), channel_id=1, source_target_pairs={{2,0},{4,2},{6,4},{1,3},{3,5},{5,7},{10,8},{12,10},{14,12},{9,11},... | collective-permute-start | bytes 1572872 | tf_op jit(solution)/shard_map/ppermute | solution.py:277
  25.3 6.4 %collective-permute-done.6.d_edge = f32[8,64,256]{2,1,0:T(8,128)S(1)} collective-permute-done((f32[8,64,256]{2,1,0:T(8,128)S(1)}, f32[8,64,256]{2,1,0:T(8,128)S(1)}, u32[]{:S(2)}, u32[]{:S(2)}) %collective-permute-start.6) | collective-permute-done | bytes 524320 | tf_op jit(solution)/shard_map/ppermute | solution.py:277
  31.9 2.1 %collective-permute-done.3 = f32[4,16,256]{2,1,0:T(8,128)S(1)} collective-permute-done((f32[4,16,256]{2,1,0:T(8,128)S(1)}, f32[4,16,256]{2,1,0:T(8,128)S(1)}, u32[]{:S(2)}, u32[]{:S(2)}) %collective-permute-start.3) | collective-permute-done | bytes 65568 | tf_op jit(solution)/shard_map/ppermute | solution.py:277
  34.0 2.2 %collective-permute-start.4 = (f32[8,64,256]{2,1,0:T(8,128)S(1)}, f32[8,64,256]{2,1,0:T(8,128)S(1)}, u32[]{:S(2)}, u32[]{:S(2)}) collective-permute-start(f32[8,64,256]{2,1,0:T(8,128)S(1)} %collective-permute-done.cur_oth), channel_id=1, source_target_pairs={{0,2},{2,4},{4,6},{3,1},{5,3},{7,5},{8,10},{10,12},{12,14},{11,9},... | collective-permute-start | bytes 1572872 | tf_op jit(solution)/shard_map/ppermute | solution.py:277
  36.8 2.8 %receivers.1.q_ref.refs_4_.refs_5_ = f32[3,64,128]{2,1,0:T(8,128)S(1)} custom-call(s32[7]{0:T(128)S(1)} %stack.31.scal_ref, f32[8,16,256]{2,1,0:T(8,128)S(1)} %pad_maximum_fusion.1.gathered_ref), custom_call_target="tpu_custom_call" | custom-call | bytes 1048576 | tf_op jit(solution)/shard_map/receivers/pallas_call | solution.py:250
  39.6 3.5 %collective-permute-done.10.lat_rest = f32[4,64,256]{2,1,0:T(8,128)S(1)} collective-permute-done((f32[4,64,256]{2,1,0:T(8,128)S(1)}, f32[4,64,256]{2,1,0:T(8,128)S(1)}, u32[]{:S(2)}, u32[]{:S(2)}) %collective-permute-start.10) | collective-permute-done | bytes 262176 | tf_op jit(solution)/shard_map/ppermute | solution.py:277
  48.1 2.0 %first.1 = (f32[32,64,256]{2,1,0:T(8,128)S(1)}, f32[24,64,256]{2,1,0:T(8,128)S(1)}, f32[8,64,256]{2,1,0:T(8,128)S(1)}) custom-call(s32[7]{0:T(128)S(1)} %stack.31.scal_ref, f32[8,64,256]{2,1,0:T(8,128)S(1)} %collective-permute-done.4.r_cur, f32[32,64,256]{2,1,0:T(8,128)S(1)} %get-tuple-element.77.e_ref.e_in, ...), custom_call_target="tpu_custom_call", output_to_operand_aliasing={{0}: (2, {}), {1}: (3, {})} | custom-call | flops 31457280 | bytes 1048576 | tf_op jit(solution)/shard_map/first/pallas_call | solution.py:250
  51.0 1.9 %side_b0.1 = (f32[32,64,256]{2,1,0:T(8,128)S(1)}, f32[24,64,256]{2,1,0:T(8,128)S(1)}, f32[8,64,256]{2,1,0:T(8,128)S(1)}) custom-call(s32[7]{0:T(128)S(1)} %stack.31.scal_ref, f32[32,64,256]{2,1,0:T(8,128)S(1)} %get-tuple-element.84.refs_0_, f32[24,64,256]{2,1,0:T(8,128)S(1)} %get-tuple-element.85.refs_1_, ...), custom_call_target="tpu_custom_call", output_to_operand_aliasing={{0}: (1, {}), {1}: (2, {})} | custom-call | flops 31457280 | bytes 1048576 | tf_op jit(solution)/shard_map/side_b0/pallas_call | solution.py:250
  54.5 7.0 %collective-permute-done.12.refs_0_ = f32[8,64,256]{2,1,0:T(8,128)S(1)} collective-permute-done((f32[8,64,256]{2,1,0:T(8,128)S(1)}, f32[8,64,256]{2,1,0:T(8,128)S(1)}, u32[]{:S(2)}, u32[]{:S(2)}) %collective-permute-start.12) | collective-permute-done | bytes 524320 | tf_op jit(solution)/shard_map/ppermute | solution.py:277
  68.3 5.7 %collective-permute-done.14.refs_0_ = f32[8,64,256]{2,1,0:T(8,128)S(1)} collective-permute-done((f32[8,64,256]{2,1,0:T(8,128)S(1)}, f32[8,64,256]{2,1,0:T(8,128)S(1)}, u32[]{:S(2)}, u32[]{:S(2)}) %collective-permute-start.14) | collective-permute-done | bytes 524320 | tf_op jit(solution)/shard_map/ppermute | solution.py:277
  77.8 2.0 %side_b2.1 = (f32[32,64,256]{2,1,0:T(8,128)S(1)}, f32[24,64,256]{2,1,0:T(8,128)S(1)}, f32[8,64,256]{2,1,0:T(8,128)S(1)}) custom-call(s32[7]{0:T(128)S(1)} %stack.31.scal_ref, f32[8,64,256]{2,1,0:T(8,128)S(1)} %collective-permute-done.13.refs_0_, f32[32,64,256]{2,1,0:T(8,128)S(1)} %get-tuple-element.100.refs_1_, ...), custom_call_target="tpu_custom_call", output_to_operand_aliasing={{0}: (2, {}), {1}: (3, {})} | custom-call | flops 31457280 | bytes 1048576 | tf_op jit(solution)/shard_map/side_b2/pallas_call | solution.py:250
  81.2 4.8 %collective-permute-done.16.refs_0_ = f32[8,64,256]{2,1,0:T(8,128)S(1)} collective-permute-done((f32[8,64,256]{2,1,0:T(8,128)S(1)}, f32[8,64,256]{2,1,0:T(8,128)S(1)}, u32[]{:S(2)}, u32[]{:S(2)}) %collective-permute-start.16) | collective-permute-done | bytes 524320 | tf_op jit(solution)/shard_map/ppermute | solution.py:277
  86.0 2.1 %side_a3.1 = (f32[32,64,256]{2,1,0:T(8,128)S(1)}, f32[24,64,256]{2,1,0:T(8,128)S(1)}, f32[8,64,256]{2,1,0:T(8,128)S(1)}) custom-call(s32[7]{0:T(128)S(1)} %stack.31.scal_ref, f32[8,64,256]{2,1,0:T(8,128)S(1)} %collective-permute-done.16.refs_0_, f32[32,64,256]{2,1,0:T(8,128)S(1)} %get-tuple-element.104.e_ref.refs_1_, ...), custom_call_target="tpu_custom_call", output_to_operand_aliasing={{0}: (2, {}), {1}: (3, {})} | custom-call | flops 31457280 | bytes 1048576 | tf_op jit(solution)/shard_map/side_a3/pallas_call | solution.py:250
  89.9 2.0 %side_b3.1 = (f32[32,64,256]{2,1,0:T(8,128)S(1)}, f32[24,64,256]{2,1,0:T(8,128)S(1)}, f32[8,64,256]{2,1,0:T(8,128)S(1)}) custom-call(s32[7]{0:T(128)S(1)} %stack.31.scal_ref, f32[8,64,256]{2,1,0:T(8,128)S(1)} %collective-permute-done.15.refs_0_, f32[32,64,256]{2,1,0:T(8,128)S(1)} %get-tuple-element.108.refs_1_, ...), custom_call_target="tpu_custom_call", output_to_operand_aliasing={{0}: (2, {}), {1}: (3, {})} | custom-call | flops 31457280 | bytes 1048576 | tf_op jit(solution)/shard_map/side_b3/pallas_call | solution.py:250
  93.4 5.3 %collective-permute-done.18.refs_0_ = f32[8,64,256]{2,1,0:T(8,128)S(1)} collective-permute-done((f32[8,64,256]{2,1,0:T(8,128)S(1)}, f32[8,64,256]{2,1,0:T(8,128)S(1)}, u32[]{:S(2)}, u32[]{:S(2)}) %collective-permute-start.18) | collective-permute-done | bytes 524320 | tf_op jit(solution)/shard_map/ppermute | solution.py:277
  102.3 2.0 %side_b4.1 = (f32[32,64,256]{2,1,0:T(8,128)S(1)}, f32[24,64,256]{2,1,0:T(8,128)S(1)}, f32[8,64,256]{2,1,0:T(8,128)S(1)}) custom-call(s32[7]{0:T(128)S(1)} %stack.31.scal_ref, f32[8,64,256]{2,1,0:T(8,128)S(1)} %collective-permute-done.17.refs_0_, f32[32,64,256]{2,1,0:T(8,128)S(1)} %get-tuple-element.116.refs_1_, ...), custom_call_target="tpu_custom_call", output_to_operand_aliasing={{0}: (2, {}), {1}: (3, {})} | custom-call | flops 31457280 | bytes 1048576 | tf_op jit(solution)/shard_map/side_b4/pallas_call | solution.py:250
  105.8 4.0 %collective-permute-done.20.refs_0_ = f32[8,64,256]{2,1,0:T(8,128)S(1)} collective-permute-done((f32[8,64,256]{2,1,0:T(8,128)S(1)}, f32[8,64,256]{2,1,0:T(8,128)S(1)}, u32[]{:S(2)}, u32[]{:S(2)}) %collective-permute-start.20) | collective-permute-done | bytes 524320 | tf_op jit(solution)/shard_map/ppermute | solution.py:277
  110.3 3.2 %collective-permute-done.19.refs_0_ = f32[8,64,256]{2,1,0:T(8,128)S(1)} collective-permute-done((f32[8,64,256]{2,1,0:T(8,128)S(1)}, f32[8,64,256]{2,1,0:T(8,128)S(1)}, u32[]{:S(2)}, u32[]{:S(2)}) %collective-permute-start.19) | collective-permute-done | bytes 524320 | tf_op jit(solution)/shard_map/ppermute | solution.py:277
  113.5 2.0 %side_b5.1 = (f32[32,64,256]{2,1,0:T(8,128)S(1)}, f32[24,64,256]{2,1,0:T(8,128)S(1)}) custom-call(s32[7]{0:T(128)S(1)} %stack.31.scal_ref, f32[8,64,256]{2,1,0:T(8,128)S(1)} %collective-permute-done.19.refs_0_, f32[32,64,256]{2,1,0:T(8,128)S(1)} %get-tuple-element.124.refs_1_, ...), custom_call_target="tpu_custom_call", output_to_operand_aliasing={{0}: (2, {}), {1}: (3, {})} | custom-call | flops 31457280 | bytes 1048576 | tf_op jit(solution)/shard_map/side_b5/pallas_call | solution.py:250
  120.6 4.1 %collective-permute-done.22 = f32[8,16,256]{2,1,0:T(8,128)S(1)} collective-permute-done((f32[8,16,256]{2,1,0:T(8,128)S(1)}, f32[8,16,256]{2,1,0:T(8,128)S(1)}, u32[]{:S(2)}, u32[]{:S(2)}) %collective-permute-start.22) | collective-permute-done | bytes 131104 | tf_op jit(solution)/shard_map/ppermute | solution.py:277
  (70 shorter events, 43.9 us)
Async XLA Ops:
  2.5 40.6 %copy-start.1 = (f32[1,8,64,256]{3,2,1,0:T(8,128)S(1)}, f32[1,8,64,256]{3,2,1,0:T(8,128)}, u32[]{:S(2)}) copy-start(f32[1,8,64,256]{3,2,1,0:T(8,128)} %param.13) | copy-start | bytes 1572868
  2.5 14.7 %collective-permute-start.5 = (f32[8,64,256]{2,1,0:T(8,128)S(1)}, f32[8,64,256]{2,1,0:T(8,128)S(1)}, u32[]{:S(2)}, u32[]{:S(2)}) collective-permute-start(f32[8,64,256]{2,1,0:T(8,128)S(1)} %get-tuple-element.71), channel_id=1, source_target_pairs={{0,1},{1,0},{2,3},{3,2},{4,5},{5,4},{6,7},{7,6},{8,9},{9,8},{10,11... | collective-permute-start | bytes 1572872 | tf_op jit(solution)/shard_map/ppermute | solution.py:277
  6.4 3.7 %collective-permute-start.1 = (f32[1,16,256]{2,1,0:T(8,128)S(1)}, f32[1,16,256]{2,1,0:T(8,128)S(1)}, u32[]{:S(2)}, u32[]{:S(2)}) collective-permute-start(f32[1,16,256]{2,1,0:T(8,128)S(1)} %maximum_bitcast_fusion), channel_id=1, source_target_pairs={{0,2},{1,3},{2,0},{3,1},{4,6},{5,7},{6,4},{7,5},{8,10},{9,11},{10,... | collective-permute-start | bytes 49160 | tf_op jit(solution)/shard_map/ppermute | solution.py:277
  10.1 4.8 %collective-permute-start.2 = (f32[2,16,256]{2,1,0:T(8,128)S(1)}, f32[2,16,256]{2,1,0:T(8,128)S(1)}, u32[]{:S(2)}, u32[]{:S(2)}) collective-permute-start(f32[2,16,256]{2,1,0:T(8,128)S(1)} %pad_maximum_fusion.3), channel_id=1, source_target_pairs={{0,4},{1,5},{2,6},{3,7},{4,0},{5,1},{6,2},{7,3},{8,12},{9,13},{10,... | collective-permute-start | bytes 98312 | tf_op jit(solution)/shard_map/ppermute | solution.py:277
  14.9 16.7 %collective-permute-start.6 = (f32[8,64,256]{2,1,0:T(8,128)S(1)}, f32[8,64,256]{2,1,0:T(8,128)S(1)}, u32[]{:S(2)}, u32[]{:S(2)}) collective-permute-start(f32[8,64,256]{2,1,0:T(8,128)S(1)} %get-tuple-element.71), channel_id=1, source_target_pairs={{2,0},{4,2},{6,4},{1,3},{3,5},{5,7},{10,8},{12,10},{14,12},{9,11},... | collective-permute-start | bytes 1572872 | tf_op jit(solution)/shard_map/ppermute | solution.py:277
  17.3 14.4 %collective-permute-start.7 = (f32[8,64,256]{2,1,0:T(8,128)S(1)}, f32[8,64,256]{2,1,0:T(8,128)S(1)}, u32[]{:S(2)}, u32[]{:S(2)}) collective-permute-start(f32[8,64,256]{2,1,0:T(8,128)S(1)} %collective-permute-done.5.lat_edge.m_oth), channel_id=1, source_target_pairs={{0,2},{2,4},{4,6},{3,1},{5,3},{7,5},{8,10},{10,12},{12,14},{11,9},... | collective-permute-start | bytes 1572872 | tf_op jit(solution)/shard_map/ppermute | solution.py:277
  20.8 13.1 %collective-permute-start = (f32[8,64,256]{2,1,0:T(8,128)}, f32[8,64,256]{2,1,0:T(8,128)S(1)}, u32[]{:S(2)}, u32[]{:S(2)}) collective-permute-start(f32[8,64,256]{2,1,0:T(8,128)} %bitcast.30), channel_id=1, source_target_pairs={{0,1},{1,0},{2,3},{3,2},{4,5},{5,4},{6,7},{7,6},{8,9},{9,8},{10,11... | collective-permute-start | bytes 1572872 | tf_op jit(solution)/shard_map/ppermute | solution.py:277
  21.4 12.6 %collective-permute-start.3 = (f32[4,16,256]{2,1,0:T(8,128)S(1)}, f32[4,16,256]{2,1,0:T(8,128)S(1)}, u32[]{:S(2)}, u32[]{:S(2)}) collective-permute-start(f32[4,16,256]{2,1,0:T(8,128)S(1)} %pad_maximum_fusion.2), channel_id=1, source_target_pairs={{0,1},{1,0},{2,3},{3,2},{4,5},{5,4},{6,7},{7,6},{8,9},{9,8},{10,11... | collective-permute-start | bytes 196616 | tf_op jit(solution)/shard_map/ppermute | solution.py:277
  22.9 21.2 %collective-permute-start.9 = (f32[8,64,256]{2,1,0:T(8,128)}, f32[8,64,256]{2,1,0:T(8,128)S(1)}, u32[]{:S(2)}, u32[]{:S(2)}) collective-permute-start(f32[8,64,256]{2,1,0:T(8,128)} %bitcast.31), channel_id=1, source_target_pairs={{2,0},{4,2},{6,4},{1,3},{3,5},{5,7},{10,8},{12,10},{14,12},{9,11},... | collective-permute-start | bytes 1572872 | tf_op jit(solution)/shard_map/ppermute | solution.py:277
  31.8 12.3 %collective-permute-start.8 = (f32[8,64,256]{2,1,0:T(8,128)S(1)}, f32[8,64,256]{2,1,0:T(8,128)S(1)}, u32[]{:S(2)}, u32[]{:S(2)}) collective-permute-start(f32[8,64,256]{2,1,0:T(8,128)S(1)} %pad_maximum_fusion), channel_id=1, source_target_pairs={{0,8},{1,9},{2,10},{3,11},{4,12},{5,13},{6,14},{7,15},{8,0},{9,1},... | collective-permute-start | bytes 1572872 | tf_op jit(solution)/shard_map/ppermute | solution.py:277
  34.0 14.1 %collective-permute-start.4 = (f32[8,64,256]{2,1,0:T(8,128)S(1)}, f32[8,64,256]{2,1,0:T(8,128)S(1)}, u32[]{:S(2)}, u32[]{:S(2)}) collective-permute-start(f32[8,64,256]{2,1,0:T(8,128)S(1)} %collective-permute-done.cur_oth), channel_id=1, source_target_pairs={{0,2},{2,4},{4,6},{3,1},{5,3},{7,5},{8,10},{10,12},{12,14},{11,9},... | collective-permute-start | bytes 1572872 | tf_op jit(solution)/shard_map/ppermute | solution.py:277
  36.1 7.0 %collective-permute-start.10 = (f32[4,64,256]{2,1,0:T(8,128)S(1)}, f32[4,64,256]{2,1,0:T(8,128)S(1)}, u32[]{:S(2)}, u32[]{:S(2)}) collective-permute-start(f32[4,64,256]{2,1,0:T(8,128)S(1)} %get-tuple-element.74), channel_id=1, source_target_pairs={{0,1},{1,0},{2,3},{3,2},{4,5},{5,4},{6,7},{7,6},{8,9},{9,8},{10,11... | collective-permute-start | bytes 786440 | tf_op jit(solution)/shard_map/ppermute | solution.py:277
  50.1 11.4 %collective-permute-start.12 = (f32[8,64,256]{2,1,0:T(8,128)S(1)}, f32[8,64,256]{2,1,0:T(8,128)S(1)}, u32[]{:S(2)}, u32[]{:S(2)}) collective-permute-start(f32[8,64,256]{2,1,0:T(8,128)S(1)} %get-tuple-element.87), channel_id=1, source_target_pairs={{0,2},{1,3},{2,0},{3,1},{4,6},{5,7},{6,4},{7,5},{8,10},{9,11},{10,... | collective-permute-start | bytes 1572872 | tf_op jit(solution)/shard_map/ppermute | solution.py:277
  53.0 11.9 %collective-permute-start.11 = (f32[8,64,256]{2,1,0:T(8,128)S(1)}, f32[8,64,256]{2,1,0:T(8,128)S(1)}, u32[]{:S(2)}, u32[]{:S(2)}) collective-permute-start(f32[8,64,256]{2,1,0:T(8,128)S(1)} %get-tuple-element.86), channel_id=1, source_target_pairs={{0,1},{1,0},{2,4},{3,5},{4,2},{5,3},{6,7},{7,6},{8,9},{9,8},{10,12... | collective-permute-start | bytes 1572872 | tf_op jit(solution)/shard_map/ppermute | solution.py:277
  63.4 10.6 %collective-permute-start.14 = (f32[8,64,256]{2,1,0:T(8,128)S(1)}, f32[8,64,256]{2,1,0:T(8,128)S(1)}, u32[]{:S(2)}, u32[]{:S(2)}) collective-permute-start(f32[8,64,256]{2,1,0:T(8,128)S(1)} %get-tuple-element.95), channel_id=1, source_target_pairs={{0,2},{1,3},{2,0},{3,1},{4,6},{5,7},{6,4},{7,5},{8,10},{9,11},{10,... | collective-permute-start | bytes 1572872 | tf_op jit(solution)/shard_map/ppermute | solution.py:277
  66.8 11.0 %collective-permute-start.13 = (f32[8,64,256]{2,1,0:T(8,128)S(1)}, f32[8,64,256]{2,1,0:T(8,128)S(1)}, u32[]{:S(2)}, u32[]{:S(2)}) collective-permute-start(f32[8,64,256]{2,1,0:T(8,128)S(1)} %get-tuple-element.94), channel_id=1, source_target_pairs={{0,1},{1,0},{2,4},{3,5},{4,2},{5,3},{6,7},{7,6},{8,9},{9,8},{10,12... | collective-permute-start | bytes 1572872 | tf_op jit(solution)/shard_map/ppermute | solution.py:277
  75.9 10.1 %collective-permute-start.16 = (f32[8,64,256]{2,1,0:T(8,128)S(1)}, f32[8,64,256]{2,1,0:T(8,128)S(1)}, u32[]{:S(2)}, u32[]{:S(2)}) collective-permute-start(f32[8,64,256]{2,1,0:T(8,128)S(1)} %get-tuple-element.103), channel_id=1, source_target_pairs={{0,2},{1,3},{2,0},{3,1},{4,6},{5,7},{6,4},{7,5},{8,10},{9,11},{10,... | collective-permute-start | bytes 1572872 | tf_op jit(solution)/shard_map/ppermute | solution.py:277
  79.7 10.2 %collective-permute-start.15 = (f32[8,64,256]{2,1,0:T(8,128)S(1)}, f32[8,64,256]{2,1,0:T(8,128)S(1)}, u32[]{:S(2)}, u32[]{:S(2)}) collective-permute-start(f32[8,64,256]{2,1,0:T(8,128)S(1)} %get-tuple-element.102), channel_id=1, source_target_pairs={{0,1},{1,0},{2,4},{3,5},{4,2},{5,3},{6,7},{7,6},{8,9},{9,8},{10,12... | collective-permute-start | bytes 1572872 | tf_op jit(solution)/shard_map/ppermute | solution.py:277
  88.1 10.5 %collective-permute-start.18 = (f32[8,64,256]{2,1,0:T(8,128)S(1)}, f32[8,64,256]{2,1,0:T(8,128)S(1)}, u32[]{:S(2)}, u32[]{:S(2)}) collective-permute-start(f32[8,64,256]{2,1,0:T(8,128)S(1)} %get-tuple-element.111), channel_id=1, source_target_pairs={{0,2},{1,3},{2,0},{3,1},{4,6},{5,7},{6,4},{7,5},{8,10},{9,11},{10,... | collective-permute-start | bytes 1572872 | tf_op jit(solution)/shard_map/ppermute | solution.py:277
  91.9 10.4 %collective-permute-start.17 = (f32[8,64,256]{2,1,0:T(8,128)S(1)}, f32[8,64,256]{2,1,0:T(8,128)S(1)}, u32[]{:S(2)}, u32[]{:S(2)}) collective-permute-start(f32[8,64,256]{2,1,0:T(8,128)S(1)} %get-tuple-element.110), channel_id=1, source_target_pairs={{0,1},{1,0},{2,4},{3,5},{4,2},{5,3},{6,7},{7,6},{8,9},{9,8},{10,12... | collective-permute-start | bytes 1572872 | tf_op jit(solution)/shard_map/ppermute | solution.py:277
  100.5 9.2 %collective-permute-start.20 = (f32[8,64,256]{2,1,0:T(8,128)S(1)}, f32[8,64,256]{2,1,0:T(8,128)S(1)}, u32[]{:S(2)}, u32[]{:S(2)}) collective-permute-start(f32[8,64,256]{2,1,0:T(8,128)S(1)} %get-tuple-element.119), channel_id=1, source_target_pairs={{0,2},{1,3},{2,0},{3,1},{4,6},{5,7},{6,4},{7,5},{8,10},{9,11},{10,... | collective-permute-start | bytes 1572872 | tf_op jit(solution)/shard_map/ppermute | solution.py:277
  104.3 9.2 %collective-permute-start.19 = (f32[8,64,256]{2,1,0:T(8,128)S(1)}, f32[8,64,256]{2,1,0:T(8,128)S(1)}, u32[]{:S(2)}, u32[]{:S(2)}) collective-permute-start(f32[8,64,256]{2,1,0:T(8,128)S(1)} %get-tuple-element.118), channel_id=1, source_target_pairs={{0,1},{1,0},{2,4},{3,5},{4,2},{5,3},{6,7},{7,6},{8,9},{9,8},{10,12... | collective-permute-start | bytes 1572872 | tf_op jit(solution)/shard_map/ppermute | solution.py:277
  116.9 1.5 %collective-permute-start.21 = (f32[8,32,256]{2,1,0:T(8,128)S(1)}, f32[8,32,256]{2,1,0:T(8,128)S(1)}, u32[]{:S(2)}, u32[]{:S(2)}) collective-permute-start(f32[8,32,256]{2,1,0:T(8,128)S(1)} %get-tuple-element.131), channel_id=1, source_target_pairs={{0,8},{1,9},{2,10},{3,11},{4,12},{5,13},{6,14},{7,15},{8,0},{9,1},... | collective-permute-start | bytes 786440 | tf_op jit(solution)/shard_map/ppermute | solution.py:277
  119.0 5.6 %collective-permute-start.22 = (f32[8,16,256]{2,1,0:T(8,128)S(1)}, f32[8,16,256]{2,1,0:T(8,128)S(1)}, u32[]{:S(2)}, u32[]{:S(2)}) collective-permute-start(f32[8,16,256]{2,1,0:T(8,128)S(1)} %get-tuple-element.133), channel_id=1, source_target_pairs={{0,16},{1,17},{2,18},{3,19},{4,20},{5,21},{6,22},{7,23},{8,24},{9,... | collective-permute-start | bytes 393224 | tf_op jit(solution)/shard_map/ppermute | solution.py:277
  (3 other events, 54.8 us)

commit v5 on v4

--- a/solution.py
+++ b/solution.py
@@ -101,15 +101,12 @@
 
 
 def pack_kernel(scal_ref, later_ref, c_ref, edge_ref, rest_ref, sems):
-    half = rest_ref.shape[0]
-    two = half // 2
-    y, core = scal_ref[2], scal_ref[3]
-    copies = [
-        (later_ref.at[pl.ds(half * y, half)], edge_ref.at[0:half]),
-        (c_ref.at[pl.ds(half * y + two * core, two)], edge_ref.at[half : half + two]),
-        (c_ref.at[pl.ds(half * (1 - y) + two * core, two)], edge_ref.at[half + two : 2 * half]),
-        (later_ref.at[pl.ds(half * (1 - y), half)], rest_ref),
-    ]
+    half = edge_ref.shape[0] // 2
+    y = scal_ref[2]
+    copies = []
+    for out, at in ((edge_ref, half * y), (rest_ref, half * (1 - y))):
+        for i, src in enumerate((later_ref, c_ref)):
+            copies.append((src.at[pl.ds(at, half)], out.at[i * half : (i + 1) * half]))
     copies = [pltpu.make_async_copy(src, dst, sems.at[i]) for i, (src, dst) in enumerate(copies)]
     for copy in copies:
         copy.start()
@@ -117,56 +114,54 @@
         copy.wait()
 
 
-def field_kernel(scal_ref, cur_own, cur_oth, lat_own, lat_edge, lat_rest, e_ref, o_ref, wz_ref, wy_ref):
-    length, ny, nz = cur_own.shape
+def cur_kernel(scal_ref, own, other, e_ref, send_a, send_b):
+    length = own.shape[0]
+    y = scal_ref[2]
+    for p in range(length):
+        e_ref[local_of(scal_ref, y * length + p, length) + 8] = own[p]
+        e_ref[local_of(scal_ref, (1 - y) * length + p, length) + 8] = other[p]
+    send_a[...] = e_ref[16:24]
+    send_b[...] = e_ref[8:16]
+
+
+def edge_kernel(scal_ref, own, other, send_a, send_b):
+    half = own.shape[0] // 2
+    odd = scal_ref[1]
+
+    def put(dst, src):
+        for p in range(half):
+            at = jnp.where(odd == 1, half - 1 - p, p)
+            dst[at] = src[p]
+            dst[half + at] = src[half + p]
+
+    def split(a, b):
+        put(send_a, a)
+        put(send_b, b)
+
+    own_a = (odd + scal_ref[2]) % 2
+    pl.when(own_a == 1)(lambda: split(own, other))
+    pl.when(own_a == 0)(lambda: split(other, own))
+
+
+def model_kernel(scal_ref, c_own, lat_own, edge, rest, o_ref, a_ref, c_ref, wz_ref, wy_ref):
+    length, ny, nz = c_own.shape
     half = length // 2
     y = scal_ref[2]
+
+    def put(g, later, cv):
+        j = local_of(scal_ref, g, length) + 4
+        o_ref[j] = later
+        c_ref[j] = cv * (1.0 / SCALE)
+        a_ref[j] = 2.0 + CENTRE * cv
+
     for p in range(length):
-        j = local_of(scal_ref, y * length + p, length)
-        e_ref[j + 8] = cur_own[p]
-        o_ref[j + 4] = lat_own[p]
-        j = local_of(scal_ref, (1 - y) * length + p, length)
-        e_ref[j + 8] = cur_oth[p]
+        put(y * length + p, lat_own[p], c_own[p])
+    base = (1 - y) * length
     for p in range(half):
-        j = local_of(scal_ref, (1 - y) * length + half * (1 - y) + p, length)
-        o_ref[j + 4] = lat_edge[p]
-        j = local_of(scal_ref, (1 - y) * length + half * y + p, length)
-        o_ref[j + 4] = lat_rest[p]
+        put(base + half * (1 - y) + p, edge[p], edge[half + p])
+        put(base + half * y + p, rest[p], rest[half + p])
     wz_ref[...] = band(2 * nz, nz, nz)
     wy_ref[...] = band(4 * ny, 8 * ny, ny)
-
-
-def halo_at(scal_ref, upper, p, depth, length):
-    g = jnp.where(upper == 1, 2 * length + p, p - depth)
-    return local_of(scal_ref, g, length)
-
-
-def model_kernel(scal_ref, c_own, m_oth, c_core, d_cur, d_edge, r_edge, e_in, o_in, a_ref, c_ref, e_ref, o_ref):
-    length = c_own.shape[0]
-    half, two = length // 2, length // 4
-    y, core = scal_ref[2], scal_ref[3]
-    near, far = scal_ref[6 - y], scal_ref[5 + y]
-
-    def put(j, cv):
-        c_ref[j + 4] = cv * (1.0 / SCALE)
-        a_ref[j + 4] = 2.0 + CENTRE * cv
-
-    for p in range(length):
-        put(local_of(scal_ref, y * length + p, length), c_own[p])
-    base = (1 - y) * length
-    for p in range(two):
-        for who, piece, at in ((core, m_oth, half), (1 - core, c_core, 0)):
-            put(local_of(scal_ref, base + half * (1 - y) + two * who + p, length), piece[at + p])
-            put(local_of(scal_ref, base + half * y + two * who + p, length), piece[at + two + p])
-        put(halo_at(scal_ref, 1 - y, two * core + p, half, length), keep_if(near, d_edge[half + p]))
-        put(halo_at(scal_ref, 1 - y, two * (1 - core) + p, half, length), keep_if(near, c_core[half + p]))
-        put(halo_at(scal_ref, y, two * core + p, half, length), keep_if(far, r_edge[half + p]))
-        put(halo_at(scal_ref, y, two * (1 - core) + p, half, length), keep_if(far, c_core[half + two + p]))
-    for p in range(length):
-        e_ref[halo_at(scal_ref, 1 - y, p, length, length) + 8] = keep_if(near, d_cur[p])
-    for p in range(half):
-        o_ref[halo_at(scal_ref, 1 - y, p, half, length) + 4] = keep_if(near, d_edge[p])
-        o_ref[halo_at(scal_ref, y, p, half, length) + 4] = keep_if(far, r_edge[p])
 
 
 def inner_kernel(scal_ref, e_ref, o_in, a_ref, c_ref, q_ref, wz_ref, wy_ref, f_ref, g_in, o_ref, g_ref, *, r, length):
@@ -184,30 +179,28 @@
     advance(o_ref, 4, e_ref, 8, e_ref, 8, *args, 8 if side == "a" else 0, 2, 2 * r + 1, extra=new)
 
 
-def first_kernel(scal_ref, r_cur, e_in, o_in, a_ref, c_ref, q_ref, wz_ref, wy_ref, e_ref, o_ref, new):
-    length = r_cur.shape[0]
-    y = scal_ref[2]
-    far = scal_ref[5 + y]
-    for p in range(length):
-        e_ref[halo_at(scal_ref, y, p, length, length) + 8] = keep_if(far, r_cur[p])
-    side_steps("a", 0, e_ref, o_ref, (a_ref, c_ref, q_ref, wz_ref, wy_ref), new)
-
-
-def side_kernel(scal_ref, *refs, r, side, recv, last):
-    if recv:
-        refs, recv_ref = refs[1:], refs[0]
-    e_in, o_in, a_ref, c_ref, q_ref, wz_ref, wy_ref, e_ref, o_ref = refs[:9]
-    new = None if last else refs[9]
+def side_kernel(scal_ref, recv_ref, *refs, r, side, last):
+    if r == 0:
+        edge_ref, e_in, o_in, a_in, c_in, q_ref, wz_ref, wy_ref, e_ref, o_ref, a_ref, c_ref, new = refs
+    else:
+        e_in, o_in, a_ref, c_ref, q_ref, wz_ref, wy_ref, e_ref, o_ref = refs[:9]
+        new = None if last else refs[9]
 
     def work():
-        if recv:
-            odd = scal_ref[1]
-            inside = scal_ref[6 - odd] if side == "a" else scal_ref[5 + odd]
-            for i in range(8):
-                if side == "a":
-                    e_ref[24 + i] = keep_if(inside, recv_ref[7 - i])
-                else:
-                    e_ref[7 - i] = keep_if(inside, recv_ref[i])
+        odd = scal_ref[1]
+        inside = scal_ref[6 - odd] if side == "a" else scal_ref[5 + odd]
+        for i in range(8):
+            if side == "a":
+                e_ref[24 + i] = keep_if(inside, recv_ref[7 - i])
+            else:
+                e_ref[7 - i] = keep_if(inside, recv_ref[i])
+        if r == 0:
+            for i in range(4):
+                to, at = (20 + i, 3 - i) if side == "a" else (3 - i, i)
+                o_ref[to] = keep_if(inside, edge_ref[at])
+                cv = keep_if(inside, edge_ref[4 + at])
+                c_ref[to] = cv * (1.0 / SCALE)
+                a_ref[to] = 2.0 + CENTRE * cv
         side_steps(side, r, e_ref, o_ref, (a_ref, c_ref, q_ref, wz_ref, wy_ref), new)
 
     if last:
@@ -290,12 +283,10 @@
         return out
 
     swap_y = everywhere([(i, i ^ 1) for i in range(n)])
-    hops = [(2 * lv, 2 * lv + 2) for lv in range(levels - 1)] + [(2 * lv + 1, 2 * lv - 1) for lv in range(1, levels)]
-    relay = everywhere(hops)
-    direct = [(j, i) for i, j in relay]
     swap_core = [(s * n + i, (s ^ 1) * n + i) for s in range(shots) for i in range(n)]
     swap_x = [(s * n + i, (s ^ 2) * n + i) for s in range(shots) for i in range(n)]
     swap_a, swap_b = level_swap(0), level_swap(1)
+    near_a, near_b = [[(i, j) for i, j in p if i ^ j != 1] for p in (swap_a, swap_b)]
 
     def after(x, *others):
         return lax.optimization_barrier((x, *others))[0]
@@ -307,54 +298,46 @@
     reach = 2
     while reach < n:
         gathered = jnp.concatenate([gathered, move(gathered, everywhere([(i, i ^ reach) for i in range(n)]))], 0)
+        if reach == 2:
+            early = gathered
         reach *= 2
 
-    half, two = length // 2, length // 4
+    half = length // 2
     plane = lambda k: VM((k, ny, nz), F32)
     edge, rest = pl.pallas_call(
         pack_kernel,
-        out_shape=[plane(length), plane(half)],
+        out_shape=[plane(length), plane(length)],
         in_specs=[pl.BlockSpec(memory_space=pltpu.SMEM)] + [pl.BlockSpec(memory_space=pl.ANY)] * 2,
         out_specs=[pl.BlockSpec(memory_space=VM)] * 2,
         scratch_shapes=[pltpu.SemaphoreType.DMA((4,))],
         compiler_params=pltpu.CompilerParams(vmem_limit_bytes=LIMIT),
         name="pack",
     )(scal, *[pltpu.with_memory_space_constraint(x, pltpu.HBM) for x in (later, courant_sq)])
-    y_edge = move(edge, swap_y)
-    y_cur = move(after(cur, edge), swap_y)
-    y_rest = move(after(rest, y_edge), swap_y)
-    d_edge = move(after(edge, gathered), direct)
-    d_cur = move(after(cur, gathered), direct)
-    gathered = jnp.concatenate([gathered, move(gathered, swap_y)], 0)
-    r_edge = move(y_edge, relay)
-    r_cur = move(after(y_cur, gathered), relay)
-    x_c = move(jnp.concatenate([y_edge[half:], d_edge[half : half + two], r_edge[half : half + two]], 0), swap_core)
-
-    e, o, wz, wy = call(
-        field_kernel,
-        [plane(32), plane(24), VM((2 * nz, nz), BF16), VM((4 * ny, 8 * ny), BF16)],
-        [scal, cur, y_cur, later, y_edge, y_rest],
-        free=(1, 3),
-        name="fields",
-    )
+    y_cur = move(cur, swap_y)
+    y_edge = move(after(edge, early), swap_y)
+    y_rest = move(after(rest, early), swap_y)
+
+    e, send_a, send_b = call(cur_kernel, [plane(32), plane(8), plane(8)], [scal, cur, y_cur], free=(1,), name="field")
+    recv_a, recv_b = move(send_a, near_a), move(send_b, near_b)
+    gathered = jnp.concatenate([gathered, move(after(gathered, recv_b), swap_y)], 0)
+    edge_a, edge_b = call(edge_kernel, [plane(8), plane(8)], [scal, edge, y_edge], name="edges")
+    edge_a, edge_b = move(edge_a, near_a), move(edge_b, near_b)
     q = call(
         functools.partial(q_kernel, steps=steps, length=length),
         VM((3, ny, 128), F32),
         [scal, gathered],
         name="receivers",
     )
-    a, c, e, o = call(
+    o, a, c, wz, wy = call(
         model_kernel,
-        [plane(24), plane(24), plane(32), plane(24)],
-        [scal, courant_sq, y_edge, x_c, d_cur, d_edge, r_edge, e, o],
-        {7: 2, 8: 3},
-        free=(1,),
+        [plane(24), plane(24), plane(24), VM((2 * nz, nz), BF16), VM((4 * ny, 8 * ny), BF16)],
+        [scal, courant_sq, later, y_edge, y_rest],
+        free=(1, 2),
         name="model",
     )
     g = jnp.zeros((length, ny, nz), F32)
     work = 2 * 16 * ny * nz * 60
     rounds = steps // 2
-    send_a = send_b = None
     for r in range(rounds):
         if r:
             recv_a = move(send_a, swap_a)
@@ -368,17 +351,23 @@
             name=f"inner{r}",
         )
         last = r == rounds - 1
-        outs = [plane(32), plane(24)] + ([] if last else [plane(8)])
-        model = [a, c, q, wz, wy]
-        if r == 0:
-            e, o, send_a = call(first_kernel, outs, [scal, r_cur, e, o] + model, {2: 0, 3: 1}, flops=work, name="first")
-            kern = functools.partial(side_kernel, r=r, side="b", recv=False, last=False)
-            e, o, send_b = call(kern, outs, [scal, e, o] + model, {1: 0, 2: 1}, flops=work, name="side_b0")
-            continue
         sent = []
-        for side, recv in (("a", recv_a), ("b", recv_b)):
-            kern = functools.partial(side_kernel, r=r, side=side, recv=True, last=last)
-            e, o, *new = call(kern, outs, [scal, recv, e, o] + model, {2: 0, 3: 1}, flops=work, name=f"side_{side}{r}")
+        for side in "ab":
+            got = [recv_a if side == "a" else recv_b]
+            if r == 0:
+                got.append(edge_a if side == "a" else edge_b)
+            kept = 4 if r == 0 else 2
+            at = 1 + len(got)
+            e, o, *new = call(
+                functools.partial(side_kernel, r=r, side=side, last=last),
+                [plane(32), plane(24), plane(24), plane(24)][:kept] + ([] if last else [plane(8)]),
+                [scal, *got, e, o, a, c, q, wz, wy],
+                {at + i: i for i in range(kept)},
+                flops=work,
+                name=f"side_{side}{r}",
+            )
+            if r == 0:
+                a, c, *new = new
             sent += new
         if not last:
             send_a, send_b = sent

time: 127 us -> 123 us (0.969)
  waiting for transfers between devices: 55.2 us -> 50 us
  starting transfers between devices: 26.4 us -> 28.7 us
    ppermute x23 -> x22, waiting for transfers between devices: 55.2 us -> 50 us  [move(): return lax.ppermute(x, ('shot', 'space'), pairs)]
    ppermute x23 -> x22, starting transfers between devices: 26.4 us -> 28.7 us  [move(): return lax.ppermute(x, ('shot', 'space'), pairs)]
    pallas_call x23 -> x24, Pallas kernels: 36.9 us -> 37.5 us  [call(): pl.pallas_call(kernel, out_shape=out_shapes, in_specs=specs, out_specs=ja...]
  transfers between devices with their start and end apart: 23 -> 22, of which waited for: 14 -> 14; matrix products, arithmetic and copies ran while one was open for 1% -> 1% of each run, Pallas kernels for 25% -> 29%
where the time goes in v5:
time: 123 us; the launch traced here: 122 us
  waiting for transfers between devices  50 us (41%)
  Pallas kernels  39.2 us (32%)
  starting transfers between devices  28.7 us (23%)
  other arithmetic  2.19 us (2%)
  between operations  1.59 us (1%)
    ppermute x22, waiting for transfers between devices, move(): return lax.ppermute(x, ('shot', 'space'), pairs)  50 us
    pallas_call x24, Pallas kernels, call(): pl.pallas_call(kernel, out_shape=out_shapes, in_specs=specs, out_specs=ja...  37.5 us
    ppermute x22, starting transfers between devices, move(): return lax.ppermute(x, ('shot', 'space'), pairs)  28.7 us
  transfers between devices with their start and end apart: 22, of which 14 were waited for; matrix products, arithmetic and copies ran while one was open for 1% of the time, Pallas kernels for 29%

profile of v5, /device:TPU:16, one launch (start us, length us, event | category | flops | bytes accessed | tf_op | source)
XLA Modules:
  0.0 121.9 jit_solution(16783110198764602954)
XLA Ops:
  8.7 7.0 %collective-permute-done.other = f32[8,64,256]{2,1,0:T(8,128)S(1)} collective-permute-done((f32[8,64,256]{2,1,0:T(8,128)}, f32[8,64,256]{2,1,0:T(8,128)S(1)}, u32[]{:S(2)}, u32[]{:S(2)}) %collective-permute-start) | collective-permute-done | bytes 524320 | tf_op jit(solution)/shard_map/ppermute | solution.py:270
  16.4 2.4 %collective-permute-start.1 = (f32[8,64,256]{2,1,0:T(8,128)S(1)}, f32[8,64,256]{2,1,0:T(8,128)S(1)}, u32[]{:S(2)}, u32[]{:S(2)}) collective-permute-start(f32[8,64,256]{2,1,0:T(8,128)S(1)} %get-tuple-element.72), channel_id=1, source_target_pairs={{2,4},{3,5},{4,2},{5,3},{10,12},{11,13},{12,10},{13,11},{18,20},{1... | collective-permute-start | bytes 1572872 | tf_op jit(solution)/shard_map/ppermute | solution.py:270
  20.4 3.0 %collective-permute-start.5 = (f32[8,64,256]{2,1,0:T(8,128)S(1)}, f32[8,64,256]{2,1,0:T(8,128)S(1)}, u32[]{:S(2)}, u32[]{:S(2)}) collective-permute-start(f32[8,64,256]{2,1,0:T(8,128)S(1)} %get-tuple-element.76), channel_id=1, source_target_pairs={{0,2},{1,3},{2,0},{3,1},{4,6},{5,7},{6,4},{7,5},{8,10},{9,11},{10,... | collective-permute-start | bytes 1572872 | tf_op jit(solution)/shard_map/ppermute | solution.py:270
  23.4 3.5 %collective-permute-done.3.other.edge = f32[8,64,256]{2,1,0:T(8,128)S(1)} collective-permute-done((f32[8,64,256]{2,1,0:T(8,128)S(1)}, f32[8,64,256]{2,1,0:T(8,128)S(1)}, u32[]{:S(2)}, u32[]{:S(2)}) %collective-permute-start.3) | collective-permute-done | bytes 524320 | tf_op jit(solution)/shard_map/ppermute | solution.py:270
  29.3 3.5 %collective-permute-start.4 = (f32[8,64,256]{2,1,0:T(8,128)S(1)}, f32[8,64,256]{2,1,0:T(8,128)S(1)}, u32[]{:S(2)}, u32[]{:S(2)}) collective-permute-start(f32[8,64,256]{2,1,0:T(8,128)S(1)} %get-tuple-element.75), channel_id=1, source_target_pairs={{2,4},{3,5},{4,2},{5,3},{10,12},{11,13},{12,10},{13,11},{18,20},{1... | collective-permute-start | bytes 1572872 | tf_op jit(solution)/shard_map/ppermute | solution.py:270
  34.4 3.3 %collective-permute-done.7.rest = f32[8,64,256]{2,1,0:T(8,128)S(1)} collective-permute-done((f32[8,64,256]{2,1,0:T(8,128)S(1)}, f32[8,64,256]{2,1,0:T(8,128)S(1)}, u32[]{:S(2)}, u32[]{:S(2)}) %collective-permute-start.7) | collective-permute-done | bytes 524320 | tf_op jit(solution)/shard_map/ppermute | solution.py:270
  38.9 2.9 %receivers.1.q_ref.refs_5_.refs_4_ = f32[3,64,128]{2,1,0:T(8,128)S(1)} custom-call(s32[7]{0:T(128)S(1)} %stack.31.scal_ref, f32[8,16,256]{2,1,0:T(8,128)S(1)} %pad_maximum_fusion.gathered_ref), custom_call_target="tpu_custom_call" | custom-call | bytes 1048576 | tf_op jit(solution)/shard_map/receivers/pallas_call | solution.py:243
  44.4 1.9 %side_a0.1 = (f32[32,64,256]{2,1,0:T(8,128)S(1)}, f32[24,64,256]{2,1,0:T(8,128)S(1)}, f32[24,64,256]{2,1,0:T(8,128)S(1)}, f32[24,64,256]{2,1,0:T(8,128)S(1)}, f32[8,64,256]{2,1,0:T(8,128)S(1)}) custom-call(s32[7]{0:T(128)S(1)} %stack.31.scal_ref, ...), custom_call_target="tpu_custom_call", output_to_operand_aliasing={{0}: (3, {}), {1}: (4, {}), {2}: (5, {}), {3}: (6, {})} | custom-call | flops 31457280 | bytes 1048576 | tf_op jit(solution)/shard_map/side_a0/pallas_call | solution.py:243
  48.1 1.9 %side_b0.1 = (f32[32,64,256]{2,1,0:T(8,128)S(1)}, f32[24,64,256]{2,1,0:T(8,128)S(1)}, f32[24,64,256]{2,1,0:T(8,128)S(1)}, f32[24,64,256]{2,1,0:T(8,128)S(1)}, f32[8,64,256]{2,1,0:T(8,128)S(1)}) custom-call(s32[7]{0:T(128)S(1)} %stack.31.scal_ref, ...), custom_call_target="tpu_custom_call", output_to_operand_aliasing={{0}: (3, {}), {1}: (4, {}), {2}: (5, {}), {3}: (6, {})} | custom-call | flops 31457280 | bytes 1048576 | tf_op jit(solution)/shard_map/side_b0/pallas_call | solution.py:243
  52.0 5.5 %collective-permute-done.11.recv_ref = f32[8,64,256]{2,1,0:T(8,128)S(1)} collective-permute-done((f32[8,64,256]{2,1,0:T(8,128)S(1)}, f32[8,64,256]{2,1,0:T(8,128)S(1)}, u32[]{:S(2)}, u32[]{:S(2)}) %collective-permute-start.11) | collective-permute-done | bytes 524320 | tf_op jit(solution)/shard_map/ppermute | solution.py:270
  57.5 1.9 %side_a1.1 = (f32[32,64,256]{2,1,0:T(8,128)S(1)}, f32[24,64,256]{2,1,0:T(8,128)S(1)}, f32[8,64,256]{2,1,0:T(8,128)S(1)}) custom-call(s32[7]{0:T(128)S(1)} %stack.31.scal_ref, f32[8,64,256]{2,1,0:T(8,128)S(1)} %collective-permute-done.11.recv_ref, f32[32,64,256]{2,1,0:T(8,128)S(1)} %get-tuple-element.94.e_ref.refs_0_, ...), custom_call_target="tpu_custom_call", output_to_operand_aliasing={{0}: (2, {}), {1}: (3, {})} | custom-call | flops 31457280 | bytes 1048576 | tf_op jit(solution)/shard_map/side_a1/pallas_call | solution.py:243
  61.1 1.9 %side_b1.1 = (f32[32,64,256]{2,1,0:T(8,128)S(1)}, f32[24,64,256]{2,1,0:T(8,128)S(1)}, f32[8,64,256]{2,1,0:T(8,128)S(1)}) custom-call(s32[7]{0:T(128)S(1)} %stack.31.scal_ref, f32[8,64,256]{2,1,0:T(8,128)S(1)} %collective-permute-done.10.recv_ref, f32[32,64,256]{2,1,0:T(8,128)S(1)} %get-tuple-element.100.refs_0_, ...), custom_call_target="tpu_custom_call", output_to_operand_aliasing={{0}: (2, {}), {1}: (3, {})} | custom-call | flops 31457280 | bytes 1048576 | tf_op jit(solution)/shard_map/side_b1/pallas_call | solution.py:243
  64.5 5.2 %collective-permute-done.13.recv_ref = f32[8,64,256]{2,1,0:T(8,128)S(1)} collective-permute-done((f32[8,64,256]{2,1,0:T(8,128)S(1)}, f32[8,64,256]{2,1,0:T(8,128)S(1)}, u32[]{:S(2)}, u32[]{:S(2)}) %collective-permute-start.13) | collective-permute-done | bytes 524320 | tf_op jit(solution)/shard_map/ppermute | solution.py:270
  73.2 2.0 %side_b2.1 = (f32[32,64,256]{2,1,0:T(8,128)S(1)}, f32[24,64,256]{2,1,0:T(8,128)S(1)}, f32[8,64,256]{2,1,0:T(8,128)S(1)}) custom-call(s32[7]{0:T(128)S(1)} %stack.31.scal_ref, f32[8,64,256]{2,1,0:T(8,128)S(1)} %collective-permute-done.12.recv_ref, f32[32,64,256]{2,1,0:T(8,128)S(1)} %get-tuple-element.108.refs_0_, ...), custom_call_target="tpu_custom_call", output_to_operand_aliasing={{0}: (2, {}), {1}: (3, {})} | custom-call | flops 31457280 | bytes 1048576 | tf_op jit(solution)/shard_map/side_b2/pallas_call | solution.py:243
  76.6 5.0 %collective-permute-done.15.recv_ref = f32[8,64,256]{2,1,0:T(8,128)S(1)} collective-permute-done((f32[8,64,256]{2,1,0:T(8,128)S(1)}, f32[8,64,256]{2,1,0:T(8,128)S(1)}, u32[]{:S(2)}, u32[]{:S(2)}) %collective-permute-start.15) | collective-permute-done | bytes 524320 | tf_op jit(solution)/shard_map/ppermute | solution.py:270
  81.6 2.1 %side_a3.1 = (f32[32,64,256]{2,1,0:T(8,128)S(1)}, f32[24,64,256]{2,1,0:T(8,128)S(1)}, f32[8,64,256]{2,1,0:T(8,128)S(1)}) custom-call(s32[7]{0:T(128)S(1)} %stack.31.scal_ref, f32[8,64,256]{2,1,0:T(8,128)S(1)} %collective-permute-done.15.recv_ref, f32[32,64,256]{2,1,0:T(8,128)S(1)} %get-tuple-element.112.e_ref.refs_0_, ...), custom_call_target="tpu_custom_call", output_to_operand_aliasing={{0}: (2, {}), {1}: (3, {})} | custom-call | flops 31457280 | bytes 1048576 | tf_op jit(solution)/shard_map/side_a3/pallas_call | solution.py:243
  85.5 2.0 %side_b3.1 = (f32[32,64,256]{2,1,0:T(8,128)S(1)}, f32[24,64,256]{2,1,0:T(8,128)S(1)}, f32[8,64,256]{2,1,0:T(8,128)S(1)}) custom-call(s32[7]{0:T(128)S(1)} %stack.31.scal_ref, f32[8,64,256]{2,1,0:T(8,128)S(1)} %collective-permute-done.14.recv_ref, f32[32,64,256]{2,1,0:T(8,128)S(1)} %get-tuple-element.116.refs_0_, ...), custom_call_target="tpu_custom_call", output_to_operand_aliasing={{0}: (2, {}), {1}: (3, {})} | custom-call | flops 31457280 | bytes 1048576 | tf_op jit(solution)/shard_map/side_b3/pallas_call | solution.py:243
  88.9 6.0 %collective-permute-done.17.recv_ref = f32[8,64,256]{2,1,0:T(8,128)S(1)} collective-permute-done((f32[8,64,256]{2,1,0:T(8,128)S(1)}, f32[8,64,256]{2,1,0:T(8,128)S(1)}, u32[]{:S(2)}, u32[]{:S(2)}) %collective-permute-start.17) | collective-permute-done | bytes 524320 | tf_op jit(solution)/shard_map/ppermute | solution.py:270
  96.8 2.1 %collective-permute-start.19 = (f32[8,64,256]{2,1,0:T(8,128)S(1)}, f32[8,64,256]{2,1,0:T(8,128)S(1)}, u32[]{:S(2)}, u32[]{:S(2)}) collective-permute-start(f32[8,64,256]{2,1,0:T(8,128)S(1)} %get-tuple-element.127), channel_id=1, source_target_pairs={{0,2},{1,3},{2,0},{3,1},{4,6},{5,7},{6,4},{7,5},{8,10},{9,11},{10,... | collective-permute-start | bytes 1572872 | tf_op jit(solution)/shard_map/ppermute | solution.py:270
  98.9 2.0 %side_b4.1 = (f32[32,64,256]{2,1,0:T(8,128)S(1)}, f32[24,64,256]{2,1,0:T(8,128)S(1)}, f32[8,64,256]{2,1,0:T(8,128)S(1)}) custom-call(s32[7]{0:T(128)S(1)} %stack.31.scal_ref, f32[8,64,256]{2,1,0:T(8,128)S(1)} %collective-permute-done.16.recv_ref, f32[32,64,256]{2,1,0:T(8,128)S(1)} %get-tuple-element.124.refs_0_, ...), custom_call_target="tpu_custom_call", output_to_operand_aliasing={{0}: (2, {}), {1}: (3, {})} | custom-call | flops 31457280 | bytes 1048576 | tf_op jit(solution)/shard_map/side_b4/pallas_call | solution.py:243
  102.3 3.7 %collective-permute-done.19.recv_ref = f32[8,64,256]{2,1,0:T(8,128)S(1)} collective-permute-done((f32[8,64,256]{2,1,0:T(8,128)S(1)}, f32[8,64,256]{2,1,0:T(8,128)S(1)}, u32[]{:S(2)}, u32[]{:S(2)}) %collective-permute-start.19) | collective-permute-done | bytes 524320 | tf_op jit(solution)/shard_map/ppermute | solution.py:270
  106.6 3.5 %collective-permute-done.18.recv_ref = f32[8,64,256]{2,1,0:T(8,128)S(1)} collective-permute-done((f32[8,64,256]{2,1,0:T(8,128)S(1)}, f32[8,64,256]{2,1,0:T(8,128)S(1)}, u32[]{:S(2)}, u32[]{:S(2)}) %collective-permute-start.18) | collective-permute-done | bytes 524320 | tf_op jit(solution)/shard_map/ppermute | solution.py:270
  110.1 2.0 %side_b5.1 = (f32[32,64,256]{2,1,0:T(8,128)S(1)}, f32[24,64,256]{2,1,0:T(8,128)S(1)}) custom-call(s32[7]{0:T(128)S(1)} %stack.31.scal_ref, f32[8,64,256]{2,1,0:T(8,128)S(1)} %collective-permute-done.18.recv_ref, f32[32,64,256]{2,1,0:T(8,128)S(1)} %get-tuple-element.132.refs_0_, ...), custom_call_target="tpu_custom_call", output_to_operand_aliasing={{0}: (2, {}), {1}: (3, {})} | custom-call | flops 31457280 | bytes 1048576 | tf_op jit(solution)/shard_map/side_b5/pallas_call | solution.py:243
  117.1 4.0 %collective-permute-done.21 = f32[8,16,256]{2,1,0:T(8,128)S(1)} collective-permute-done((f32[8,16,256]{2,1,0:T(8,128)S(1)}, f32[8,16,256]{2,1,0:T(8,128)S(1)}, u32[]{:S(2)}, u32[]{:S(2)}) %collective-permute-start.21) | collective-permute-done | bytes 131104 | tf_op jit(solution)/shard_map/ppermute | solution.py:270
  (65 shorter events, 42.0 us)
Async XLA Ops:
  0.6 15.1 %collective-permute-start = (f32[8,64,256]{2,1,0:T(8,128)}, f32[8,64,256]{2,1,0:T(8,128)S(1)}, u32[]{:S(2)}, u32[]{:S(2)}) collective-permute-start(f32[8,64,256]{2,1,0:T(8,128)} %bitcast.30), channel_id=1, source_target_pairs={{0,1},{1,0},{2,3},{3,2},{4,5},{5,4},{6,7},{7,6},{8,9},{9,8},{10,11... | collective-permute-start | bytes 1572872 | tf_op jit(solution)/shard_map/ppermute | solution.py:270
  4.5 3.7 %collective-permute-start.2 = (f32[1,16,256]{2,1,0:T(8,128)S(1)}, f32[1,16,256]{2,1,0:T(8,128)S(1)}, u32[]{:S(2)}, u32[]{:S(2)}) collective-permute-start(f32[1,16,256]{2,1,0:T(8,128)S(1)} %maximum_bitcast_fusion), channel_id=1, source_target_pairs={{0,2},{1,3},{2,0},{3,1},{4,6},{5,7},{6,4},{7,5},{8,10},{9,11},{10,... | collective-permute-start | bytes 49160 | tf_op jit(solution)/shard_map/ppermute | solution.py:270
  6.1 31.6 %copy-start.1 = (f32[1,8,64,256]{3,2,1,0:T(8,128)S(1)}, f32[1,8,64,256]{3,2,1,0:T(8,128)}, u32[]{:S(2)}) copy-start(f32[1,8,64,256]{3,2,1,0:T(8,128)} %param.13) | copy-start | bytes 1572868
  6.1 31.6 %copy-start.2 = (f32[8,64,256]{2,1,0:T(8,128)S(1)}, f32[8,64,256]{2,1,0:T(8,128)}, u32[]{:S(2)}) copy-start(f32[8,64,256]{2,1,0:T(8,128)} %c_own.1) | copy-start | bytes 1572868
  8.2 18.8 %collective-permute-start.3 = (f32[8,64,256]{2,1,0:T(8,128)S(1)}, f32[8,64,256]{2,1,0:T(8,128)S(1)}, u32[]{:S(2)}, u32[]{:S(2)}) collective-permute-start(f32[8,64,256]{2,1,0:T(8,128)S(1)} %get-tuple-element.74.own), channel_id=1, source_target_pairs={{0,1},{1,0},{2,3},{3,2},{4,5},{5,4},{6,7},{7,6},{8,9},{9,8},{10,11... | collective-permute-start | bytes 1572872 | tf_op jit(solution)/shard_map/ppermute | solution.py:270
  16.4 16.4 %collective-permute-start.1 = (f32[8,64,256]{2,1,0:T(8,128)S(1)}, f32[8,64,256]{2,1,0:T(8,128)S(1)}, u32[]{:S(2)}, u32[]{:S(2)}) collective-permute-start(f32[8,64,256]{2,1,0:T(8,128)S(1)} %get-tuple-element.72), channel_id=1, source_target_pairs={{2,4},{3,5},{4,2},{5,3},{10,12},{11,13},{12,10},{13,11},{18,20},{1... | collective-permute-start | bytes 1572872 | tf_op jit(solution)/shard_map/ppermute | solution.py:270
  18.8 19.0 %collective-permute-start.7 = (f32[8,64,256]{2,1,0:T(8,128)S(1)}, f32[8,64,256]{2,1,0:T(8,128)S(1)}, u32[]{:S(2)}, u32[]{:S(2)}) collective-permute-start(f32[8,64,256]{2,1,0:T(8,128)S(1)} %get-tuple-element.80), channel_id=1, source_target_pairs={{0,1},{1,0},{2,3},{3,2},{4,5},{5,4},{6,7},{7,6},{8,9},{9,8},{10,11... | collective-permute-start | bytes 1572872 | tf_op jit(solution)/shard_map/ppermute | solution.py:270
  20.4 9.0 %collective-permute-start.8 = (f32[2,16,256]{2,1,0:T(8,128)S(1)}, f32[2,16,256]{2,1,0:T(8,128)S(1)}, u32[]{:S(2)}, u32[]{:S(2)}) collective-permute-start(f32[2,16,256]{2,1,0:T(8,128)S(1)} %pad_maximum_fusion.2), channel_id=1, source_target_pairs={{0,4},{1,5},{2,6},{3,7},{4,0},{5,1},{6,2},{7,3},{8,12},{9,13},{10,... | collective-permute-start | bytes 98312 | tf_op jit(solution)/shard_map/ppermute | solution.py:270
  20.4 22.8 %collective-permute-start.5 = (f32[8,64,256]{2,1,0:T(8,128)S(1)}, f32[8,64,256]{2,1,0:T(8,128)S(1)}, u32[]{:S(2)}, u32[]{:S(2)}) collective-permute-start(f32[8,64,256]{2,1,0:T(8,128)S(1)} %get-tuple-element.76), channel_id=1, source_target_pairs={{0,2},{1,3},{2,0},{3,1},{4,6},{5,7},{6,4},{7,5},{8,10},{9,11},{10,... | collective-permute-start | bytes 1572872 | tf_op jit(solution)/shard_map/ppermute | solution.py:270
  27.6 16.8 %collective-permute-start.6 = (f32[8,64,256]{2,1,0:T(8,128)S(1)}, f32[8,64,256]{2,1,0:T(8,128)S(1)}, u32[]{:S(2)}, u32[]{:S(2)}) collective-permute-start(f32[8,64,256]{2,1,0:T(8,128)S(1)} %get-tuple-element.77), channel_id=1, source_target_pairs={{0,2},{1,3},{2,0},{3,1},{4,6},{5,7},{6,4},{7,5},{8,10},{9,11},{10,... | collective-permute-start | bytes 1572872 | tf_op jit(solution)/shard_map/ppermute | solution.py:270
  29.3 18.8 %collective-permute-start.4 = (f32[8,64,256]{2,1,0:T(8,128)S(1)}, f32[8,64,256]{2,1,0:T(8,128)S(1)}, u32[]{:S(2)}, u32[]{:S(2)}) collective-permute-start(f32[8,64,256]{2,1,0:T(8,128)S(1)} %get-tuple-element.75), channel_id=1, source_target_pairs={{2,4},{3,5},{4,2},{5,3},{10,12},{11,13},{12,10},{13,11},{18,20},{1... | collective-permute-start | bytes 1572872 | tf_op jit(solution)/shard_map/ppermute | solution.py:270
  32.9 6.0 %collective-permute-start.9 = (f32[4,16,256]{2,1,0:T(8,128)S(1)}, f32[4,16,256]{2,1,0:T(8,128)S(1)}, u32[]{:S(2)}, u32[]{:S(2)}) collective-permute-start(f32[4,16,256]{2,1,0:T(8,128)S(1)} %pad_maximum_fusion.1), channel_id=1, source_target_pairs={{0,1},{1,0},{2,3},{3,2},{4,5},{5,4},{6,7},{7,6},{8,9},{9,8},{10,11... | collective-permute-start | bytes 196616 | tf_op jit(solution)/shard_map/ppermute | solution.py:270
  46.3 11.2 %collective-permute-start.11 = (f32[8,64,256]{2,1,0:T(8,128)S(1)}, f32[8,64,256]{2,1,0:T(8,128)S(1)}, u32[]{:S(2)}, u32[]{:S(2)}) collective-permute-start(f32[8,64,256]{2,1,0:T(8,128)S(1)} %get-tuple-element.93), channel_id=1, source_target_pairs={{0,2},{1,3},{2,0},{3,1},{4,6},{5,7},{6,4},{7,5},{8,10},{9,11},{10,... | collective-permute-start | bytes 1572872 | tf_op jit(solution)/shard_map/ppermute | solution.py:270
  50.1 11.0 %collective-permute-start.10 = (f32[8,64,256]{2,1,0:T(8,128)S(1)}, f32[8,64,256]{2,1,0:T(8,128)S(1)}, u32[]{:S(2)}, u32[]{:S(2)}) collective-permute-start(f32[8,64,256]{2,1,0:T(8,128)S(1)} %get-tuple-element.92), channel_id=1, source_target_pairs={{0,1},{1,0},{2,4},{3,5},{4,2},{5,3},{6,7},{7,6},{8,9},{9,8},{10,12... | collective-permute-start | bytes 1572872 | tf_op jit(solution)/shard_map/ppermute | solution.py:270
  59.4 10.3 %collective-permute-start.13 = (f32[8,64,256]{2,1,0:T(8,128)S(1)}, f32[8,64,256]{2,1,0:T(8,128)S(1)}, u32[]{:S(2)}, u32[]{:S(2)}) collective-permute-start(f32[8,64,256]{2,1,0:T(8,128)S(1)} %get-tuple-element.103), channel_id=1, source_target_pairs={{0,2},{1,3},{2,0},{3,1},{4,6},{5,7},{6,4},{7,5},{8,10},{9,11},{10,... | collective-permute-start | bytes 1572872 | tf_op jit(solution)/shard_map/ppermute | solution.py:270
  63.0 10.1 %collective-permute-start.12 = (f32[8,64,256]{2,1,0:T(8,128)S(1)}, f32[8,64,256]{2,1,0:T(8,128)S(1)}, u32[]{:S(2)}, u32[]{:S(2)}) collective-permute-start(f32[8,64,256]{2,1,0:T(8,128)S(1)} %get-tuple-element.102), channel_id=1, source_target_pairs={{0,1},{1,0},{2,4},{3,5},{4,2},{5,3},{6,7},{7,6},{8,9},{9,8},{10,12... | collective-permute-start | bytes 1572872 | tf_op jit(solution)/shard_map/ppermute | solution.py:270
  71.6 10.0 %collective-permute-start.15 = (f32[8,64,256]{2,1,0:T(8,128)S(1)}, f32[8,64,256]{2,1,0:T(8,128)S(1)}, u32[]{:S(2)}, u32[]{:S(2)}) collective-permute-start(f32[8,64,256]{2,1,0:T(8,128)S(1)} %get-tuple-element.111), channel_id=1, source_target_pairs={{0,2},{1,3},{2,0},{3,1},{4,6},{5,7},{6,4},{7,5},{8,10},{9,11},{10,... | collective-permute-start | bytes 1572872 | tf_op jit(solution)/shard_map/ppermute | solution.py:270
  75.1 10.4 %collective-permute-start.14 = (f32[8,64,256]{2,1,0:T(8,128)S(1)}, f32[8,64,256]{2,1,0:T(8,128)S(1)}, u32[]{:S(2)}, u32[]{:S(2)}) collective-permute-start(f32[8,64,256]{2,1,0:T(8,128)S(1)} %get-tuple-element.110), channel_id=1, source_target_pairs={{0,1},{1,0},{2,4},{3,5},{4,2},{5,3},{6,7},{7,6},{8,9},{9,8},{10,12... | collective-permute-start | bytes 1572872 | tf_op jit(solution)/shard_map/ppermute | solution.py:270
  83.7 11.2 %collective-permute-start.17 = (f32[8,64,256]{2,1,0:T(8,128)S(1)}, f32[8,64,256]{2,1,0:T(8,128)S(1)}, u32[]{:S(2)}, u32[]{:S(2)}) collective-permute-start(f32[8,64,256]{2,1,0:T(8,128)S(1)} %get-tuple-element.119), channel_id=1, source_target_pairs={{0,2},{1,3},{2,0},{3,1},{4,6},{5,7},{6,4},{7,5},{8,10},{9,11},{10,... | collective-permute-start | bytes 1572872 | tf_op jit(solution)/shard_map/ppermute | solution.py:270
  87.4 11.4 %collective-permute-start.16 = (f32[8,64,256]{2,1,0:T(8,128)S(1)}, f32[8,64,256]{2,1,0:T(8,128)S(1)}, u32[]{:S(2)}, u32[]{:S(2)}) collective-permute-start(f32[8,64,256]{2,1,0:T(8,128)S(1)} %get-tuple-element.118), channel_id=1, source_target_pairs={{0,1},{1,0},{2,4},{3,5},{4,2},{5,3},{6,7},{7,6},{8,9},{9,8},{10,12... | collective-permute-start | bytes 1572872 | tf_op jit(solution)/shard_map/ppermute | solution.py:270
  96.8 9.3 %collective-permute-start.19 = (f32[8,64,256]{2,1,0:T(8,128)S(1)}, f32[8,64,256]{2,1,0:T(8,128)S(1)}, u32[]{:S(2)}, u32[]{:S(2)}) collective-permute-start(f32[8,64,256]{2,1,0:T(8,128)S(1)} %get-tuple-element.127), channel_id=1, source_target_pairs={{0,2},{1,3},{2,0},{3,1},{4,6},{5,7},{6,4},{7,5},{8,10},{9,11},{10,... | collective-permute-start | bytes 1572872 | tf_op jit(solution)/shard_map/ppermute | solution.py:270
  100.8 9.2 %collective-permute-start.18 = (f32[8,64,256]{2,1,0:T(8,128)S(1)}, f32[8,64,256]{2,1,0:T(8,128)S(1)}, u32[]{:S(2)}, u32[]{:S(2)}) collective-permute-start(f32[8,64,256]{2,1,0:T(8,128)S(1)} %get-tuple-element.126), channel_id=1, source_target_pairs={{0,1},{1,0},{2,4},{3,5},{4,2},{5,3},{6,7},{7,6},{8,9},{9,8},{10,12... | collective-permute-start | bytes 1572872 | tf_op jit(solution)/shard_map/ppermute | solution.py:270
  113.5 1.5 %collective-permute-start.20 = (f32[8,32,256]{2,1,0:T(8,128)S(1)}, f32[8,32,256]{2,1,0:T(8,128)S(1)}, u32[]{:S(2)}, u32[]{:S(2)}) collective-permute-start(f32[8,32,256]{2,1,0:T(8,128)S(1)} %get-tuple-element.139), channel_id=1, source_target_pairs={{0,8},{1,9},{2,10},{3,11},{4,12},{5,13},{6,14},{7,15},{8,0},{9,1},... | collective-permute-start | bytes 786440 | tf_op jit(solution)/shard_map/ppermute | solution.py:270
  115.6 5.6 %collective-permute-start.21 = (f32[8,16,256]{2,1,0:T(8,128)S(1)}, f32[8,16,256]{2,1,0:T(8,128)S(1)}, u32[]{:S(2)}, u32[]{:S(2)}) collective-permute-start(f32[8,16,256]{2,1,0:T(8,128)S(1)} %get-tuple-element.141), channel_id=1, source_target_pairs={{0,16},{1,17},{2,18},{3,19},{4,20},{5,21},{6,22},{7,23},{8,24},{9,... | collective-permute-start | bytes 393224 | tf_op jit(solution)/shard_map/ppermute | solution.py:270
  (2 other events, 24.2 us)

commit v6 on v5

--- a/solution.py
+++ b/solution.py
@@ -210,29 +210,37 @@
         work()
 
 
-def final_kernel(scal_ref, e_ref, o_ref, f_ref, g_in, field_ref, give_ref, keep_ref, *, steps):
-    length, ny, _ = field_ref.shape
+def share_kernel(scal_ref, e_ref, o_ref, f_ref, g_in, g_ref, *, steps, give):
+    length, rows, _ = g_ref.shape
+    part = rows // 2
     y, core = scal_ref[2], scal_ref[3]
-    part = ny // 4
+    mine = 1 - core if give else core
     for p in range(length):
         j = local_of(scal_ref, y * length + p, length)
-        last = e_ref[j + 8]
-        field_ref[p] = last
-        g = g_in[p] + o_ref[j + 4] * f_ref[steps - 2, p].astype(F32) + last * f_ref[steps - 1, p].astype(F32)
         for x in range(2):
-            zero, one = g[2 * x * part : (2 * x + 1) * part], g[(2 * x + 1) * part : (2 * x + 2) * part]
-            give_ref[p, x * part : (x + 1) * part] = jnp.where(core == 1, zero, one)
-            keep_ref[p, x * part : (x + 1) * part] = jnp.where(core == 1, one, zero)
-
-
-def pair_kernel(scal_ref, keep_ref, recv_ref, give_ref, mine_ref):
+            at = pl.ds(pl.multiple_of(part * (2 * x + mine), part), part)
+            g_ref[p, x * part : (x + 1) * part] = (
+                g_in[p, at]
+                + o_ref[j + 4, at] * f_ref[steps - 2, p, at].astype(F32)
+                + e_ref[j + 8, at] * f_ref[steps - 1, p, at].astype(F32)
+            )
+
+
+def pair_kernel(scal_ref, keep_ref, recv_ref, give_ref):
     x = scal_ref[4]
     part = give_ref.shape[1]
+    at = pl.ds(pl.multiple_of(part * (1 - x), part), part)
     for p in range(keep_ref.shape[0]):
-        low = keep_ref[p, :part] + recv_ref[p, :part]
-        high = keep_ref[p, part:] + recv_ref[p, part:]
-        give_ref[p] = jnp.where(x == 1, low, high)
-        mine_ref[p] = jnp.where(x == 1, high, low)
+        give_ref[p] = keep_ref[p, at] + recv_ref[p, at]
+
+
+def own_kernel(scal_ref, e_ref, keep_ref, recv_ref, late_ref, field_ref, mine_ref):
+    x = scal_ref[4]
+    length, part, _ = mine_ref.shape
+    at = pl.ds(pl.multiple_of(part * x, part), part)
+    for p in range(length):
+        field_ref[p] = e_ref[local_of(scal_ref, scal_ref[2] * length + p, length) + 8]
+        mine_ref[p] = keep_ref[p, at] + recv_ref[p, at]
 
 
 def call(kernel, out_shapes, args, aliases=None, free=(), flops=0, name=None):
@@ -279,14 +287,15 @@
                 up = lv % 2 == parity
                 to = lv + 1 if up else lv - 1
                 for i in range(2):
-                    out.append((s * n + 2 * lv + i, s * n + (2 * to + i if 0 <= to < levels else 2 * lv + 1 - i)))
+                    at = 2 * lv + i
+                    out.append((s * n + at, s * n + 2 * to + i if 0 <= to < levels else (s ^ 1) * n + at))
         return out
 
     swap_y = everywhere([(i, i ^ 1) for i in range(n)])
     swap_core = [(s * n + i, (s ^ 1) * n + i) for s in range(shots) for i in range(n)]
     swap_x = [(s * n + i, (s ^ 2) * n + i) for s in range(shots) for i in range(n)]
     swap_a, swap_b = level_swap(0), level_swap(1)
-    near_a, near_b = [[(i, j) for i, j in p if i ^ j != 1] for p in (swap_a, swap_b)]
+    near_a, near_b = [[(i, j) for i, j in p if i // n == j // n] for p in (swap_a, swap_b)]
 
     def after(x, *others):
         return lax.optimization_barrier((x, *others))[0]
@@ -317,7 +326,7 @@
     y_edge = move(after(edge, early), swap_y)
     y_rest = move(after(rest, early), swap_y)
 
-    e, send_a, send_b = call(cur_kernel, [plane(32), plane(8), plane(8)], [scal, cur, y_cur], free=(1,), name="field")
+    e, send_a, send_b = call(cur_kernel, [plane(32), plane(8), plane(8)], [scal, cur, after(y_cur, gathered)], free=(1,), name="field")
     recv_a, recv_b = move(send_a, near_a), move(send_b, near_b)
     gathered = jnp.concatenate([gathered, move(after(gathered, recv_b), swap_y)], 0)
     edge_a, edge_b = call(edge_kernel, [plane(8), plane(8)], [scal, edge, y_edge], name="edges")
@@ -373,19 +382,21 @@
             send_a, send_b = sent
 
     part = ny // 4
-    field, give, keep = call(
-        functools.partial(final_kernel, steps=steps),
-        [jax.ShapeDtypeStruct((length, ny, nz), F32), VM((length, 2 * part, nz), F32), VM((length, 2 * part, nz), F32)],
-        [scal, e, o, forward, g],
-        name="final",
+    shares = [scal, e, o, forward, g]
+    share = VM((length, 2 * part, nz), F32)
+    give = call(functools.partial(share_kernel, steps=steps, give=True), [share], shares, name="give")[0]
+    recv = move(give, swap_core)
+    keep = call(functools.partial(share_kernel, steps=steps, give=False), [share], shares, name="keep")[0]
+    give = call(pair_kernel, [VM((length, part, nz), F32)], [scal, keep, recv], name="pair")[0]
+    last = move(give, swap_x)
+    field, mine = call(
+        own_kernel,
+        [jax.ShapeDtypeStruct((length, ny, nz), F32), VM((length, part, nz), F32)],
+        [scal, e, keep, recv, give],
+        flops=work,
+        name="own",
     )
-    give, mine = call(
-        pair_kernel,
-        [VM((length, part, nz), F32)] * 2,
-        [scal, keep, move(give, swap_core)],
-        name="pair",
-    )
-    return field[None], mine + move(give, swap_x)
+    return field[None], mine + last
 
 
 def solution(mesh):

time: 123 us -> 122 us (level)
  starting transfers between devices: 28.7 us -> 23.2 us
  waiting for transfers between devices: 50 us -> 53.9 us
    ppermute x22, starting transfers between devices: 28.7 us -> 23.2 us  [move(): return lax.ppermute(x, ('shot', 'space'), pairs)]
    ppermute x22, waiting for transfers between devices: 50 us -> 53.9 us  [move(): return lax.ppermute(x, ('shot', 'space'), pairs)]
    pallas_call x24 -> x26, Pallas kernels: 37.5 us -> 38.6 us  [call(): pl.pallas_call(kernel, out_shape=out_shapes, in_specs=specs, out_specs=ja...]
  transfers between devices with their start and end apart: 22 -> 22, of which waited for: 14 -> 13; matrix products, arithmetic and copies ran while one was open for 1% -> 1% of each run, Pallas kernels for 29% -> 31%
where the time goes in v6:
time: 122 us; the launch traced here: 121 us
  waiting for transfers between devices  53.9 us (44%)
  Pallas kernels  40.4 us (33%)
  starting transfers between devices  23.2 us (19%)
  other arithmetic  2.18 us (2%)
  between operations  1.61 us (1%)
    ppermute x22, waiting for transfers between devices, move(): return lax.ppermute(x, ('shot', 'space'), pairs)  53.9 us
    pallas_call x26, Pallas kernels, call(): pl.pallas_call(kernel, out_shape=out_shapes, in_specs=specs, out_specs=ja...  38.6 us
    ppermute x22, starting transfers between devices, move(): return lax.ppermute(x, ('shot', 'space'), pairs)  23.2 us
  transfers between devices with their start and end apart: 22, of which 13 were waited for; matrix products, arithmetic and copies ran while one was open for 1% of the time, Pallas kernels for 31%

profile of v6, /device:TPU:16, one launch (start us, length us, event | category | flops | bytes accessed | tf_op | source)
XLA Modules:
  0.0 121.5 jit_solution(7813651368305417942)
XLA Ops:
  8.8 4.7 %collective-permute-done.2 = f32[2,16,256]{2,1,0:T(8,128)S(1)} collective-permute-done((f32[2,16,256]{2,1,0:T(8,128)S(1)}, f32[2,16,256]{2,1,0:T(8,128)S(1)}, u32[]{:S(2)}, u32[]{:S(2)}) %collective-permute-start.2) | collective-permute-done | bytes 32800 | tf_op jit(solution)/shard_map/ppermute | solution.py:278
  13.6 2.2 %collective-permute-done.other = f32[8,64,256]{2,1,0:T(8,128)S(1)} collective-permute-done((f32[8,64,256]{2,1,0:T(8,128)}, f32[8,64,256]{2,1,0:T(8,128)S(1)}, u32[]{:S(2)}, u32[]{:S(2)}) %collective-permute-start) | collective-permute-done | bytes 524320 | tf_op jit(solution)/shard_map/ppermute | solution.py:278
  16.4 2.4 %collective-permute-start.3 = (f32[8,64,256]{2,1,0:T(8,128)S(1)}, f32[8,64,256]{2,1,0:T(8,128)S(1)}, u32[]{:S(2)}, u32[]{:S(2)}) collective-permute-start(f32[8,64,256]{2,1,0:T(8,128)S(1)} %get-tuple-element.71), channel_id=1, source_target_pairs={{2,4},{3,5},{4,2},{5,3},{10,12},{11,13},{12,10},{13,11},{18,20},{1... | collective-permute-start | bytes 1572872 | tf_op jit(solution)/shard_map/ppermute | solution.py:278
  20.4 6.6 %collective-permute-done.4.other.edge = f32[8,64,256]{2,1,0:T(8,128)S(1)} collective-permute-done((f32[8,64,256]{2,1,0:T(8,128)S(1)}, f32[8,64,256]{2,1,0:T(8,128)S(1)}, u32[]{:S(2)}, u32[]{:S(2)}) %collective-permute-start.4) | collective-permute-done | bytes 524320 | tf_op jit(solution)/shard_map/ppermute | solution.py:278
  29.2 1.9 %collective-permute-start.5 = (f32[8,64,256]{2,1,0:T(8,128)S(1)}, f32[8,64,256]{2,1,0:T(8,128)S(1)}, u32[]{:S(2)}, u32[]{:S(2)}) collective-permute-start(f32[8,64,256]{2,1,0:T(8,128)S(1)} %get-tuple-element.74), channel_id=1, source_target_pairs={{2,4},{3,5},{4,2},{5,3},{10,12},{11,13},{12,10},{13,11},{18,20},{1... | collective-permute-start | bytes 1572872 | tf_op jit(solution)/shard_map/ppermute | solution.py:278
  32.8 5.0 %collective-permute-done.8.rest = f32[8,64,256]{2,1,0:T(8,128)S(1)} collective-permute-done((f32[8,64,256]{2,1,0:T(8,128)S(1)}, f32[8,64,256]{2,1,0:T(8,128)S(1)}, u32[]{:S(2)}, u32[]{:S(2)}) %collective-permute-start.8) | collective-permute-done | bytes 524320 | tf_op jit(solution)/shard_map/ppermute | solution.py:278
  38.9 2.9 %receivers.1.q_ref.refs_5_.refs_4_ = f32[3,64,128]{2,1,0:T(8,128)S(1)} custom-call(s32[7]{0:T(128)S(1)} %stack.31.scal_ref, f32[8,16,256]{2,1,0:T(8,128)S(1)} %pad_maximum_fusion.gathered_ref), custom_call_target="tpu_custom_call" | custom-call | bytes 1048576 | tf_op jit(solution)/shard_map/receivers/pallas_call | solution.py:251
  43.2 1.9 %side_a0.1 = (f32[32,64,256]{2,1,0:T(8,128)S(1)}, f32[24,64,256]{2,1,0:T(8,128)S(1)}, f32[24,64,256]{2,1,0:T(8,128)S(1)}, f32[24,64,256]{2,1,0:T(8,128)S(1)}, f32[8,64,256]{2,1,0:T(8,128)S(1)}) custom-call(s32[7]{0:T(128)S(1)} %stack.31.scal_ref, ...), custom_call_target="tpu_custom_call", output_to_operand_aliasing={{0}: (3, {}), {1}: (4, {}), {2}: (5, {}), {3}: (6, {})} | custom-call | flops 31457280 | bytes 1048576 | tf_op jit(solution)/shard_map/side_a0/pallas_call | solution.py:251
  46.7 1.9 %side_b0.1 = (f32[32,64,256]{2,1,0:T(8,128)S(1)}, f32[24,64,256]{2,1,0:T(8,128)S(1)}, f32[24,64,256]{2,1,0:T(8,128)S(1)}, f32[24,64,256]{2,1,0:T(8,128)S(1)}, f32[8,64,256]{2,1,0:T(8,128)S(1)}) custom-call(s32[7]{0:T(128)S(1)} %stack.31.scal_ref, ...), custom_call_target="tpu_custom_call", output_to_operand_aliasing={{0}: (3, {}), {1}: (4, {}), {2}: (5, {}), {3}: (6, {})} | custom-call | flops 31457280 | bytes 1048576 | tf_op jit(solution)/shard_map/side_b0/pallas_call | solution.py:251
  50.2 7.4 %collective-permute-done.11.recv_ref = f32[8,64,256]{2,1,0:T(8,128)S(1)} collective-permute-done((f32[8,64,256]{2,1,0:T(8,128)S(1)}, f32[8,64,256]{2,1,0:T(8,128)S(1)}, u32[]{:S(2)}, u32[]{:S(2)}) %collective-permute-start.11) | collective-permute-done | bytes 524320 | tf_op jit(solution)/shard_map/ppermute | solution.py:278
  57.5 1.9 %side_a1.1 = (f32[32,64,256]{2,1,0:T(8,128)S(1)}, f32[24,64,256]{2,1,0:T(8,128)S(1)}, f32[8,64,256]{2,1,0:T(8,128)S(1)}) custom-call(s32[7]{0:T(128)S(1)} %stack.31.scal_ref, f32[8,64,256]{2,1,0:T(8,128)S(1)} %collective-permute-done.11.recv_ref, f32[32,64,256]{2,1,0:T(8,128)S(1)} %get-tuple-element.93.e_ref.refs_0_, ...), custom_call_target="tpu_custom_call", output_to_operand_aliasing={{0}: (2, {}), {1}: (3, {})} | custom-call | flops 31457280 | bytes 1048576 | tf_op jit(solution)/shard_map/side_a1/pallas_call | solution.py:251
  61.1 1.9 %side_b1.1 = (f32[32,64,256]{2,1,0:T(8,128)S(1)}, f32[24,64,256]{2,1,0:T(8,128)S(1)}, f32[8,64,256]{2,1,0:T(8,128)S(1)}) custom-call(s32[7]{0:T(128)S(1)} %stack.31.scal_ref, f32[8,64,256]{2,1,0:T(8,128)S(1)} %collective-permute-done.10.recv_ref, f32[32,64,256]{2,1,0:T(8,128)S(1)} %get-tuple-element.99.refs_0_, ...), custom_call_target="tpu_custom_call", output_to_operand_aliasing={{0}: (2, {}), {1}: (3, {})} | custom-call | flops 31457280 | bytes 1048576 | tf_op jit(solution)/shard_map/side_b1/pallas_call | solution.py:251
  64.5 6.4 %collective-permute-done.13.recv_ref = f32[8,64,256]{2,1,0:T(8,128)S(1)} collective-permute-done((f32[8,64,256]{2,1,0:T(8,128)S(1)}, f32[8,64,256]{2,1,0:T(8,128)S(1)}, u32[]{:S(2)}, u32[]{:S(2)}) %collective-permute-start.13) | collective-permute-done | bytes 524320 | tf_op jit(solution)/shard_map/ppermute | solution.py:278
  70.9 1.9 %side_a2.1 = (f32[32,64,256]{2,1,0:T(8,128)S(1)}, f32[24,64,256]{2,1,0:T(8,128)S(1)}, f32[8,64,256]{2,1,0:T(8,128)S(1)}) custom-call(s32[7]{0:T(128)S(1)} %stack.31.scal_ref, f32[8,64,256]{2,1,0:T(8,128)S(1)} %collective-permute-done.13.recv_ref, f32[32,64,256]{2,1,0:T(8,128)S(1)} %get-tuple-element.103.e_ref.refs_0_, ...), custom_call_target="tpu_custom_call", output_to_operand_aliasing={{0}: (2, {}), {1}: (3, {})} | custom-call | flops 31457280 | bytes 1048576 | tf_op jit(solution)/shard_map/side_a2/pallas_call | solution.py:251
  74.5 2.0 %side_b2.1 = (f32[32,64,256]{2,1,0:T(8,128)S(1)}, f32[24,64,256]{2,1,0:T(8,128)S(1)}, f32[8,64,256]{2,1,0:T(8,128)S(1)}) custom-call(s32[7]{0:T(128)S(1)} %stack.31.scal_ref, f32[8,64,256]{2,1,0:T(8,128)S(1)} %collective-permute-done.12.recv_ref, f32[32,64,256]{2,1,0:T(8,128)S(1)} %get-tuple-element.107.refs_0_, ...), custom_call_target="tpu_custom_call", output_to_operand_aliasing={{0}: (2, {}), {1}: (3, {})} | custom-call | flops 31457280 | bytes 1048576 | tf_op jit(solution)/shard_map/side_b2/pallas_call | solution.py:251
  78.0 5.4 %collective-permute-done.15.recv_ref = f32[8,64,256]{2,1,0:T(8,128)S(1)} collective-permute-done((f32[8,64,256]{2,1,0:T(8,128)S(1)}, f32[8,64,256]{2,1,0:T(8,128)S(1)}, u32[]{:S(2)}, u32[]{:S(2)}) %collective-permute-start.15) | collective-permute-done | bytes 524320 | tf_op jit(solution)/shard_map/ppermute | solution.py:278
  83.4 2.1 %side_a3.1 = (f32[32,64,256]{2,1,0:T(8,128)S(1)}, f32[24,64,256]{2,1,0:T(8,128)S(1)}, f32[8,64,256]{2,1,0:T(8,128)S(1)}) custom-call(s32[7]{0:T(128)S(1)} %stack.31.scal_ref, f32[8,64,256]{2,1,0:T(8,128)S(1)} %collective-permute-done.15.recv_ref, f32[32,64,256]{2,1,0:T(8,128)S(1)} %get-tuple-element.111.e_ref.refs_0_, ...), custom_call_target="tpu_custom_call", output_to_operand_aliasing={{0}: (2, {}), {1}: (3, {})} | custom-call | flops 31457280 | bytes 1048576 | tf_op jit(solution)/shard_map/side_a3/pallas_call | solution.py:251
  87.2 2.0 %side_b3.1 = (f32[32,64,256]{2,1,0:T(8,128)S(1)}, f32[24,64,256]{2,1,0:T(8,128)S(1)}, f32[8,64,256]{2,1,0:T(8,128)S(1)}) custom-call(s32[7]{0:T(128)S(1)} %stack.31.scal_ref, f32[8,64,256]{2,1,0:T(8,128)S(1)} %collective-permute-done.14.recv_ref, f32[32,64,256]{2,1,0:T(8,128)S(1)} %get-tuple-element.115.refs_0_, ...), custom_call_target="tpu_custom_call", output_to_operand_aliasing={{0}: (2, {}), {1}: (3, {})} | custom-call | flops 31457280 | bytes 1048576 | tf_op jit(solution)/shard_map/side_b3/pallas_call | solution.py:251
  90.6 5.1 %collective-permute-done.17.recv_ref = f32[8,64,256]{2,1,0:T(8,128)S(1)} collective-permute-done((f32[8,64,256]{2,1,0:T(8,128)S(1)}, f32[8,64,256]{2,1,0:T(8,128)S(1)}, u32[]{:S(2)}, u32[]{:S(2)}) %collective-permute-start.17) | collective-permute-done | bytes 524320 | tf_op jit(solution)/shard_map/ppermute | solution.py:278
  99.2 2.0 %side_b4.1 = (f32[32,64,256]{2,1,0:T(8,128)S(1)}, f32[24,64,256]{2,1,0:T(8,128)S(1)}, f32[8,64,256]{2,1,0:T(8,128)S(1)}) custom-call(s32[7]{0:T(128)S(1)} %stack.31.scal_ref, f32[8,64,256]{2,1,0:T(8,128)S(1)} %collective-permute-done.16.recv_ref, f32[32,64,256]{2,1,0:T(8,128)S(1)} %get-tuple-element.123.refs_0_, ...), custom_call_target="tpu_custom_call", output_to_operand_aliasing={{0}: (2, {}), {1}: (3, {})} | custom-call | flops 31457280 | bytes 1048576 | tf_op jit(solution)/shard_map/side_b4/pallas_call | solution.py:251
  102.7 4.2 %collective-permute-done.19.recv_ref = f32[8,64,256]{2,1,0:T(8,128)S(1)} collective-permute-done((f32[8,64,256]{2,1,0:T(8,128)S(1)}, f32[8,64,256]{2,1,0:T(8,128)S(1)}, u32[]{:S(2)}, u32[]{:S(2)}) %collective-permute-start.19) | collective-permute-done | bytes 524320 | tf_op jit(solution)/shard_map/ppermute | solution.py:278
  107.4 3.0 %collective-permute-done.18.recv_ref = f32[8,64,256]{2,1,0:T(8,128)S(1)} collective-permute-done((f32[8,64,256]{2,1,0:T(8,128)S(1)}, f32[8,64,256]{2,1,0:T(8,128)S(1)}, u32[]{:S(2)}, u32[]{:S(2)}) %collective-permute-start.18) | collective-permute-done | bytes 524320 | tf_op jit(solution)/shard_map/ppermute | solution.py:278
  110.5 2.0 %side_b5.1 = (f32[32,64,256]{2,1,0:T(8,128)S(1)}, f32[24,64,256]{2,1,0:T(8,128)S(1)}) custom-call(s32[7]{0:T(128)S(1)} %stack.31.scal_ref, f32[8,64,256]{2,1,0:T(8,128)S(1)} %collective-permute-done.18.recv_ref, f32[32,64,256]{2,1,0:T(8,128)S(1)} %get-tuple-element.131.refs_0_, ...), custom_call_target="tpu_custom_call", output_to_operand_aliasing={{0}: (2, {}), {1}: (3, {})} | custom-call | flops 31457280 | bytes 1048576 | tf_op jit(solution)/shard_map/side_b5/pallas_call | solution.py:251
  118.1 2.7 %collective-permute-done.21 = f32[8,16,256]{2,1,0:T(8,128)S(1)} collective-permute-done((f32[8,16,256]{2,1,0:T(8,128)S(1)}, f32[8,16,256]{2,1,0:T(8,128)S(1)}, u32[]{:S(2)}, u32[]{:S(2)}) %collective-permute-start.21) | collective-permute-done | bytes 131104 | tf_op jit(solution)/shard_map/ppermute | solution.py:278
  (67 shorter events, 40.5 us)
Async XLA Ops:
  0.6 15.1 %collective-permute-start = (f32[8,64,256]{2,1,0:T(8,128)}, f32[8,64,256]{2,1,0:T(8,128)S(1)}, u32[]{:S(2)}, u32[]{:S(2)}) collective-permute-start(f32[8,64,256]{2,1,0:T(8,128)} %bitcast.31), channel_id=1, source_target_pairs={{0,1},{1,0},{2,3},{3,2},{4,5},{5,4},{6,7},{7,6},{8,9},{9,8},{10,11... | collective-permute-start | bytes 1572872 | tf_op jit(solution)/shard_map/ppermute | solution.py:278
  4.5 3.7 %collective-permute-start.1 = (f32[1,16,256]{2,1,0:T(8,128)S(1)}, f32[1,16,256]{2,1,0:T(8,128)S(1)}, u32[]{:S(2)}, u32[]{:S(2)}) collective-permute-start(f32[1,16,256]{2,1,0:T(8,128)S(1)} %maximum_bitcast_fusion), channel_id=1, source_target_pairs={{0,2},{1,3},{2,0},{3,1},{4,6},{5,7},{6,4},{7,5},{8,10},{9,11},{10,... | collective-permute-start | bytes 49160 | tf_op jit(solution)/shard_map/ppermute | solution.py:278
  6.1 31.6 %copy-start.1 = (f32[1,8,64,256]{3,2,1,0:T(8,128)S(1)}, f32[1,8,64,256]{3,2,1,0:T(8,128)}, u32[]{:S(2)}) copy-start(f32[1,8,64,256]{3,2,1,0:T(8,128)} %param.13) | copy-start | bytes 1572868
  6.1 31.6 %copy-start.2 = (f32[8,64,256]{2,1,0:T(8,128)S(1)}, f32[8,64,256]{2,1,0:T(8,128)}, u32[]{:S(2)}) copy-start(f32[8,64,256]{2,1,0:T(8,128)} %c_own.1) | copy-start | bytes 1572868
  8.2 18.8 %collective-permute-start.4 = (f32[8,64,256]{2,1,0:T(8,128)S(1)}, f32[8,64,256]{2,1,0:T(8,128)S(1)}, u32[]{:S(2)}, u32[]{:S(2)}) collective-permute-start(f32[8,64,256]{2,1,0:T(8,128)S(1)} %get-tuple-element.73.own), channel_id=1, source_target_pairs={{0,1},{1,0},{2,3},{3,2},{4,5},{5,4},{6,7},{7,6},{8,9},{9,8},{10,11... | collective-permute-start | bytes 1572872 | tf_op jit(solution)/shard_map/ppermute | solution.py:278
  8.7 4.8 %collective-permute-start.2 = (f32[2,16,256]{2,1,0:T(8,128)S(1)}, f32[2,16,256]{2,1,0:T(8,128)S(1)}, u32[]{:S(2)}, u32[]{:S(2)}) collective-permute-start(f32[2,16,256]{2,1,0:T(8,128)S(1)} %pad_maximum_fusion.2), channel_id=1, source_target_pairs={{0,4},{1,5},{2,6},{3,7},{4,0},{5,1},{6,2},{7,3},{8,12},{9,13},{10,... | collective-permute-start | bytes 98312 | tf_op jit(solution)/shard_map/ppermute | solution.py:278
  16.4 14.7 %collective-permute-start.3 = (f32[8,64,256]{2,1,0:T(8,128)S(1)}, f32[8,64,256]{2,1,0:T(8,128)S(1)}, u32[]{:S(2)}, u32[]{:S(2)}) collective-permute-start(f32[8,64,256]{2,1,0:T(8,128)S(1)} %get-tuple-element.71), channel_id=1, source_target_pairs={{2,4},{3,5},{4,2},{5,3},{10,12},{11,13},{12,10},{13,11},{18,20},{1... | collective-permute-start | bytes 1572872 | tf_op jit(solution)/shard_map/ppermute | solution.py:278
  18.8 19.0 %collective-permute-start.8 = (f32[8,64,256]{2,1,0:T(8,128)S(1)}, f32[8,64,256]{2,1,0:T(8,128)S(1)}, u32[]{:S(2)}, u32[]{:S(2)}) collective-permute-start(f32[8,64,256]{2,1,0:T(8,128)S(1)} %get-tuple-element.79), channel_id=1, source_target_pairs={{0,1},{1,0},{2,3},{3,2},{4,5},{5,4},{6,7},{7,6},{8,9},{9,8},{10,11... | collective-permute-start | bytes 1572872 | tf_op jit(solution)/shard_map/ppermute | solution.py:278
  20.4 22.8 %collective-permute-start.6 = (f32[8,64,256]{2,1,0:T(8,128)S(1)}, f32[8,64,256]{2,1,0:T(8,128)S(1)}, u32[]{:S(2)}, u32[]{:S(2)}) collective-permute-start(f32[8,64,256]{2,1,0:T(8,128)S(1)} %get-tuple-element.75), channel_id=1, source_target_pairs={{0,2},{1,3},{2,0},{3,1},{4,6},{5,7},{6,4},{7,5},{8,10},{9,11},{10,... | collective-permute-start | bytes 1572872 | tf_op jit(solution)/shard_map/ppermute | solution.py:278
  27.6 15.6 %collective-permute-start.7 = (f32[8,64,256]{2,1,0:T(8,128)S(1)}, f32[8,64,256]{2,1,0:T(8,128)S(1)}, u32[]{:S(2)}, u32[]{:S(2)}) collective-permute-start(f32[8,64,256]{2,1,0:T(8,128)S(1)} %get-tuple-element.76), channel_id=1, source_target_pairs={{0,2},{1,3},{2,0},{3,1},{4,6},{5,7},{6,4},{7,5},{8,10},{9,11},{10,... | collective-permute-start | bytes 1572872 | tf_op jit(solution)/shard_map/ppermute | solution.py:278
  29.2 17.5 %collective-permute-start.5 = (f32[8,64,256]{2,1,0:T(8,128)S(1)}, f32[8,64,256]{2,1,0:T(8,128)S(1)}, u32[]{:S(2)}, u32[]{:S(2)}) collective-permute-start(f32[8,64,256]{2,1,0:T(8,128)S(1)} %get-tuple-element.74), channel_id=1, source_target_pairs={{2,4},{3,5},{4,2},{5,3},{10,12},{11,13},{12,10},{13,11},{18,20},{1... | collective-permute-start | bytes 1572872 | tf_op jit(solution)/shard_map/ppermute | solution.py:278
  31.2 7.7 %collective-permute-start.9 = (f32[4,16,256]{2,1,0:T(8,128)S(1)}, f32[4,16,256]{2,1,0:T(8,128)S(1)}, u32[]{:S(2)}, u32[]{:S(2)}) collective-permute-start(f32[4,16,256]{2,1,0:T(8,128)S(1)} %pad_maximum_fusion.1), channel_id=1, source_target_pairs={{0,1},{1,0},{2,3},{3,2},{4,5},{5,4},{6,7},{7,6},{8,9},{9,8},{10,11... | collective-permute-start | bytes 196616 | tf_op jit(solution)/shard_map/ppermute | solution.py:278
  45.1 12.4 %collective-permute-start.11 = (f32[8,64,256]{2,1,0:T(8,128)S(1)}, f32[8,64,256]{2,1,0:T(8,128)S(1)}, u32[]{:S(2)}, u32[]{:S(2)}) collective-permute-start(f32[8,64,256]{2,1,0:T(8,128)S(1)} %get-tuple-element.92), channel_id=1, source_target_pairs={{0,2},{1,3},{2,0},{3,1},{4,6},{5,7},{6,4},{7,5},{8,10},{9,11},{10,... | collective-permute-start | bytes 1572872 | tf_op jit(solution)/shard_map/ppermute | solution.py:278
  48.7 12.4 %collective-permute-start.10 = (f32[8,64,256]{2,1,0:T(8,128)S(1)}, f32[8,64,256]{2,1,0:T(8,128)S(1)}, u32[]{:S(2)}, u32[]{:S(2)}) collective-permute-start(f32[8,64,256]{2,1,0:T(8,128)S(1)} %get-tuple-element.91), channel_id=1, source_target_pairs={{0,8},{1,9},{2,4},{3,5},{4,2},{5,3},{6,14},{7,15},{8,0},{9,1},{10,... | collective-permute-start | bytes 1572872 | tf_op jit(solution)/shard_map/ppermute | solution.py:278
  59.4 11.5 %collective-permute-start.13 = (f32[8,64,256]{2,1,0:T(8,128)S(1)}, f32[8,64,256]{2,1,0:T(8,128)S(1)}, u32[]{:S(2)}, u32[]{:S(2)}) collective-permute-start(f32[8,64,256]{2,1,0:T(8,128)S(1)} %get-tuple-element.102), channel_id=1, source_target_pairs={{0,2},{1,3},{2,0},{3,1},{4,6},{5,7},{6,4},{7,5},{8,10},{9,11},{10,... | collective-permute-start | bytes 1572872 | tf_op jit(solution)/shard_map/ppermute | solution.py:278
  63.0 11.4 %collective-permute-start.12 = (f32[8,64,256]{2,1,0:T(8,128)S(1)}, f32[8,64,256]{2,1,0:T(8,128)S(1)}, u32[]{:S(2)}, u32[]{:S(2)}) collective-permute-start(f32[8,64,256]{2,1,0:T(8,128)S(1)} %get-tuple-element.101), channel_id=1, source_target_pairs={{0,8},{1,9},{2,4},{3,5},{4,2},{5,3},{6,14},{7,15},{8,0},{9,1},{10,... | collective-permute-start | bytes 1572872 | tf_op jit(solution)/shard_map/ppermute | solution.py:278
  72.8 10.6 %collective-permute-start.15 = (f32[8,64,256]{2,1,0:T(8,128)S(1)}, f32[8,64,256]{2,1,0:T(8,128)S(1)}, u32[]{:S(2)}, u32[]{:S(2)}) collective-permute-start(f32[8,64,256]{2,1,0:T(8,128)S(1)} %get-tuple-element.110), channel_id=1, source_target_pairs={{0,2},{1,3},{2,0},{3,1},{4,6},{5,7},{6,4},{7,5},{8,10},{9,11},{10,... | collective-permute-start | bytes 1572872 | tf_op jit(solution)/shard_map/ppermute | solution.py:278
  76.4 10.7 %collective-permute-start.14 = (f32[8,64,256]{2,1,0:T(8,128)S(1)}, f32[8,64,256]{2,1,0:T(8,128)S(1)}, u32[]{:S(2)}, u32[]{:S(2)}) collective-permute-start(f32[8,64,256]{2,1,0:T(8,128)S(1)} %get-tuple-element.109), channel_id=1, source_target_pairs={{0,8},{1,9},{2,4},{3,5},{4,2},{5,3},{6,14},{7,15},{8,0},{9,1},{10,... | collective-permute-start | bytes 1572872 | tf_op jit(solution)/shard_map/ppermute | solution.py:278
  85.5 10.2 %collective-permute-start.17 = (f32[8,64,256]{2,1,0:T(8,128)S(1)}, f32[8,64,256]{2,1,0:T(8,128)S(1)}, u32[]{:S(2)}, u32[]{:S(2)}) collective-permute-start(f32[8,64,256]{2,1,0:T(8,128)S(1)} %get-tuple-element.118), channel_id=1, source_target_pairs={{0,2},{1,3},{2,0},{3,1},{4,6},{5,7},{6,4},{7,5},{8,10},{9,11},{10,... | collective-permute-start | bytes 1572872 | tf_op jit(solution)/shard_map/ppermute | solution.py:278
  89.1 10.1 %collective-permute-start.16 = (f32[8,64,256]{2,1,0:T(8,128)S(1)}, f32[8,64,256]{2,1,0:T(8,128)S(1)}, u32[]{:S(2)}, u32[]{:S(2)}) collective-permute-start(f32[8,64,256]{2,1,0:T(8,128)S(1)} %get-tuple-element.117), channel_id=1, source_target_pairs={{0,8},{1,9},{2,4},{3,5},{4,2},{5,3},{6,14},{7,15},{8,0},{9,1},{10,... | collective-permute-start | bytes 1572872 | tf_op jit(solution)/shard_map/ppermute | solution.py:278
  97.6 9.2 %collective-permute-start.19 = (f32[8,64,256]{2,1,0:T(8,128)S(1)}, f32[8,64,256]{2,1,0:T(8,128)S(1)}, u32[]{:S(2)}, u32[]{:S(2)}) collective-permute-start(f32[8,64,256]{2,1,0:T(8,128)S(1)} %get-tuple-element.126), channel_id=1, source_target_pairs={{0,2},{1,3},{2,0},{3,1},{4,6},{5,7},{6,4},{7,5},{8,10},{9,11},{10,... | collective-permute-start | bytes 1572872 | tf_op jit(solution)/shard_map/ppermute | solution.py:278
  101.2 9.2 %collective-permute-start.18 = (f32[8,64,256]{2,1,0:T(8,128)S(1)}, f32[8,64,256]{2,1,0:T(8,128)S(1)}, u32[]{:S(2)}, u32[]{:S(2)}) collective-permute-start(f32[8,64,256]{2,1,0:T(8,128)S(1)} %get-tuple-element.125), channel_id=1, source_target_pairs={{0,8},{1,9},{2,4},{3,5},{4,2},{5,3},{6,14},{7,15},{8,0},{9,1},{10,... | collective-permute-start | bytes 1572872 | tf_op jit(solution)/shard_map/ppermute | solution.py:278
  113.0 1.6 %collective-permute-start.20 = (f32[8,32,256]{2,1,0:T(8,128)S(1)}, f32[8,32,256]{2,1,0:T(8,128)S(1)}, u32[]{:S(2)}, u32[]{:S(2)}) collective-permute-start(f32[8,32,256]{2,1,0:T(8,128)S(1)} %give.1), channel_id=1, source_target_pairs={{0,8},{1,9},{2,10},{3,11},{4,12},{5,13},{6,14},{7,15},{8,0},{9,1},... | collective-permute-start | bytes 786440 | tf_op jit(solution)/shard_map/ppermute | solution.py:278
  115.2 5.6 %collective-permute-start.21 = (f32[8,16,256]{2,1,0:T(8,128)S(1)}, f32[8,16,256]{2,1,0:T(8,128)S(1)}, u32[]{:S(2)}, u32[]{:S(2)}) collective-permute-start(f32[8,16,256]{2,1,0:T(8,128)S(1)} %pair.1.late_ref), channel_id=1, source_target_pairs={{0,16},{1,17},{2,18},{3,19},{4,20},{5,21},{6,22},{7,23},{8,24},{9,... | collective-permute-start | bytes 393224 | tf_op jit(solution)/shard_map/ppermute | solution.py:278
  (2 other events, 30.0 us)

commit v7 on v6

--- a/solution.py
+++ b/solution.py
@@ -91,7 +91,7 @@
         return tuple(out)
 
     zero = jnp.zeros(q_ref.shape[1:], F32)
-    acc = lax.fori_loop(0, n, body, (zero, zero, zero))
+    acc = lax.fori_loop(0, n, body, (zero, zero, zero), unroll=4)
     for j in range(3):
         q_ref[j] = acc[j]
 
@@ -164,6 +164,14 @@
     wy_ref[...] = band(4 * ny, 8 * ny, ny)
 
 
+def start_kernel(scal_ref, recv_a, recv_b, e_in, o_in, a_ref, c_ref, q_ref, wz_ref, wy_ref, e_ref, o_ref):
+    odd = scal_ref[1]
+    for i in range(8):
+        e_ref[24 + i] = keep_if(scal_ref[6 - odd], recv_a[7 - i])
+        e_ref[7 - i] = keep_if(scal_ref[5 + odd], recv_b[i])
+    advance(e_ref, 8, o_ref, 4, o_ref, 4, a_ref, c_ref, q_ref, wz_ref, wy_ref, 0, 4, 0)
+
+
 def inner_kernel(scal_ref, e_ref, o_in, a_ref, c_ref, q_ref, wz_ref, wy_ref, f_ref, g_in, o_ref, g_ref, *, r, length):
     y = scal_ref[2]
     if r > 0:
@@ -174,34 +182,32 @@
     advance(e_ref, 8, o_ref, 4, o_ref, 4, a_ref, c_ref, q_ref, wz_ref, wy_ref, 4, 2, 2 * r)
 
 
-def side_steps(side, r, e_ref, o_ref, args, new):
-    advance(e_ref, 8, o_ref, 4, o_ref, 4, *args, 12 if side == "a" else -4, 2, 2 * r)
-    advance(o_ref, 4, e_ref, 8, e_ref, 8, *args, 8 if side == "a" else 0, 2, 2 * r + 1, extra=new)
-
-
-def side_kernel(scal_ref, recv_ref, *refs, r, side, last):
+def side_kernel(scal_ref, recv_ref, e_in, o_in, a_in, c_in, q_ref, wz_ref, wy_ref, e_ref, o_ref, *outs, r, side, last):
     if r == 0:
-        edge_ref, e_in, o_in, a_in, c_in, q_ref, wz_ref, wy_ref, e_ref, o_ref, a_ref, c_ref, new = refs
+        a_ref, c_ref, new = outs
     else:
-        e_in, o_in, a_ref, c_ref, q_ref, wz_ref, wy_ref, e_ref, o_ref = refs[:9]
-        new = None if last else refs[9]
+        a_ref, c_ref, new = a_in, c_in, None if last else outs[0]
 
     def work():
         odd = scal_ref[1]
         inside = scal_ref[6 - odd] if side == "a" else scal_ref[5 + odd]
-        for i in range(8):
-            if side == "a":
-                e_ref[24 + i] = keep_if(inside, recv_ref[7 - i])
-            else:
-                e_ref[7 - i] = keep_if(inside, recv_ref[i])
+        args = (a_ref, c_ref, q_ref, wz_ref, wy_ref)
         if r == 0:
             for i in range(4):
                 to, at = (20 + i, 3 - i) if side == "a" else (3 - i, i)
-                o_ref[to] = keep_if(inside, edge_ref[at])
-                cv = keep_if(inside, edge_ref[4 + at])
+                o_ref[to] = keep_if(inside, recv_ref[at])
+                cv = keep_if(inside, recv_ref[4 + at])
                 c_ref[to] = cv * (1.0 / SCALE)
                 a_ref[to] = 2.0 + CENTRE * cv
-        side_steps(side, r, e_ref, o_ref, (a_ref, c_ref, q_ref, wz_ref, wy_ref), new)
+            advance(e_ref, 8, o_ref, 4, o_ref, 4, *args, 16 if side == "a" else -4, 1, 0)
+        else:
+            for i in range(8):
+                if side == "a":
+                    e_ref[24 + i] = keep_if(inside, recv_ref[7 - i])
+                else:
+                    e_ref[7 - i] = keep_if(inside, recv_ref[i])
+            advance(e_ref, 8, o_ref, 4, o_ref, 4, *args, 12 if side == "a" else -4, 2, 2 * r)
+        advance(o_ref, 4, e_ref, 8, e_ref, 8, *args, 8 if side == "a" else 0, 2, 2 * r + 1, extra=new)
 
     if last:
         own_a = (scal_ref[1] + scal_ref[2]) % 2
@@ -330,7 +336,7 @@
     recv_a, recv_b = move(send_a, near_a), move(send_b, near_b)
     gathered = jnp.concatenate([gathered, move(after(gathered, recv_b), swap_y)], 0)
     edge_a, edge_b = call(edge_kernel, [plane(8), plane(8)], [scal, edge, y_edge], name="edges")
-    edge_a, edge_b = move(edge_a, near_a), move(edge_b, near_b)
+    edge_a, edge_b = move(edge_a, swap_a), move(edge_b, swap_b)
     q = call(
         functools.partial(q_kernel, steps=steps, length=length),
         VM((3, ny, 128), F32),
@@ -351,27 +357,35 @@
         if r:
             recv_a = move(send_a, swap_a)
             recv_b = move(send_b, swap_b)
-        o, g = call(
-            functools.partial(inner_kernel, r=r, length=length),
-            [plane(24), plane(length)],
-            [scal, e, o, a, c, q, wz, wy, forward, g],
-            {2: 0, 9: 1},
-            flops=work,
-            name=f"inner{r}",
-        )
+        if r:
+            o, g = call(
+                functools.partial(inner_kernel, r=r, length=length),
+                [plane(24), plane(length)],
+                [scal, e, o, a, c, q, wz, wy, forward, g],
+                {2: 0, 9: 1},
+                flops=work,
+                name=f"inner{r}",
+            )
+        else:
+            e, o = call(
+                start_kernel,
+                [plane(32), plane(24)],
+                [scal, recv_a, recv_b, e, o, a, c, q, wz, wy],
+                {3: 0, 4: 1},
+                flops=work,
+                name="start",
+            )
         last = r == rounds - 1
         sent = []
         for side in "ab":
-            got = [recv_a if side == "a" else recv_b]
-            if r == 0:
-                got.append(edge_a if side == "a" else edge_b)
-            kept = 4 if r == 0 else 2
-            at = 1 + len(got)
+            got = {"a": recv_a, "b": recv_b}[side] if r else {"a": edge_a, "b": edge_b}[side]
+            kept = 2 if r else 4
+            outs = [plane(32), plane(24), plane(24), plane(24)][:kept] + ([] if last else [plane(8)])
             e, o, *new = call(
                 functools.partial(side_kernel, r=r, side=side, last=last),
-                [plane(32), plane(24), plane(24), plane(24)][:kept] + ([] if last else [plane(8)]),
-                [scal, *got, e, o, a, c, q, wz, wy],
-                {at + i: i for i in range(kept)},
+                outs,
+                [scal, got, e, o, a, c, q, wz, wy],
+                {2 + i: i for i in range(kept)},
                 flops=work,
                 name=f"side_{side}{r}",
             )

time: 122 us -> 121 us (level)
  waiting for transfers between devices: 53.9 us -> 56.2 us
  starting transfers between devices: 23.2 us -> 21.3 us
  Pallas kernels: 40.4 us -> 39.1 us
    ppermute x22, waiting for transfers between devices: 53.9 us -> 56.2 us  [move(): return lax.ppermute(x, ('shot', 'space'), pairs)]
    ppermute x22, starting transfers between devices: 23.2 us -> 21.3 us  [move(): return lax.ppermute(x, ('shot', 'space'), pairs)]
    pallas_call x26, Pallas kernels: 38.6 us -> 37.4 us  [call(): pl.pallas_call(kernel, out_shape=out_shapes, in_specs=specs, out_specs=ja...]
  transfers between devices with their start and end apart: 22 -> 22, of which waited for: 13 -> 14; matrix products, arithmetic and copies ran while one was open for 1% -> 1% of each run, Pallas kernels for 31% -> 30%
where the time goes in v7:
time: 121 us
  waiting for transfers between devices  56.2 us (46%)
  Pallas kernels  39.1 us (32%)
  starting transfers between devices  21.3 us (18%)
  other arithmetic  2.19 us (2%)
  between operations  1.58 us (1%)
    ppermute x22, waiting for transfers between devices, move(): return lax.ppermute(x, ('shot', 'space'), pairs)  56.2 us
    pallas_call x26, Pallas kernels, call(): pl.pallas_call(kernel, out_shape=out_shapes, in_specs=specs, out_specs=ja...  37.4 us
    ppermute x22, starting transfers between devices, move(): return lax.ppermute(x, ('shot', 'space'), pairs)  21.3 us
  transfers between devices with their start and end apart: 22, of which 14 were waited for; matrix products, arithmetic and copies ran while one was open for 1% of the time, Pallas kernels for 30%

profile of v7, /device:TPU:16, one launch (start us, length us, event | category | flops | bytes accessed | tf_op | source)
XLA Modules:
  0.0 120.8 jit_solution(4911338865589582484)
XLA Ops:
  8.8 4.7 %collective-permute-done.5 = f32[2,16,256]{2,1,0:T(8,128)S(1)} collective-permute-done((f32[2,16,256]{2,1,0:T(8,128)S(1)}, f32[2,16,256]{2,1,0:T(8,128)S(1)}, u32[]{:S(2)}, u32[]{:S(2)}) %collective-permute-start.5) | collective-permute-done | bytes 32800 | tf_op jit(solution)/shard_map/ppermute | solution.py:284
  13.6 2.2 %collective-permute-done.4.other = f32[8,64,256]{2,1,0:T(8,128)S(1)} collective-permute-done((f32[8,64,256]{2,1,0:T(8,128)}, f32[8,64,256]{2,1,0:T(8,128)S(1)}, u32[]{:S(2)}, u32[]{:S(2)}) %collective-permute-start.4) | collective-permute-done | bytes 524320 | tf_op jit(solution)/shard_map/ppermute | solution.py:284
  16.4 2.4 %collective-permute-start.7 = (f32[8,64,256]{2,1,0:T(8,128)S(1)}, f32[8,64,256]{2,1,0:T(8,128)S(1)}, u32[]{:S(2)}, u32[]{:S(2)}) collective-permute-start(f32[8,64,256]{2,1,0:T(8,128)S(1)} %get-tuple-element.76), channel_id=1, source_target_pairs={{2,4},{3,5},{4,2},{5,3},{10,12},{11,13},{12,10},{13,11},{18,20},{1... | collective-permute-start | bytes 1572872 | tf_op jit(solution)/shard_map/ppermute | solution.py:284
  20.4 6.6 %collective-permute-done.1.other.edge = f32[8,64,256]{2,1,0:T(8,128)S(1)} collective-permute-done((f32[8,64,256]{2,1,0:T(8,128)S(1)}, f32[8,64,256]{2,1,0:T(8,128)S(1)}, u32[]{:S(2)}, u32[]{:S(2)}) %collective-permute-start.1) | collective-permute-done | bytes 524320 | tf_op jit(solution)/shard_map/ppermute | solution.py:284
  32.0 5.8 %collective-permute-done.8.rest = f32[8,64,256]{2,1,0:T(8,128)S(1)} collective-permute-done((f32[8,64,256]{2,1,0:T(8,128)S(1)}, f32[8,64,256]{2,1,0:T(8,128)S(1)}, u32[]{:S(2)}, u32[]{:S(2)}) %collective-permute-start.8) | collective-permute-done | bytes 524320 | tf_op jit(solution)/shard_map/ppermute | solution.py:284
  38.9 2.1 %receivers.1.q_ref = f32[3,64,128]{2,1,0:T(8,128)S(1)} custom-call(s32[7]{0:T(128)S(1)} %stack.31.scal_ref, f32[8,16,256]{2,1,0:T(8,128)S(1)} %pad_maximum_fusion.gathered_ref), custom_call_target="tpu_custom_call" | custom-call | bytes 1048576 | tf_op jit(solution)/shard_map/receivers/pallas_call | solution.py:257
  41.0 1.8 %start.1 = (f32[32,64,256]{2,1,0:T(8,128)S(1)}, f32[24,64,256]{2,1,0:T(8,128)S(1)}) custom-call(s32[7]{0:T(128)S(1)} %stack.31.scal_ref, f32[8,64,256]{2,1,0:T(8,128)S(1)} %collective-permute-done.6.recv_a, f32[8,64,256]{2,1,0:T(8,128)S(1)} %collective-permute-done.7.recv_b, ...), custom_call_target="tpu_custom_call", output_to_operand_aliasing={{0}: (3, {}), {1}: (4, {})} | custom-call | flops 31457280 | bytes 1048576 | tf_op jit(solution)/shard_map/start/pallas_call | solution.py:257
  49.3 7.5 %collective-permute-done.11.recv_ref = f32[8,64,256]{2,1,0:T(8,128)S(1)} collective-permute-done((f32[8,64,256]{2,1,0:T(8,128)S(1)}, f32[8,64,256]{2,1,0:T(8,128)S(1)}, u32[]{:S(2)}, u32[]{:S(2)}) %collective-permute-start.11) | collective-permute-done | bytes 524320 | tf_op jit(solution)/shard_map/ppermute | solution.py:284
  56.9 1.9 %side_a1.1 = (f32[32,64,256]{2,1,0:T(8,128)S(1)}, f32[24,64,256]{2,1,0:T(8,128)S(1)}, f32[8,64,256]{2,1,0:T(8,128)S(1)}) custom-call(s32[7]{0:T(128)S(1)} %stack.31.scal_ref, f32[8,64,256]{2,1,0:T(8,128)S(1)} %collective-permute-done.11.recv_ref, f32[32,64,256]{2,1,0:T(8,128)S(1)} %get-tuple-element.94.e_ref.e_in, ...), custom_call_target="tpu_custom_call", output_to_operand_aliasing={{0}: (2, {}), {1}: (3, {})} | custom-call | flops 31457280 | bytes 1048576 | tf_op jit(solution)/shard_map/side_a1/pallas_call | solution.py:257
  60.4 1.9 %side_b1.1 = (f32[32,64,256]{2,1,0:T(8,128)S(1)}, f32[24,64,256]{2,1,0:T(8,128)S(1)}, f32[8,64,256]{2,1,0:T(8,128)S(1)}) custom-call(s32[7]{0:T(128)S(1)} %stack.31.scal_ref, f32[8,64,256]{2,1,0:T(8,128)S(1)} %collective-permute-done.10.recv_ref, f32[32,64,256]{2,1,0:T(8,128)S(1)} %get-tuple-element.99.e_in, ...), custom_call_target="tpu_custom_call", output_to_operand_aliasing={{0}: (2, {}), {1}: (3, {})} | custom-call | flops 31457280 | bytes 1048576 | tf_op jit(solution)/shard_map/side_b1/pallas_call | solution.py:257
  63.8 6.5 %collective-permute-done.13.recv_ref = f32[8,64,256]{2,1,0:T(8,128)S(1)} collective-permute-done((f32[8,64,256]{2,1,0:T(8,128)S(1)}, f32[8,64,256]{2,1,0:T(8,128)S(1)}, u32[]{:S(2)}, u32[]{:S(2)}) %collective-permute-start.13) | collective-permute-done | bytes 524320 | tf_op jit(solution)/shard_map/ppermute | solution.py:284
  70.3 1.9 %side_a2.1 = (f32[32,64,256]{2,1,0:T(8,128)S(1)}, f32[24,64,256]{2,1,0:T(8,128)S(1)}, f32[8,64,256]{2,1,0:T(8,128)S(1)}) custom-call(s32[7]{0:T(128)S(1)} %stack.31.scal_ref, f32[8,64,256]{2,1,0:T(8,128)S(1)} %collective-permute-done.13.recv_ref, f32[32,64,256]{2,1,0:T(8,128)S(1)} %get-tuple-element.103.e_ref.e_in, ...), custom_call_target="tpu_custom_call", output_to_operand_aliasing={{0}: (2, {}), {1}: (3, {})} | custom-call | flops 31457280 | bytes 1048576 | tf_op jit(solution)/shard_map/side_a2/pallas_call | solution.py:257
  73.8 2.0 %side_b2.1 = (f32[32,64,256]{2,1,0:T(8,128)S(1)}, f32[24,64,256]{2,1,0:T(8,128)S(1)}, f32[8,64,256]{2,1,0:T(8,128)S(1)}) custom-call(s32[7]{0:T(128)S(1)} %stack.31.scal_ref, f32[8,64,256]{2,1,0:T(8,128)S(1)} %collective-permute-done.12.recv_ref, f32[32,64,256]{2,1,0:T(8,128)S(1)} %get-tuple-element.107.e_in, ...), custom_call_target="tpu_custom_call", output_to_operand_aliasing={{0}: (2, {}), {1}: (3, {})} | custom-call | flops 31457280 | bytes 1048576 | tf_op jit(solution)/shard_map/side_b2/pallas_call | solution.py:257
  77.2 5.5 %collective-permute-done.15.recv_ref = f32[8,64,256]{2,1,0:T(8,128)S(1)} collective-permute-done((f32[8,64,256]{2,1,0:T(8,128)S(1)}, f32[8,64,256]{2,1,0:T(8,128)S(1)}, u32[]{:S(2)}, u32[]{:S(2)}) %collective-permute-start.15) | collective-permute-done | bytes 524320 | tf_op jit(solution)/shard_map/ppermute | solution.py:284
  82.8 1.9 %side_a3.1 = (f32[32,64,256]{2,1,0:T(8,128)S(1)}, f32[24,64,256]{2,1,0:T(8,128)S(1)}, f32[8,64,256]{2,1,0:T(8,128)S(1)}) custom-call(s32[7]{0:T(128)S(1)} %stack.31.scal_ref, f32[8,64,256]{2,1,0:T(8,128)S(1)} %collective-permute-done.15.recv_ref, f32[32,64,256]{2,1,0:T(8,128)S(1)} %get-tuple-element.111.e_ref.e_in, ...), custom_call_target="tpu_custom_call", output_to_operand_aliasing={{0}: (2, {}), {1}: (3, {})} | custom-call | flops 31457280 | bytes 1048576 | tf_op jit(solution)/shard_map/side_a3/pallas_call | solution.py:257
  84.6 1.8 %collective-permute-start.17 = (f32[8,64,256]{2,1,0:T(8,128)S(1)}, f32[8,64,256]{2,1,0:T(8,128)S(1)}, u32[]{:S(2)}, u32[]{:S(2)}) collective-permute-start(f32[8,64,256]{2,1,0:T(8,128)S(1)} %get-tuple-element.118), channel_id=1, source_target_pairs={{0,2},{1,3},{2,0},{3,1},{4,6},{5,7},{6,4},{7,5},{8,10},{9,11},{10,... | collective-permute-start | bytes 1572872 | tf_op jit(solution)/shard_map/ppermute | solution.py:284
  86.5 2.0 %side_b3.1 = (f32[32,64,256]{2,1,0:T(8,128)S(1)}, f32[24,64,256]{2,1,0:T(8,128)S(1)}, f32[8,64,256]{2,1,0:T(8,128)S(1)}) custom-call(s32[7]{0:T(128)S(1)} %stack.31.scal_ref, f32[8,64,256]{2,1,0:T(8,128)S(1)} %collective-permute-done.14.recv_ref, f32[32,64,256]{2,1,0:T(8,128)S(1)} %get-tuple-element.115.e_in, ...), custom_call_target="tpu_custom_call", output_to_operand_aliasing={{0}: (2, {}), {1}: (3, {})} | custom-call | flops 31457280 | bytes 1048576 | tf_op jit(solution)/shard_map/side_b3/pallas_call | solution.py:257
  89.9 5.2 %collective-permute-done.17.recv_ref = f32[8,64,256]{2,1,0:T(8,128)S(1)} collective-permute-done((f32[8,64,256]{2,1,0:T(8,128)S(1)}, f32[8,64,256]{2,1,0:T(8,128)S(1)}, u32[]{:S(2)}, u32[]{:S(2)}) %collective-permute-start.17) | collective-permute-done | bytes 524320 | tf_op jit(solution)/shard_map/ppermute | solution.py:284
  95.1 1.9 %side_a4.1 = (f32[32,64,256]{2,1,0:T(8,128)S(1)}, f32[24,64,256]{2,1,0:T(8,128)S(1)}, f32[8,64,256]{2,1,0:T(8,128)S(1)}) custom-call(s32[7]{0:T(128)S(1)} %stack.31.scal_ref, f32[8,64,256]{2,1,0:T(8,128)S(1)} %collective-permute-done.17.recv_ref, f32[32,64,256]{2,1,0:T(8,128)S(1)} %get-tuple-element.119.e_ref.e_in, ...), custom_call_target="tpu_custom_call", output_to_operand_aliasing={{0}: (2, {}), {1}: (3, {})} | custom-call | flops 31457280 | bytes 1048576 | tf_op jit(solution)/shard_map/side_a4/pallas_call | solution.py:257
  98.5 2.0 %side_b4.1 = (f32[32,64,256]{2,1,0:T(8,128)S(1)}, f32[24,64,256]{2,1,0:T(8,128)S(1)}, f32[8,64,256]{2,1,0:T(8,128)S(1)}) custom-call(s32[7]{0:T(128)S(1)} %stack.31.scal_ref, f32[8,64,256]{2,1,0:T(8,128)S(1)} %collective-permute-done.16.recv_ref, f32[32,64,256]{2,1,0:T(8,128)S(1)} %get-tuple-element.123.e_in, ...), custom_call_target="tpu_custom_call", output_to_operand_aliasing={{0}: (2, {}), {1}: (3, {})} | custom-call | flops 31457280 | bytes 1048576 | tf_op jit(solution)/shard_map/side_b4/pallas_call | solution.py:257
  102.0 4.2 %collective-permute-done.19.recv_ref = f32[8,64,256]{2,1,0:T(8,128)S(1)} collective-permute-done((f32[8,64,256]{2,1,0:T(8,128)S(1)}, f32[8,64,256]{2,1,0:T(8,128)S(1)}, u32[]{:S(2)}, u32[]{:S(2)}) %collective-permute-start.19) | collective-permute-done | bytes 524320 | tf_op jit(solution)/shard_map/ppermute | solution.py:284
  106.8 3.0 %collective-permute-done.18.recv_ref = f32[8,64,256]{2,1,0:T(8,128)S(1)} collective-permute-done((f32[8,64,256]{2,1,0:T(8,128)S(1)}, f32[8,64,256]{2,1,0:T(8,128)S(1)}, u32[]{:S(2)}, u32[]{:S(2)}) %collective-permute-start.18) | collective-permute-done | bytes 524320 | tf_op jit(solution)/shard_map/ppermute | solution.py:284
  109.7 2.0 %side_b5.1 = (f32[32,64,256]{2,1,0:T(8,128)S(1)}, f32[24,64,256]{2,1,0:T(8,128)S(1)}) custom-call(s32[7]{0:T(128)S(1)} %stack.31.scal_ref, f32[8,64,256]{2,1,0:T(8,128)S(1)} %collective-permute-done.18.recv_ref, f32[32,64,256]{2,1,0:T(8,128)S(1)} %get-tuple-element.131.e_in, ...), custom_call_target="tpu_custom_call", output_to_operand_aliasing={{0}: (2, {}), {1}: (3, {})} | custom-call | flops 31457280 | bytes 1048576 | tf_op jit(solution)/shard_map/side_b5/pallas_call | solution.py:257
  117.5 2.6 %collective-permute-done.21 = f32[8,16,256]{2,1,0:T(8,128)S(1)} collective-permute-done((f32[8,16,256]{2,1,0:T(8,128)S(1)}, f32[8,16,256]{2,1,0:T(8,128)S(1)}, u32[]{:S(2)}, u32[]{:S(2)}) %collective-permute-start.21) | collective-permute-done | bytes 131104 | tf_op jit(solution)/shard_map/ppermute | solution.py:284
  (67 shorter events, 40.1 us)
Async XLA Ops:
  0.6 15.1 %collective-permute-start.4 = (f32[8,64,256]{2,1,0:T(8,128)}, f32[8,64,256]{2,1,0:T(8,128)S(1)}, u32[]{:S(2)}, u32[]{:S(2)}) collective-permute-start(f32[8,64,256]{2,1,0:T(8,128)} %bitcast.30), channel_id=1, source_target_pairs={{0,1},{1,0},{2,3},{3,2},{4,5},{5,4},{6,7},{7,6},{8,9},{9,8},{10,11... | collective-permute-start | bytes 1572872 | tf_op jit(solution)/shard_map/ppermute | solution.py:284
  4.5 3.7 %collective-permute-start = (f32[1,16,256]{2,1,0:T(8,128)S(1)}, f32[1,16,256]{2,1,0:T(8,128)S(1)}, u32[]{:S(2)}, u32[]{:S(2)}) collective-permute-start(f32[1,16,256]{2,1,0:T(8,128)S(1)} %maximum_bitcast_fusion), channel_id=1, source_target_pairs={{0,2},{1,3},{2,0},{3,1},{4,6},{5,7},{6,4},{7,5},{8,10},{9,11},{10,... | collective-permute-start | bytes 49160 | tf_op jit(solution)/shard_map/ppermute | solution.py:284
  6.1 31.6 %copy-start.1 = (f32[1,8,64,256]{3,2,1,0:T(8,128)S(1)}, f32[1,8,64,256]{3,2,1,0:T(8,128)}, u32[]{:S(2)}) copy-start(f32[1,8,64,256]{3,2,1,0:T(8,128)} %param.13) | copy-start | bytes 1572868
  6.1 31.6 %copy-start.2 = (f32[8,64,256]{2,1,0:T(8,128)S(1)}, f32[8,64,256]{2,1,0:T(8,128)}, u32[]{:S(2)}) copy-start(f32[8,64,256]{2,1,0:T(8,128)} %c_own.1) | copy-start | bytes 1572868
  8.2 18.8 %collective-permute-start.1 = (f32[8,64,256]{2,1,0:T(8,128)S(1)}, f32[8,64,256]{2,1,0:T(8,128)S(1)}, u32[]{:S(2)}, u32[]{:S(2)}) collective-permute-start(f32[8,64,256]{2,1,0:T(8,128)S(1)} %get-tuple-element.71.own), channel_id=1, source_target_pairs={{0,1},{1,0},{2,3},{3,2},{4,5},{5,4},{6,7},{7,6},{8,9},{9,8},{10,11... | collective-permute-start | bytes 1572872 | tf_op jit(solution)/shard_map/ppermute | solution.py:284
  8.7 4.8 %collective-permute-start.5 = (f32[2,16,256]{2,1,0:T(8,128)S(1)}, f32[2,16,256]{2,1,0:T(8,128)S(1)}, u32[]{:S(2)}, u32[]{:S(2)}) collective-permute-start(f32[2,16,256]{2,1,0:T(8,128)S(1)} %pad_maximum_fusion.2), channel_id=1, source_target_pairs={{0,4},{1,5},{2,6},{3,7},{4,0},{5,1},{6,2},{7,3},{8,12},{9,13},{10,... | collective-permute-start | bytes 98312 | tf_op jit(solution)/shard_map/ppermute | solution.py:284
  16.4 14.1 %collective-permute-start.7 = (f32[8,64,256]{2,1,0:T(8,128)S(1)}, f32[8,64,256]{2,1,0:T(8,128)S(1)}, u32[]{:S(2)}, u32[]{:S(2)}) collective-permute-start(f32[8,64,256]{2,1,0:T(8,128)S(1)} %get-tuple-element.76), channel_id=1, source_target_pairs={{2,4},{3,5},{4,2},{5,3},{10,12},{11,13},{12,10},{13,11},{18,20},{1... | collective-permute-start | bytes 1572872 | tf_op jit(solution)/shard_map/ppermute | solution.py:284
  18.8 19.0 %collective-permute-start.8 = (f32[8,64,256]{2,1,0:T(8,128)S(1)}, f32[8,64,256]{2,1,0:T(8,128)S(1)}, u32[]{:S(2)}, u32[]{:S(2)}) collective-permute-start(f32[8,64,256]{2,1,0:T(8,128)S(1)} %get-tuple-element.79), channel_id=1, source_target_pairs={{0,1},{1,0},{2,3},{3,2},{4,5},{5,4},{6,7},{7,6},{8,9},{9,8},{10,11... | collective-permute-start | bytes 1572872 | tf_op jit(solution)/shard_map/ppermute | solution.py:284
  20.4 20.6 %collective-permute-start.6 = (f32[8,64,256]{2,1,0:T(8,128)S(1)}, f32[8,64,256]{2,1,0:T(8,128)S(1)}, u32[]{:S(2)}, u32[]{:S(2)}) collective-permute-start(f32[8,64,256]{2,1,0:T(8,128)S(1)} %get-tuple-element.75), channel_id=1, source_target_pairs={{0,2},{1,3},{2,0},{3,1},{4,6},{5,7},{6,4},{7,5},{8,10},{9,11},{10,... | collective-permute-start | bytes 1572872 | tf_op jit(solution)/shard_map/ppermute | solution.py:284
  27.6 15.3 %collective-permute-start.3 = (f32[8,64,256]{2,1,0:T(8,128)S(1)}, f32[8,64,256]{2,1,0:T(8,128)S(1)}, u32[]{:S(2)}, u32[]{:S(2)}) collective-permute-start(f32[8,64,256]{2,1,0:T(8,128)S(1)} %get-tuple-element.73), channel_id=1, source_target_pairs={{0,2},{1,3},{2,0},{3,1},{4,6},{5,7},{6,4},{7,5},{8,10},{9,11},{10,... | collective-permute-start | bytes 1572872 | tf_op jit(solution)/shard_map/ppermute | solution.py:284
  29.2 16.8 %collective-permute-start.2 = (f32[8,64,256]{2,1,0:T(8,128)S(1)}, f32[8,64,256]{2,1,0:T(8,128)S(1)}, u32[]{:S(2)}, u32[]{:S(2)}) collective-permute-start(f32[8,64,256]{2,1,0:T(8,128)S(1)} %get-tuple-element.72), channel_id=1, source_target_pairs={{0,8},{1,9},{2,4},{3,5},{4,2},{5,3},{6,14},{7,15},{8,0},{9,1},{10,... | collective-permute-start | bytes 1572872 | tf_op jit(solution)/shard_map/ppermute | solution.py:284
  30.5 8.4 %collective-permute-start.9 = (f32[4,16,256]{2,1,0:T(8,128)S(1)}, f32[4,16,256]{2,1,0:T(8,128)S(1)}, u32[]{:S(2)}, u32[]{:S(2)}) collective-permute-start(f32[4,16,256]{2,1,0:T(8,128)S(1)} %pad_maximum_fusion.1), channel_id=1, source_target_pairs={{0,1},{1,0},{2,3},{3,2},{4,5},{5,4},{6,7},{7,6},{8,9},{9,8},{10,11... | collective-permute-start | bytes 196616 | tf_op jit(solution)/shard_map/ppermute | solution.py:284
  44.4 12.4 %collective-permute-start.11 = (f32[8,64,256]{2,1,0:T(8,128)S(1)}, f32[8,64,256]{2,1,0:T(8,128)S(1)}, u32[]{:S(2)}, u32[]{:S(2)}) collective-permute-start(f32[8,64,256]{2,1,0:T(8,128)S(1)} %get-tuple-element.93), channel_id=1, source_target_pairs={{0,2},{1,3},{2,0},{3,1},{4,6},{5,7},{6,4},{7,5},{8,10},{9,11},{10,... | collective-permute-start | bytes 1572872 | tf_op jit(solution)/shard_map/ppermute | solution.py:284
  47.6 12.8 %collective-permute-start.10 = (f32[8,64,256]{2,1,0:T(8,128)S(1)}, f32[8,64,256]{2,1,0:T(8,128)S(1)}, u32[]{:S(2)}, u32[]{:S(2)}) collective-permute-start(f32[8,64,256]{2,1,0:T(8,128)S(1)} %get-tuple-element.92), channel_id=1, source_target_pairs={{0,8},{1,9},{2,4},{3,5},{4,2},{5,3},{6,14},{7,15},{8,0},{9,1},{10,... | collective-permute-start | bytes 1572872 | tf_op jit(solution)/shard_map/ppermute | solution.py:284
  58.8 11.5 %collective-permute-start.13 = (f32[8,64,256]{2,1,0:T(8,128)S(1)}, f32[8,64,256]{2,1,0:T(8,128)S(1)}, u32[]{:S(2)}, u32[]{:S(2)}) collective-permute-start(f32[8,64,256]{2,1,0:T(8,128)S(1)} %get-tuple-element.102), channel_id=1, source_target_pairs={{0,2},{1,3},{2,0},{3,1},{4,6},{5,7},{6,4},{7,5},{8,10},{9,11},{10,... | collective-permute-start | bytes 1572872 | tf_op jit(solution)/shard_map/ppermute | solution.py:284
  62.3 11.4 %collective-permute-start.12 = (f32[8,64,256]{2,1,0:T(8,128)S(1)}, f32[8,64,256]{2,1,0:T(8,128)S(1)}, u32[]{:S(2)}, u32[]{:S(2)}) collective-permute-start(f32[8,64,256]{2,1,0:T(8,128)S(1)} %get-tuple-element.101), channel_id=1, source_target_pairs={{0,8},{1,9},{2,4},{3,5},{4,2},{5,3},{6,14},{7,15},{8,0},{9,1},{10,... | collective-permute-start | bytes 1572872 | tf_op jit(solution)/shard_map/ppermute | solution.py:284
  72.2 10.6 %collective-permute-start.15 = (f32[8,64,256]{2,1,0:T(8,128)S(1)}, f32[8,64,256]{2,1,0:T(8,128)S(1)}, u32[]{:S(2)}, u32[]{:S(2)}) collective-permute-start(f32[8,64,256]{2,1,0:T(8,128)S(1)} %get-tuple-element.110), channel_id=1, source_target_pairs={{0,2},{1,3},{2,0},{3,1},{4,6},{5,7},{6,4},{7,5},{8,10},{9,11},{10,... | collective-permute-start | bytes 1572872 | tf_op jit(solution)/shard_map/ppermute | solution.py:284
  75.7 10.7 %collective-permute-start.14 = (f32[8,64,256]{2,1,0:T(8,128)S(1)}, f32[8,64,256]{2,1,0:T(8,128)S(1)}, u32[]{:S(2)}, u32[]{:S(2)}) collective-permute-start(f32[8,64,256]{2,1,0:T(8,128)S(1)} %get-tuple-element.109), channel_id=1, source_target_pairs={{0,8},{1,9},{2,4},{3,5},{4,2},{5,3},{6,14},{7,15},{8,0},{9,1},{10,... | collective-permute-start | bytes 1572872 | tf_op jit(solution)/shard_map/ppermute | solution.py:284
  84.6 10.4 %collective-permute-start.17 = (f32[8,64,256]{2,1,0:T(8,128)S(1)}, f32[8,64,256]{2,1,0:T(8,128)S(1)}, u32[]{:S(2)}, u32[]{:S(2)}) collective-permute-start(f32[8,64,256]{2,1,0:T(8,128)S(1)} %get-tuple-element.118), channel_id=1, source_target_pairs={{0,2},{1,3},{2,0},{3,1},{4,6},{5,7},{6,4},{7,5},{8,10},{9,11},{10,... | collective-permute-start | bytes 1572872 | tf_op jit(solution)/shard_map/ppermute | solution.py:284
  88.4 10.1 %collective-permute-start.16 = (f32[8,64,256]{2,1,0:T(8,128)S(1)}, f32[8,64,256]{2,1,0:T(8,128)S(1)}, u32[]{:S(2)}, u32[]{:S(2)}) collective-permute-start(f32[8,64,256]{2,1,0:T(8,128)S(1)} %get-tuple-element.117), channel_id=1, source_target_pairs={{0,8},{1,9},{2,4},{3,5},{4,2},{5,3},{6,14},{7,15},{8,0},{9,1},{10,... | collective-permute-start | bytes 1572872 | tf_op jit(solution)/shard_map/ppermute | solution.py:284
  97.0 9.2 %collective-permute-start.19 = (f32[8,64,256]{2,1,0:T(8,128)S(1)}, f32[8,64,256]{2,1,0:T(8,128)S(1)}, u32[]{:S(2)}, u32[]{:S(2)}) collective-permute-start(f32[8,64,256]{2,1,0:T(8,128)S(1)} %get-tuple-element.126), channel_id=1, source_target_pairs={{0,2},{1,3},{2,0},{3,1},{4,6},{5,7},{6,4},{7,5},{8,10},{9,11},{10,... | collective-permute-start | bytes 1572872 | tf_op jit(solution)/shard_map/ppermute | solution.py:284
  100.5 9.2 %collective-permute-start.18 = (f32[8,64,256]{2,1,0:T(8,128)S(1)}, f32[8,64,256]{2,1,0:T(8,128)S(1)}, u32[]{:S(2)}, u32[]{:S(2)}) collective-permute-start(f32[8,64,256]{2,1,0:T(8,128)S(1)} %get-tuple-element.125), channel_id=1, source_target_pairs={{0,8},{1,9},{2,4},{3,5},{4,2},{5,3},{6,14},{7,15},{8,0},{9,1},{10,... | collective-permute-start | bytes 1572872 | tf_op jit(solution)/shard_map/ppermute | solution.py:284
  112.3 1.6 %collective-permute-start.20 = (f32[8,32,256]{2,1,0:T(8,128)S(1)}, f32[8,32,256]{2,1,0:T(8,128)S(1)}, u32[]{:S(2)}, u32[]{:S(2)}) collective-permute-start(f32[8,32,256]{2,1,0:T(8,128)S(1)} %give.1), channel_id=1, source_target_pairs={{0,8},{1,9},{2,10},{3,11},{4,12},{5,13},{6,14},{7,15},{8,0},{9,1},... | collective-permute-start | bytes 786440 | tf_op jit(solution)/shard_map/ppermute | solution.py:284
  114.5 5.6 %collective-permute-start.21 = (f32[8,16,256]{2,1,0:T(8,128)S(1)}, f32[8,16,256]{2,1,0:T(8,128)S(1)}, u32[]{:S(2)}, u32[]{:S(2)}) collective-permute-start(f32[8,16,256]{2,1,0:T(8,128)S(1)} %pair.1.late_ref), channel_id=1, source_target_pairs={{0,16},{1,17},{2,18},{3,19},{4,20},{5,21},{6,22},{7,23},{8,24},{9,... | collective-permute-start | bytes 393224 | tf_op jit(solution)/shard_map/ppermute | solution.py:284
  (2 other events, 17.0 us)

commit v8 on v7

--- a/solution.py
+++ b/solution.py
@@ -332,7 +332,7 @@
     y_edge = move(after(edge, early), swap_y)
     y_rest = move(after(rest, early), swap_y)
 
-    e, send_a, send_b = call(cur_kernel, [plane(32), plane(8), plane(8)], [scal, cur, after(y_cur, gathered)], free=(1,), name="field")
+    e, send_a, send_b = call(cur_kernel, [plane(32), plane(8), plane(8)], [scal, cur, y_cur], free=(1,), name="field")
     recv_a, recv_b = move(send_a, near_a), move(send_b, near_b)
     gathered = jnp.concatenate([gathered, move(after(gathered, recv_b), swap_y)], 0)
     edge_a, edge_b = call(edge_kernel, [plane(8), plane(8)], [scal, edge, y_edge], name="edges")

time: 121 us -> 121 us (level); the launches traced: 121 us -> 119 us
  waiting for transfers between devices: 56.2 us -> 47.8 us
  starting transfers between devices: 21.3 us -> 28 us
    ppermute x22, waiting for transfers between devices: 56.2 us -> 47.8 us  [move(): return lax.ppermute(x, ('shot', 'space'), pairs)]
    ppermute x22, starting transfers between devices: 21.3 us -> 28 us  [move(): return lax.ppermute(x, ('shot', 'space'), pairs)]
  transfers between devices with their start and end apart: 22 -> 22, of which waited for: 14 -> 15; matrix products, arithmetic and copies ran while one was open for 1% -> 1% of each run, Pallas kernels for 30% -> 30%
where the time goes in v8:
time: 121 us; the launch traced here: 119 us
  waiting for transfers between devices  47.8 us (40%)
  Pallas kernels  39.1 us (32%)
  starting transfers between devices  28 us (23%)
  other arithmetic  2.19 us (2%)
  between operations  1.59 us (1%)
    ppermute x22, waiting for transfers between devices, move(): return lax.ppermute(x, ('shot', 'space'), pairs)  47.8 us
    pallas_call x26, Pallas kernels, call(): pl.pallas_call(kernel, out_shape=out_shapes, in_specs=specs, out_specs=ja...  37.4 us
    ppermute x22, starting transfers between devices, move(): return lax.ppermute(x, ('shot', 'space'), pairs)  28 us
  transfers between devices with their start and end apart: 22, of which 15 were waited for; matrix products, arithmetic and copies ran while one was open for 1% of the time, Pallas kernels for 30%

profile of v8, /device:TPU:16, one launch (start us, length us, event | category | flops | bytes accessed | tf_op | source)
XLA Modules:
  0.0 118.9 jit_solution(13012518351145248446)
XLA Ops:
  8.7 7.0 %collective-permute-done.4.other = f32[8,64,256]{2,1,0:T(8,128)S(1)} collective-permute-done((f32[8,64,256]{2,1,0:T(8,128)}, f32[8,64,256]{2,1,0:T(8,128)S(1)}, u32[]{:S(2)}, u32[]{:S(2)}) %collective-permute-start.4) | collective-permute-done | bytes 524320 | tf_op jit(solution)/shard_map/ppermute | solution.py:284
  16.4 2.4 %collective-permute-start.6 = (f32[8,64,256]{2,1,0:T(8,128)S(1)}, f32[8,64,256]{2,1,0:T(8,128)S(1)}, u32[]{:S(2)}, u32[]{:S(2)}) collective-permute-start(f32[8,64,256]{2,1,0:T(8,128)S(1)} %get-tuple-element.74), channel_id=1, source_target_pairs={{2,4},{3,5},{4,2},{5,3},{10,12},{11,13},{12,10},{13,11},{18,20},{1... | collective-permute-start | bytes 1572872 | tf_op jit(solution)/shard_map/ppermute | solution.py:284
  20.4 3.0 %collective-permute-start.5 = (f32[8,64,256]{2,1,0:T(8,128)S(1)}, f32[8,64,256]{2,1,0:T(8,128)S(1)}, u32[]{:S(2)}, u32[]{:S(2)}) collective-permute-start(f32[8,64,256]{2,1,0:T(8,128)S(1)} %get-tuple-element.73), channel_id=1, source_target_pairs={{0,2},{1,3},{2,0},{3,1},{4,6},{5,7},{6,4},{7,5},{8,10},{9,11},{10,... | collective-permute-start | bytes 1572872 | tf_op jit(solution)/shard_map/ppermute | solution.py:284
  23.4 3.5 %collective-permute-done.1.other.edge = f32[8,64,256]{2,1,0:T(8,128)S(1)} collective-permute-done((f32[8,64,256]{2,1,0:T(8,128)S(1)}, f32[8,64,256]{2,1,0:T(8,128)S(1)}, u32[]{:S(2)}, u32[]{:S(2)}) %collective-permute-start.1) | collective-permute-done | bytes 524320 | tf_op jit(solution)/shard_map/ppermute | solution.py:284
  30.3 2.5 %collective-permute-start.2 = (f32[8,64,256]{2,1,0:T(8,128)S(1)}, f32[8,64,256]{2,1,0:T(8,128)S(1)}, u32[]{:S(2)}, u32[]{:S(2)}) collective-permute-start(f32[8,64,256]{2,1,0:T(8,128)S(1)} %get-tuple-element.71), channel_id=1, source_target_pairs={{0,8},{1,9},{2,4},{3,5},{4,2},{5,3},{6,14},{7,15},{8,0},{9,1},{10,... | collective-permute-start | bytes 1572872 | tf_op jit(solution)/shard_map/ppermute | solution.py:284
  34.4 3.3 %collective-permute-done.7.rest = f32[8,64,256]{2,1,0:T(8,128)S(1)} collective-permute-done((f32[8,64,256]{2,1,0:T(8,128)S(1)}, f32[8,64,256]{2,1,0:T(8,128)S(1)}, u32[]{:S(2)}, u32[]{:S(2)}) %collective-permute-start.7) | collective-permute-done | bytes 524320 | tf_op jit(solution)/shard_map/ppermute | solution.py:284
  38.9 2.1 %receivers.1.q_ref = f32[3,64,128]{2,1,0:T(8,128)S(1)} custom-call(s32[7]{0:T(128)S(1)} %stack.31.scal_ref, f32[8,16,256]{2,1,0:T(8,128)S(1)} %pad_maximum_fusion.gathered_ref), custom_call_target="tpu_custom_call" | custom-call | bytes 1048576 | tf_op jit(solution)/shard_map/receivers/pallas_call | solution.py:257
  51.3 5.9 %collective-permute-done.11.recv_ref = f32[8,64,256]{2,1,0:T(8,128)S(1)} collective-permute-done((f32[8,64,256]{2,1,0:T(8,128)S(1)}, f32[8,64,256]{2,1,0:T(8,128)S(1)}, u32[]{:S(2)}, u32[]{:S(2)}) %collective-permute-start.11) | collective-permute-done | bytes 524320 | tf_op jit(solution)/shard_map/ppermute | solution.py:284
  57.2 1.9 %side_a1.1 = (f32[32,64,256]{2,1,0:T(8,128)S(1)}, f32[24,64,256]{2,1,0:T(8,128)S(1)}, f32[8,64,256]{2,1,0:T(8,128)S(1)}) custom-call(s32[7]{0:T(128)S(1)} %stack.31.scal_ref, f32[8,64,256]{2,1,0:T(8,128)S(1)} %collective-permute-done.11.recv_ref, f32[32,64,256]{2,1,0:T(8,128)S(1)} %get-tuple-element.92.e_ref.e_in, ...), custom_call_target="tpu_custom_call", output_to_operand_aliasing={{0}: (2, {}), {1}: (3, {})} | custom-call | flops 31457280 | bytes 1048576 | tf_op jit(solution)/shard_map/side_a1/pallas_call | solution.py:257
  60.9 1.9 %side_b1.1 = (f32[32,64,256]{2,1,0:T(8,128)S(1)}, f32[24,64,256]{2,1,0:T(8,128)S(1)}, f32[8,64,256]{2,1,0:T(8,128)S(1)}) custom-call(s32[7]{0:T(128)S(1)} %stack.31.scal_ref, f32[8,64,256]{2,1,0:T(8,128)S(1)} %collective-permute-done.10.recv_ref, f32[32,64,256]{2,1,0:T(8,128)S(1)} %get-tuple-element.97.e_in, ...), custom_call_target="tpu_custom_call", output_to_operand_aliasing={{0}: (2, {}), {1}: (3, {})} | custom-call | flops 31457280 | bytes 1048576 | tf_op jit(solution)/shard_map/side_b1/pallas_call | solution.py:257
  64.3 5.1 %collective-permute-done.13.recv_ref = f32[8,64,256]{2,1,0:T(8,128)S(1)} collective-permute-done((f32[8,64,256]{2,1,0:T(8,128)S(1)}, f32[8,64,256]{2,1,0:T(8,128)S(1)}, u32[]{:S(2)}, u32[]{:S(2)}) %collective-permute-start.13) | collective-permute-done | bytes 524320 | tf_op jit(solution)/shard_map/ppermute | solution.py:284
  69.4 1.9 %side_a2.1 = (f32[32,64,256]{2,1,0:T(8,128)S(1)}, f32[24,64,256]{2,1,0:T(8,128)S(1)}, f32[8,64,256]{2,1,0:T(8,128)S(1)}) custom-call(s32[7]{0:T(128)S(1)} %stack.31.scal_ref, f32[8,64,256]{2,1,0:T(8,128)S(1)} %collective-permute-done.13.recv_ref, f32[32,64,256]{2,1,0:T(8,128)S(1)} %get-tuple-element.101.e_ref.e_in, ...), custom_call_target="tpu_custom_call", output_to_operand_aliasing={{0}: (2, {}), {1}: (3, {})} | custom-call | flops 31457280 | bytes 1048576 | tf_op jit(solution)/shard_map/side_a2/pallas_call | solution.py:257
  73.1 2.0 %side_b2.1 = (f32[32,64,256]{2,1,0:T(8,128)S(1)}, f32[24,64,256]{2,1,0:T(8,128)S(1)}, f32[8,64,256]{2,1,0:T(8,128)S(1)}) custom-call(s32[7]{0:T(128)S(1)} %stack.31.scal_ref, f32[8,64,256]{2,1,0:T(8,128)S(1)} %collective-permute-done.12.recv_ref, f32[32,64,256]{2,1,0:T(8,128)S(1)} %get-tuple-element.105.e_in, ...), custom_call_target="tpu_custom_call", output_to_operand_aliasing={{0}: (2, {}), {1}: (3, {})} | custom-call | flops 31457280 | bytes 1048576 | tf_op jit(solution)/shard_map/side_b2/pallas_call | solution.py:257
  76.6 4.4 %collective-permute-done.15.recv_ref = f32[8,64,256]{2,1,0:T(8,128)S(1)} collective-permute-done((f32[8,64,256]{2,1,0:T(8,128)S(1)}, f32[8,64,256]{2,1,0:T(8,128)S(1)}, u32[]{:S(2)}, u32[]{:S(2)}) %collective-permute-start.15) | collective-permute-done | bytes 524320 | tf_op jit(solution)/shard_map/ppermute | solution.py:284
  81.0 1.9 %side_a3.1 = (f32[32,64,256]{2,1,0:T(8,128)S(1)}, f32[24,64,256]{2,1,0:T(8,128)S(1)}, f32[8,64,256]{2,1,0:T(8,128)S(1)}) custom-call(s32[7]{0:T(128)S(1)} %stack.31.scal_ref, f32[8,64,256]{2,1,0:T(8,128)S(1)} %collective-permute-done.15.recv_ref, f32[32,64,256]{2,1,0:T(8,128)S(1)} %get-tuple-element.109.e_ref.e_in, ...), custom_call_target="tpu_custom_call", output_to_operand_aliasing={{0}: (2, {}), {1}: (3, {})} | custom-call | flops 31457280 | bytes 1048576 | tf_op jit(solution)/shard_map/side_a3/pallas_call | solution.py:257
  82.9 2.0 %collective-permute-start.17 = (f32[8,64,256]{2,1,0:T(8,128)S(1)}, f32[8,64,256]{2,1,0:T(8,128)S(1)}, u32[]{:S(2)}, u32[]{:S(2)}) collective-permute-start(f32[8,64,256]{2,1,0:T(8,128)S(1)} %get-tuple-element.116), channel_id=1, source_target_pairs={{0,2},{1,3},{2,0},{3,1},{4,6},{5,7},{6,4},{7,5},{8,10},{9,11},{10,... | collective-permute-start | bytes 1572872 | tf_op jit(solution)/shard_map/ppermute | solution.py:284
  84.9 2.0 %side_b3.1 = (f32[32,64,256]{2,1,0:T(8,128)S(1)}, f32[24,64,256]{2,1,0:T(8,128)S(1)}, f32[8,64,256]{2,1,0:T(8,128)S(1)}) custom-call(s32[7]{0:T(128)S(1)} %stack.31.scal_ref, f32[8,64,256]{2,1,0:T(8,128)S(1)} %collective-permute-done.14.recv_ref, f32[32,64,256]{2,1,0:T(8,128)S(1)} %get-tuple-element.113.e_in, ...), custom_call_target="tpu_custom_call", output_to_operand_aliasing={{0}: (2, {}), {1}: (3, {})} | custom-call | flops 31457280 | bytes 1048576 | tf_op jit(solution)/shard_map/side_b3/pallas_call | solution.py:257
  88.3 4.4 %collective-permute-done.17.recv_ref = f32[8,64,256]{2,1,0:T(8,128)S(1)} collective-permute-done((f32[8,64,256]{2,1,0:T(8,128)S(1)}, f32[8,64,256]{2,1,0:T(8,128)S(1)}, u32[]{:S(2)}, u32[]{:S(2)}) %collective-permute-start.17) | collective-permute-done | bytes 524320 | tf_op jit(solution)/shard_map/ppermute | solution.py:284
  92.7 1.9 %side_a4.1 = (f32[32,64,256]{2,1,0:T(8,128)S(1)}, f32[24,64,256]{2,1,0:T(8,128)S(1)}, f32[8,64,256]{2,1,0:T(8,128)S(1)}) custom-call(s32[7]{0:T(128)S(1)} %stack.31.scal_ref, f32[8,64,256]{2,1,0:T(8,128)S(1)} %collective-permute-done.17.recv_ref, f32[32,64,256]{2,1,0:T(8,128)S(1)} %get-tuple-element.117.e_ref.e_in, ...), custom_call_target="tpu_custom_call", output_to_operand_aliasing={{0}: (2, {}), {1}: (3, {})} | custom-call | flops 31457280 | bytes 1048576 | tf_op jit(solution)/shard_map/side_a4/pallas_call | solution.py:257
  96.7 2.0 %side_b4.1 = (f32[32,64,256]{2,1,0:T(8,128)S(1)}, f32[24,64,256]{2,1,0:T(8,128)S(1)}, f32[8,64,256]{2,1,0:T(8,128)S(1)}) custom-call(s32[7]{0:T(128)S(1)} %stack.31.scal_ref, f32[8,64,256]{2,1,0:T(8,128)S(1)} %collective-permute-done.16.recv_ref, f32[32,64,256]{2,1,0:T(8,128)S(1)} %get-tuple-element.121.e_in, ...), custom_call_target="tpu_custom_call", output_to_operand_aliasing={{0}: (2, {}), {1}: (3, {})} | custom-call | flops 31457280 | bytes 1048576 | tf_op jit(solution)/shard_map/side_b4/pallas_call | solution.py:257
  100.1 3.7 %collective-permute-done.19.recv_ref = f32[8,64,256]{2,1,0:T(8,128)S(1)} collective-permute-done((f32[8,64,256]{2,1,0:T(8,128)S(1)}, f32[8,64,256]{2,1,0:T(8,128)S(1)}, u32[]{:S(2)}, u32[]{:S(2)}) %collective-permute-start.19) | collective-permute-done | bytes 524320 | tf_op jit(solution)/shard_map/ppermute | solution.py:284
  104.4 3.5 %collective-permute-done.18.recv_ref = f32[8,64,256]{2,1,0:T(8,128)S(1)} collective-permute-done((f32[8,64,256]{2,1,0:T(8,128)S(1)}, f32[8,64,256]{2,1,0:T(8,128)S(1)}, u32[]{:S(2)}, u32[]{:S(2)}) %collective-permute-start.18) | collective-permute-done | bytes 524320 | tf_op jit(solution)/shard_map/ppermute | solution.py:284
  107.9 2.0 %side_b5.1 = (f32[32,64,256]{2,1,0:T(8,128)S(1)}, f32[24,64,256]{2,1,0:T(8,128)S(1)}) custom-call(s32[7]{0:T(128)S(1)} %stack.31.scal_ref, f32[8,64,256]{2,1,0:T(8,128)S(1)} %collective-permute-done.18.recv_ref, f32[32,64,256]{2,1,0:T(8,128)S(1)} %get-tuple-element.129.e_in, ...), custom_call_target="tpu_custom_call", output_to_operand_aliasing={{0}: (2, {}), {1}: (3, {})} | custom-call | flops 31457280 | bytes 1048576 | tf_op jit(solution)/shard_map/side_b5/pallas_call | solution.py:257
  115.6 2.7 %collective-permute-done.21 = f32[8,16,256]{2,1,0:T(8,128)S(1)} collective-permute-done((f32[8,16,256]{2,1,0:T(8,128)S(1)}, f32[8,16,256]{2,1,0:T(8,128)S(1)}, u32[]{:S(2)}, u32[]{:S(2)}) %collective-permute-start.21) | collective-permute-done | bytes 131104 | tf_op jit(solution)/shard_map/ppermute | solution.py:284
  (67 shorter events, 44.5 us)
Async XLA Ops:
  0.6 15.1 %collective-permute-start.4 = (f32[8,64,256]{2,1,0:T(8,128)}, f32[8,64,256]{2,1,0:T(8,128)S(1)}, u32[]{:S(2)}, u32[]{:S(2)}) collective-permute-start(f32[8,64,256]{2,1,0:T(8,128)} %bitcast.30), channel_id=1, source_target_pairs={{0,1},{1,0},{2,3},{3,2},{4,5},{5,4},{6,7},{7,6},{8,9},{9,8},{10,11... | collective-permute-start | bytes 1572872 | tf_op jit(solution)/shard_map/ppermute | solution.py:284
  4.5 3.7 %collective-permute-start = (f32[1,16,256]{2,1,0:T(8,128)S(1)}, f32[1,16,256]{2,1,0:T(8,128)S(1)}, u32[]{:S(2)}, u32[]{:S(2)}) collective-permute-start(f32[1,16,256]{2,1,0:T(8,128)S(1)} %maximum_bitcast_fusion), channel_id=1, source_target_pairs={{0,2},{1,3},{2,0},{3,1},{4,6},{5,7},{6,4},{7,5},{8,10},{9,11},{10,... | collective-permute-start | bytes 49160 | tf_op jit(solution)/shard_map/ppermute | solution.py:284
  6.1 31.6 %copy-start.1 = (f32[1,8,64,256]{3,2,1,0:T(8,128)S(1)}, f32[1,8,64,256]{3,2,1,0:T(8,128)}, u32[]{:S(2)}) copy-start(f32[1,8,64,256]{3,2,1,0:T(8,128)} %param.13) | copy-start | bytes 1572868
  6.1 31.6 %copy-start.2 = (f32[8,64,256]{2,1,0:T(8,128)S(1)}, f32[8,64,256]{2,1,0:T(8,128)}, u32[]{:S(2)}) copy-start(f32[8,64,256]{2,1,0:T(8,128)} %c_own.1) | copy-start | bytes 1572868
  8.2 18.8 %collective-permute-start.1 = (f32[8,64,256]{2,1,0:T(8,128)S(1)}, f32[8,64,256]{2,1,0:T(8,128)S(1)}, u32[]{:S(2)}, u32[]{:S(2)}) collective-permute-start(f32[8,64,256]{2,1,0:T(8,128)S(1)} %get-tuple-element.70.own), channel_id=1, source_target_pairs={{0,1},{1,0},{2,3},{3,2},{4,5},{5,4},{6,7},{7,6},{8,9},{9,8},{10,11... | collective-permute-start | bytes 1572872 | tf_op jit(solution)/shard_map/ppermute | solution.py:284
  16.4 16.4 %collective-permute-start.6 = (f32[8,64,256]{2,1,0:T(8,128)S(1)}, f32[8,64,256]{2,1,0:T(8,128)S(1)}, u32[]{:S(2)}, u32[]{:S(2)}) collective-permute-start(f32[8,64,256]{2,1,0:T(8,128)S(1)} %get-tuple-element.74), channel_id=1, source_target_pairs={{2,4},{3,5},{4,2},{5,3},{10,12},{11,13},{12,10},{13,11},{18,20},{1... | collective-permute-start | bytes 1572872 | tf_op jit(solution)/shard_map/ppermute | solution.py:284
  18.8 19.0 %collective-permute-start.7 = (f32[8,64,256]{2,1,0:T(8,128)S(1)}, f32[8,64,256]{2,1,0:T(8,128)S(1)}, u32[]{:S(2)}, u32[]{:S(2)}) collective-permute-start(f32[8,64,256]{2,1,0:T(8,128)S(1)} %get-tuple-element.77), channel_id=1, source_target_pairs={{0,1},{1,0},{2,3},{3,2},{4,5},{5,4},{6,7},{7,6},{8,9},{9,8},{10,11... | collective-permute-start | bytes 1572872 | tf_op jit(solution)/shard_map/ppermute | solution.py:284
  20.4 10.0 %collective-permute-start.8 = (f32[2,16,256]{2,1,0:T(8,128)S(1)}, f32[2,16,256]{2,1,0:T(8,128)S(1)}, u32[]{:S(2)}, u32[]{:S(2)}) collective-permute-start(f32[2,16,256]{2,1,0:T(8,128)S(1)} %pad_maximum_fusion.2), channel_id=1, source_target_pairs={{0,4},{1,5},{2,6},{3,7},{4,0},{5,1},{6,2},{7,3},{8,12},{9,13},{10,... | collective-permute-start | bytes 98312 | tf_op jit(solution)/shard_map/ppermute | solution.py:284
  20.4 20.6 %collective-permute-start.5 = (f32[8,64,256]{2,1,0:T(8,128)S(1)}, f32[8,64,256]{2,1,0:T(8,128)S(1)}, u32[]{:S(2)}, u32[]{:S(2)}) collective-permute-start(f32[8,64,256]{2,1,0:T(8,128)S(1)} %get-tuple-element.73), channel_id=1, source_target_pairs={{0,2},{1,3},{2,0},{3,1},{4,6},{5,7},{6,4},{7,5},{8,10},{9,11},{10,... | collective-permute-start | bytes 1572872 | tf_op jit(solution)/shard_map/ppermute | solution.py:284
  27.6 16.8 %collective-permute-start.3 = (f32[8,64,256]{2,1,0:T(8,128)S(1)}, f32[8,64,256]{2,1,0:T(8,128)S(1)}, u32[]{:S(2)}, u32[]{:S(2)}) collective-permute-start(f32[8,64,256]{2,1,0:T(8,128)S(1)} %get-tuple-element.72), channel_id=1, source_target_pairs={{0,2},{1,3},{2,0},{3,1},{4,6},{5,7},{6,4},{7,5},{8,10},{9,11},{10,... | collective-permute-start | bytes 1572872 | tf_op jit(solution)/shard_map/ppermute | solution.py:284
  30.3 17.4 %collective-permute-start.2 = (f32[8,64,256]{2,1,0:T(8,128)S(1)}, f32[8,64,256]{2,1,0:T(8,128)S(1)}, u32[]{:S(2)}, u32[]{:S(2)}) collective-permute-start(f32[8,64,256]{2,1,0:T(8,128)S(1)} %get-tuple-element.71), channel_id=1, source_target_pairs={{0,8},{1,9},{2,4},{3,5},{4,2},{5,3},{6,14},{7,15},{8,0},{9,1},{10,... | collective-permute-start | bytes 1572872 | tf_op jit(solution)/shard_map/ppermute | solution.py:284
  32.8 6.0 %collective-permute-start.9 = (f32[4,16,256]{2,1,0:T(8,128)S(1)}, f32[4,16,256]{2,1,0:T(8,128)S(1)}, u32[]{:S(2)}, u32[]{:S(2)}) collective-permute-start(f32[4,16,256]{2,1,0:T(8,128)S(1)} %pad_maximum_fusion.1), channel_id=1, source_target_pairs={{0,1},{1,0},{2,3},{3,2},{4,5},{5,4},{6,7},{7,6},{8,9},{9,8},{10,11... | collective-permute-start | bytes 196616 | tf_op jit(solution)/shard_map/ppermute | solution.py:284
  46.0 11.2 %collective-permute-start.11 = (f32[8,64,256]{2,1,0:T(8,128)S(1)}, f32[8,64,256]{2,1,0:T(8,128)S(1)}, u32[]{:S(2)}, u32[]{:S(2)}) collective-permute-start(f32[8,64,256]{2,1,0:T(8,128)S(1)} %get-tuple-element.91), channel_id=1, source_target_pairs={{0,2},{1,3},{2,0},{3,1},{4,6},{5,7},{6,4},{7,5},{8,10},{9,11},{10,... | collective-permute-start | bytes 1572872 | tf_op jit(solution)/shard_map/ppermute | solution.py:284
  49.3 11.6 %collective-permute-start.10 = (f32[8,64,256]{2,1,0:T(8,128)S(1)}, f32[8,64,256]{2,1,0:T(8,128)S(1)}, u32[]{:S(2)}, u32[]{:S(2)}) collective-permute-start(f32[8,64,256]{2,1,0:T(8,128)S(1)} %get-tuple-element.90), channel_id=1, source_target_pairs={{0,8},{1,9},{2,4},{3,5},{4,2},{5,3},{6,14},{7,15},{8,0},{9,1},{10,... | collective-permute-start | bytes 1572872 | tf_op jit(solution)/shard_map/ppermute | solution.py:284
  59.1 10.3 %collective-permute-start.13 = (f32[8,64,256]{2,1,0:T(8,128)S(1)}, f32[8,64,256]{2,1,0:T(8,128)S(1)}, u32[]{:S(2)}, u32[]{:S(2)}) collective-permute-start(f32[8,64,256]{2,1,0:T(8,128)S(1)} %get-tuple-element.100), channel_id=1, source_target_pairs={{0,2},{1,3},{2,0},{3,1},{4,6},{5,7},{6,4},{7,5},{8,10},{9,11},{10,... | collective-permute-start | bytes 1572872 | tf_op jit(solution)/shard_map/ppermute | solution.py:284
  62.9 10.3 %collective-permute-start.12 = (f32[8,64,256]{2,1,0:T(8,128)S(1)}, f32[8,64,256]{2,1,0:T(8,128)S(1)}, u32[]{:S(2)}, u32[]{:S(2)}) collective-permute-start(f32[8,64,256]{2,1,0:T(8,128)S(1)} %get-tuple-element.99), channel_id=1, source_target_pairs={{0,8},{1,9},{2,4},{3,5},{4,2},{5,3},{6,14},{7,15},{8,0},{9,1},{10,... | collective-permute-start | bytes 1572872 | tf_op jit(solution)/shard_map/ppermute | solution.py:284
  71.3 9.7 %collective-permute-start.15 = (f32[8,64,256]{2,1,0:T(8,128)S(1)}, f32[8,64,256]{2,1,0:T(8,128)S(1)}, u32[]{:S(2)}, u32[]{:S(2)}) collective-permute-start(f32[8,64,256]{2,1,0:T(8,128)S(1)} %get-tuple-element.108), channel_id=1, source_target_pairs={{0,2},{1,3},{2,0},{3,1},{4,6},{5,7},{6,4},{7,5},{8,10},{9,11},{10,... | collective-permute-start | bytes 1572872 | tf_op jit(solution)/shard_map/ppermute | solution.py:284
  75.1 9.8 %collective-permute-start.14 = (f32[8,64,256]{2,1,0:T(8,128)S(1)}, f32[8,64,256]{2,1,0:T(8,128)S(1)}, u32[]{:S(2)}, u32[]{:S(2)}) collective-permute-start(f32[8,64,256]{2,1,0:T(8,128)S(1)} %get-tuple-element.107), channel_id=1, source_target_pairs={{0,8},{1,9},{2,4},{3,5},{4,2},{5,3},{6,14},{7,15},{8,0},{9,1},{10,... | collective-permute-start | bytes 1572872 | tf_op jit(solution)/shard_map/ppermute | solution.py:284
  82.9 9.8 %collective-permute-start.17 = (f32[8,64,256]{2,1,0:T(8,128)S(1)}, f32[8,64,256]{2,1,0:T(8,128)S(1)}, u32[]{:S(2)}, u32[]{:S(2)}) collective-permute-start(f32[8,64,256]{2,1,0:T(8,128)S(1)} %get-tuple-element.116), channel_id=1, source_target_pairs={{0,2},{1,3},{2,0},{3,1},{4,6},{5,7},{6,4},{7,5},{8,10},{9,11},{10,... | collective-permute-start | bytes 1572872 | tf_op jit(solution)/shard_map/ppermute | solution.py:284
  86.9 9.8 %collective-permute-start.16 = (f32[8,64,256]{2,1,0:T(8,128)S(1)}, f32[8,64,256]{2,1,0:T(8,128)S(1)}, u32[]{:S(2)}, u32[]{:S(2)}) collective-permute-start(f32[8,64,256]{2,1,0:T(8,128)S(1)} %get-tuple-element.115), channel_id=1, source_target_pairs={{0,8},{1,9},{2,4},{3,5},{4,2},{5,3},{6,14},{7,15},{8,0},{9,1},{10,... | collective-permute-start | bytes 1572872 | tf_op jit(solution)/shard_map/ppermute | solution.py:284
  94.6 9.2 %collective-permute-start.19 = (f32[8,64,256]{2,1,0:T(8,128)S(1)}, f32[8,64,256]{2,1,0:T(8,128)S(1)}, u32[]{:S(2)}, u32[]{:S(2)}) collective-permute-start(f32[8,64,256]{2,1,0:T(8,128)S(1)} %get-tuple-element.124), channel_id=1, source_target_pairs={{0,2},{1,3},{2,0},{3,1},{4,6},{5,7},{6,4},{7,5},{8,10},{9,11},{10,... | collective-permute-start | bytes 1572872 | tf_op jit(solution)/shard_map/ppermute | solution.py:284
  98.7 9.2 %collective-permute-start.18 = (f32[8,64,256]{2,1,0:T(8,128)S(1)}, f32[8,64,256]{2,1,0:T(8,128)S(1)}, u32[]{:S(2)}, u32[]{:S(2)}) collective-permute-start(f32[8,64,256]{2,1,0:T(8,128)S(1)} %get-tuple-element.123), channel_id=1, source_target_pairs={{0,8},{1,9},{2,4},{3,5},{4,2},{5,3},{6,14},{7,15},{8,0},{9,1},{10,... | collective-permute-start | bytes 1572872 | tf_op jit(solution)/shard_map/ppermute | solution.py:284
  110.5 1.6 %collective-permute-start.20 = (f32[8,32,256]{2,1,0:T(8,128)S(1)}, f32[8,32,256]{2,1,0:T(8,128)S(1)}, u32[]{:S(2)}, u32[]{:S(2)}) collective-permute-start(f32[8,32,256]{2,1,0:T(8,128)S(1)} %give.1), channel_id=1, source_target_pairs={{0,8},{1,9},{2,10},{3,11},{4,12},{5,13},{6,14},{7,15},{8,0},{9,1},... | collective-permute-start | bytes 786440 | tf_op jit(solution)/shard_map/ppermute | solution.py:284
  112.7 5.6 %collective-permute-start.21 = (f32[8,16,256]{2,1,0:T(8,128)S(1)}, f32[8,16,256]{2,1,0:T(8,128)S(1)}, u32[]{:S(2)}, u32[]{:S(2)}) collective-permute-start(f32[8,16,256]{2,1,0:T(8,128)S(1)} %pair.1.late_ref), channel_id=1, source_target_pairs={{0,16},{1,17},{2,18},{3,19},{4,20},{5,21},{6,22},{7,23},{8,24},{9,... | collective-permute-start | bytes 393224 | tf_op jit(solution)/shard_map/ppermute | solution.py:284
  (2 other events, 17.2 us)

commit v9 on v8

--- a/solution.py
+++ b/solution.py
@@ -230,6 +230,12 @@
                 + o_ref[j + 4, at] * f_ref[steps - 2, p, at].astype(F32)
                 + e_ref[j + 8, at] * f_ref[steps - 1, p, at].astype(F32)
             )
+
+
+def last_kernel(scal_ref, recv_ref, *refs, r, steps):
+    state, (f_ref, g_in, e_ref, o_ref, give_ref) = refs[:7], refs[7:]
+    side_kernel(scal_ref, recv_ref, *state, e_ref, o_ref, r=r, side="b", last=True)
+    share_kernel(scal_ref, e_ref, o_ref, f_ref, g_in, give_ref, steps=steps, give=True)
 
 
 def pair_kernel(scal_ref, keep_ref, recv_ref, give_ref):
@@ -378,6 +384,16 @@
         last = r == rounds - 1
         sent = []
         for side in "ab":
+            if last and side == "b":
+                e, o, give = call(
+                    functools.partial(last_kernel, r=r, steps=steps),
+                    [plane(32), plane(24), VM((length, ny // 2, nz), F32)],
+                    [scal, recv_b, e, o, a, c, q, wz, wy, forward, g],
+                    {2: 0, 3: 1},
+                    flops=work,
+                    name="last",
+                )
+                continue
             got = {"a": recv_a, "b": recv_b}[side] if r else {"a": edge_a, "b": edge_b}[side]
             kept = 2 if r else 4
             outs = [plane(32), plane(24), plane(24), plane(24)][:kept] + ([] if last else [plane(8)])
@@ -398,7 +414,6 @@
     part = ny // 4
     shares = [scal, e, o, forward, g]
     share = VM((length, 2 * part, nz), F32)
-    give = call(functools.partial(share_kernel, steps=steps, give=True), [share], shares, name="give")[0]
     recv = move(give, swap_core)
     keep = call(functools.partial(share_kernel, steps=steps, give=False), [share], shares, name="keep")[0]
     give = call(pair_kernel, [VM((length, part, nz), F32)], [scal, keep, recv], name="pair")[0]

time: 121 us -> 120 us (level)
    pallas_call x26 -> x25, Pallas kernels: 37.4 us -> 36.8 us  [call(): pl.pallas_call(kernel, out_shape=out_shapes, in_specs=specs, out_specs=ja...]
where the time goes in v9:
time: 120 us; the launch traced here: 118 us
  waiting for transfers between devices  47.8 us (40%)
  Pallas kernels  38.6 us (32%)
  starting transfers between devices  28 us (23%)
  other arithmetic  2.19 us (2%)
  between operations  1.58 us (1%)
    ppermute x22, waiting for transfers between devices, move(): return lax.ppermute(x, ('shot', 'space'), pairs)  47.8 us
    pallas_call x25, Pallas kernels, call(): pl.pallas_call(kernel, out_shape=out_shapes, in_specs=specs, out_specs=ja...  36.8 us
    ppermute x22, starting transfers between devices, move(): return lax.ppermute(x, ('shot', 'space'), pairs)  28 us
  transfers between devices with their start and end apart: 22, of which 15 were waited for; matrix products, arithmetic and copies ran while one was open for 1% of the time, Pallas kernels for 30%

profile of v9, /device:TPU:16, one launch (start us, length us, event | category | flops | bytes accessed | tf_op | source)
XLA Modules:
  0.0 118.4 jit_solution(14907631517695514944)
XLA Ops:
  8.7 7.0 %collective-permute-done.4.other = f32[8,64,256]{2,1,0:T(8,128)S(1)} collective-permute-done((f32[8,64,256]{2,1,0:T(8,128)}, f32[8,64,256]{2,1,0:T(8,128)S(1)}, u32[]{:S(2)}, u32[]{:S(2)}) %collective-permute-start.4) | collective-permute-done | bytes 524320 | tf_op jit(solution)/shard_map/ppermute | solution.py:290
  16.4 2.4 %collective-permute-start.6 = (f32[8,64,256]{2,1,0:T(8,128)S(1)}, f32[8,64,256]{2,1,0:T(8,128)S(1)}, u32[]{:S(2)}, u32[]{:S(2)}) collective-permute-start(f32[8,64,256]{2,1,0:T(8,128)S(1)} %get-tuple-element.75), channel_id=1, source_target_pairs={{2,4},{3,5},{4,2},{5,3},{10,12},{11,13},{12,10},{13,11},{18,20},{1... | collective-permute-start | bytes 1572872 | tf_op jit(solution)/shard_map/ppermute | solution.py:290
  20.4 3.0 %collective-permute-start.5 = (f32[8,64,256]{2,1,0:T(8,128)S(1)}, f32[8,64,256]{2,1,0:T(8,128)S(1)}, u32[]{:S(2)}, u32[]{:S(2)}) collective-permute-start(f32[8,64,256]{2,1,0:T(8,128)S(1)} %get-tuple-element.74), channel_id=1, source_target_pairs={{0,2},{1,3},{2,0},{3,1},{4,6},{5,7},{6,4},{7,5},{8,10},{9,11},{10,... | collective-permute-start | bytes 1572872 | tf_op jit(solution)/shard_map/ppermute | solution.py:290
  23.4 3.5 %collective-permute-done.1.other.edge = f32[8,64,256]{2,1,0:T(8,128)S(1)} collective-permute-done((f32[8,64,256]{2,1,0:T(8,128)S(1)}, f32[8,64,256]{2,1,0:T(8,128)S(1)}, u32[]{:S(2)}, u32[]{:S(2)}) %collective-permute-start.1) | collective-permute-done | bytes 524320 | tf_op jit(solution)/shard_map/ppermute | solution.py:290
  30.3 2.5 %collective-permute-start.2 = (f32[8,64,256]{2,1,0:T(8,128)S(1)}, f32[8,64,256]{2,1,0:T(8,128)S(1)}, u32[]{:S(2)}, u32[]{:S(2)}) collective-permute-start(f32[8,64,256]{2,1,0:T(8,128)S(1)} %get-tuple-element.72), channel_id=1, source_target_pairs={{0,8},{1,9},{2,4},{3,5},{4,2},{5,3},{6,14},{7,15},{8,0},{9,1},{10,... | collective-permute-start | bytes 1572872 | tf_op jit(solution)/shard_map/ppermute | solution.py:290
  34.4 3.3 %collective-permute-done.7.rest = f32[8,64,256]{2,1,0:T(8,128)S(1)} collective-permute-done((f32[8,64,256]{2,1,0:T(8,128)S(1)}, f32[8,64,256]{2,1,0:T(8,128)S(1)}, u32[]{:S(2)}, u32[]{:S(2)}) %collective-permute-start.7) | collective-permute-done | bytes 524320 | tf_op jit(solution)/shard_map/ppermute | solution.py:290
  38.9 2.1 %receivers.1.q_ref.refs_4_ = f32[3,64,128]{2,1,0:T(8,128)S(1)} custom-call(s32[7]{0:T(128)S(1)} %stack.31.scal_ref, f32[8,16,256]{2,1,0:T(8,128)S(1)} %pad_maximum_fusion.gathered_ref), custom_call_target="tpu_custom_call" | custom-call | bytes 1048576 | tf_op jit(solution)/shard_map/receivers/pallas_call | solution.py:263
  51.3 5.9 %collective-permute-done.11.recv_ref = f32[8,64,256]{2,1,0:T(8,128)S(1)} collective-permute-done((f32[8,64,256]{2,1,0:T(8,128)S(1)}, f32[8,64,256]{2,1,0:T(8,128)S(1)}, u32[]{:S(2)}, u32[]{:S(2)}) %collective-permute-start.11) | collective-permute-done | bytes 524320 | tf_op jit(solution)/shard_map/ppermute | solution.py:290
  57.2 1.9 %side_a1.1 = (f32[32,64,256]{2,1,0:T(8,128)S(1)}, f32[24,64,256]{2,1,0:T(8,128)S(1)}, f32[8,64,256]{2,1,0:T(8,128)S(1)}) custom-call(s32[7]{0:T(128)S(1)} %stack.31.scal_ref, f32[8,64,256]{2,1,0:T(8,128)S(1)} %collective-permute-done.11.recv_ref, f32[32,64,256]{2,1,0:T(8,128)S(1)} %get-tuple-element.93.e_ref.e_in, ...), custom_call_target="tpu_custom_call", output_to_operand_aliasing={{0}: (2, {}), {1}: (3, {})} | custom-call | flops 31457280 | bytes 1048576 | tf_op jit(solution)/shard_map/side_a1/pallas_call | solution.py:263
  60.9 1.9 %side_b1.1 = (f32[32,64,256]{2,1,0:T(8,128)S(1)}, f32[24,64,256]{2,1,0:T(8,128)S(1)}, f32[8,64,256]{2,1,0:T(8,128)S(1)}) custom-call(s32[7]{0:T(128)S(1)} %stack.31.scal_ref, f32[8,64,256]{2,1,0:T(8,128)S(1)} %collective-permute-done.10.recv_ref, f32[32,64,256]{2,1,0:T(8,128)S(1)} %get-tuple-element.98.e_in, ...), custom_call_target="tpu_custom_call", output_to_operand_aliasing={{0}: (2, {}), {1}: (3, {})} | custom-call | flops 31457280 | bytes 1048576 | tf_op jit(solution)/shard_map/side_b1/pallas_call | solution.py:263
  64.3 5.1 %collective-permute-done.13.recv_ref = f32[8,64,256]{2,1,0:T(8,128)S(1)} collective-permute-done((f32[8,64,256]{2,1,0:T(8,128)S(1)}, f32[8,64,256]{2,1,0:T(8,128)S(1)}, u32[]{:S(2)}, u32[]{:S(2)}) %collective-permute-start.13) | collective-permute-done | bytes 524320 | tf_op jit(solution)/shard_map/ppermute | solution.py:290
  69.4 1.9 %side_a2.1 = (f32[32,64,256]{2,1,0:T(8,128)S(1)}, f32[24,64,256]{2,1,0:T(8,128)S(1)}, f32[8,64,256]{2,1,0:T(8,128)S(1)}) custom-call(s32[7]{0:T(128)S(1)} %stack.31.scal_ref, f32[8,64,256]{2,1,0:T(8,128)S(1)} %collective-permute-done.13.recv_ref, f32[32,64,256]{2,1,0:T(8,128)S(1)} %get-tuple-element.102.e_ref.e_in, ...), custom_call_target="tpu_custom_call", output_to_operand_aliasing={{0}: (2, {}), {1}: (3, {})} | custom-call | flops 31457280 | bytes 1048576 | tf_op jit(solution)/shard_map/side_a2/pallas_call | solution.py:263
  73.1 2.0 %side_b2.1 = (f32[32,64,256]{2,1,0:T(8,128)S(1)}, f32[24,64,256]{2,1,0:T(8,128)S(1)}, f32[8,64,256]{2,1,0:T(8,128)S(1)}) custom-call(s32[7]{0:T(128)S(1)} %stack.31.scal_ref, f32[8,64,256]{2,1,0:T(8,128)S(1)} %collective-permute-done.12.recv_ref, f32[32,64,256]{2,1,0:T(8,128)S(1)} %get-tuple-element.106.e_in, ...), custom_call_target="tpu_custom_call", output_to_operand_aliasing={{0}: (2, {}), {1}: (3, {})} | custom-call | flops 31457280 | bytes 1048576 | tf_op jit(solution)/shard_map/side_b2/pallas_call | solution.py:263
  76.6 4.4 %collective-permute-done.15.recv_ref = f32[8,64,256]{2,1,0:T(8,128)S(1)} collective-permute-done((f32[8,64,256]{2,1,0:T(8,128)S(1)}, f32[8,64,256]{2,1,0:T(8,128)S(1)}, u32[]{:S(2)}, u32[]{:S(2)}) %collective-permute-start.15) | collective-permute-done | bytes 524320 | tf_op jit(solution)/shard_map/ppermute | solution.py:290
  81.0 1.9 %side_a3.1 = (f32[32,64,256]{2,1,0:T(8,128)S(1)}, f32[24,64,256]{2,1,0:T(8,128)S(1)}, f32[8,64,256]{2,1,0:T(8,128)S(1)}) custom-call(s32[7]{0:T(128)S(1)} %stack.31.scal_ref, f32[8,64,256]{2,1,0:T(8,128)S(1)} %collective-permute-done.15.recv_ref, f32[32,64,256]{2,1,0:T(8,128)S(1)} %get-tuple-element.110.e_ref.e_in, ...), custom_call_target="tpu_custom_call", output_to_operand_aliasing={{0}: (2, {}), {1}: (3, {})} | custom-call | flops 31457280 | bytes 1048576 | tf_op jit(solution)/shard_map/side_a3/pallas_call | solution.py:263
  82.9 2.0 %collective-permute-start.17 = (f32[8,64,256]{2,1,0:T(8,128)S(1)}, f32[8,64,256]{2,1,0:T(8,128)S(1)}, u32[]{:S(2)}, u32[]{:S(2)}) collective-permute-start(f32[8,64,256]{2,1,0:T(8,128)S(1)} %get-tuple-element.117), channel_id=1, source_target_pairs={{0,2},{1,3},{2,0},{3,1},{4,6},{5,7},{6,4},{7,5},{8,10},{9,11},{10,... | collective-permute-start | bytes 1572872 | tf_op jit(solution)/shard_map/ppermute | solution.py:290
  84.9 2.0 %side_b3.1 = (f32[32,64,256]{2,1,0:T(8,128)S(1)}, f32[24,64,256]{2,1,0:T(8,128)S(1)}, f32[8,64,256]{2,1,0:T(8,128)S(1)}) custom-call(s32[7]{0:T(128)S(1)} %stack.31.scal_ref, f32[8,64,256]{2,1,0:T(8,128)S(1)} %collective-permute-done.14.recv_ref, f32[32,64,256]{2,1,0:T(8,128)S(1)} %get-tuple-element.114.e_in, ...), custom_call_target="tpu_custom_call", output_to_operand_aliasing={{0}: (2, {}), {1}: (3, {})} | custom-call | flops 31457280 | bytes 1048576 | tf_op jit(solution)/shard_map/side_b3/pallas_call | solution.py:263
  88.3 4.4 %collective-permute-done.17.recv_ref = f32[8,64,256]{2,1,0:T(8,128)S(1)} collective-permute-done((f32[8,64,256]{2,1,0:T(8,128)S(1)}, f32[8,64,256]{2,1,0:T(8,128)S(1)}, u32[]{:S(2)}, u32[]{:S(2)}) %collective-permute-start.17) | collective-permute-done | bytes 524320 | tf_op jit(solution)/shard_map/ppermute | solution.py:290
  92.7 1.9 %side_a4.1 = (f32[32,64,256]{2,1,0:T(8,128)S(1)}, f32[24,64,256]{2,1,0:T(8,128)S(1)}, f32[8,64,256]{2,1,0:T(8,128)S(1)}) custom-call(s32[7]{0:T(128)S(1)} %stack.31.scal_ref, f32[8,64,256]{2,1,0:T(8,128)S(1)} %collective-permute-done.17.recv_ref, f32[32,64,256]{2,1,0:T(8,128)S(1)} %get-tuple-element.118.e_ref.e_in, ...), custom_call_target="tpu_custom_call", output_to_operand_aliasing={{0}: (2, {}), {1}: (3, {})} | custom-call | flops 31457280 | bytes 1048576 | tf_op jit(solution)/shard_map/side_a4/pallas_call | solution.py:263
  96.7 2.0 %side_b4.1 = (f32[32,64,256]{2,1,0:T(8,128)S(1)}, f32[24,64,256]{2,1,0:T(8,128)S(1)}, f32[8,64,256]{2,1,0:T(8,128)S(1)}) custom-call(s32[7]{0:T(128)S(1)} %stack.31.scal_ref, f32[8,64,256]{2,1,0:T(8,128)S(1)} %collective-permute-done.16.recv_ref, f32[32,64,256]{2,1,0:T(8,128)S(1)} %get-tuple-element.122.e_in, ...), custom_call_target="tpu_custom_call", output_to_operand_aliasing={{0}: (2, {}), {1}: (3, {})} | custom-call | flops 31457280 | bytes 1048576 | tf_op jit(solution)/shard_map/side_b4/pallas_call | solution.py:263
  100.1 3.7 %collective-permute-done.19.recv_ref = f32[8,64,256]{2,1,0:T(8,128)S(1)} collective-permute-done((f32[8,64,256]{2,1,0:T(8,128)S(1)}, f32[8,64,256]{2,1,0:T(8,128)S(1)}, u32[]{:S(2)}, u32[]{:S(2)}) %collective-permute-start.19) | collective-permute-done | bytes 524320 | tf_op jit(solution)/shard_map/ppermute | solution.py:290
  104.4 3.5 %collective-permute-done.18.recv_ref = f32[8,64,256]{2,1,0:T(8,128)S(1)} collective-permute-done((f32[8,64,256]{2,1,0:T(8,128)S(1)}, f32[8,64,256]{2,1,0:T(8,128)S(1)}, u32[]{:S(2)}, u32[]{:S(2)}) %collective-permute-start.18) | collective-permute-done | bytes 524320 | tf_op jit(solution)/shard_map/ppermute | solution.py:290
  107.9 2.0 %last.1 = (f32[32,64,256]{2,1,0:T(8,128)S(1)}, f32[24,64,256]{2,1,0:T(8,128)S(1)}, f32[8,32,256]{2,1,0:T(8,128)S(1)}) custom-call(s32[7]{0:T(128)S(1)} %stack.31.scal_ref, f32[8,64,256]{2,1,0:T(8,128)S(1)} %collective-permute-done.18.recv_ref, f32[32,64,256]{2,1,0:T(8,128)S(1)} %get-tuple-element.130.refs_0_, ...), custom_call_target="tpu_custom_call", output_to_operand_aliasing={{0}: (2, {}), {1}: (3, {})} | custom-call | flops 31457280 | bytes 1048576 | tf_op jit(solution)/shard_map/last/pallas_call | solution.py:263
  115.1 2.7 %collective-permute-done.21 = f32[8,16,256]{2,1,0:T(8,128)S(1)} collective-permute-done((f32[8,16,256]{2,1,0:T(8,128)S(1)}, f32[8,16,256]{2,1,0:T(8,128)S(1)}, u32[]{:S(2)}, u32[]{:S(2)}) %collective-permute-start.21) | collective-permute-done | bytes 131104 | tf_op jit(solution)/shard_map/ppermute | solution.py:290
  (66 shorter events, 43.9 us)
Async XLA Ops:
  0.6 15.1 %collective-permute-start.4 = (f32[8,64,256]{2,1,0:T(8,128)}, f32[8,64,256]{2,1,0:T(8,128)S(1)}, u32[]{:S(2)}, u32[]{:S(2)}) collective-permute-start(f32[8,64,256]{2,1,0:T(8,128)} %bitcast.30), channel_id=1, source_target_pairs={{0,1},{1,0},{2,3},{3,2},{4,5},{5,4},{6,7},{7,6},{8,9},{9,8},{10,11... | collective-permute-start | bytes 1572872 | tf_op jit(solution)/shard_map/ppermute | solution.py:290
  4.5 3.7 %collective-permute-start = (f32[1,16,256]{2,1,0:T(8,128)S(1)}, f32[1,16,256]{2,1,0:T(8,128)S(1)}, u32[]{:S(2)}, u32[]{:S(2)}) collective-permute-start(f32[1,16,256]{2,1,0:T(8,128)S(1)} %maximum_bitcast_fusion), channel_id=1, source_target_pairs={{0,2},{1,3},{2,0},{3,1},{4,6},{5,7},{6,4},{7,5},{8,10},{9,11},{10,... | collective-permute-start | bytes 49160 | tf_op jit(solution)/shard_map/ppermute | solution.py:290
  6.1 31.6 %copy-start.1 = (f32[1,8,64,256]{3,2,1,0:T(8,128)S(1)}, f32[1,8,64,256]{3,2,1,0:T(8,128)}, u32[]{:S(2)}) copy-start(f32[1,8,64,256]{3,2,1,0:T(8,128)} %param.13) | copy-start | bytes 1572868
  6.1 31.6 %copy-start.2 = (f32[8,64,256]{2,1,0:T(8,128)S(1)}, f32[8,64,256]{2,1,0:T(8,128)}, u32[]{:S(2)}) copy-start(f32[8,64,256]{2,1,0:T(8,128)} %c_own.1) | copy-start | bytes 1572868
  8.2 18.8 %collective-permute-start.1 = (f32[8,64,256]{2,1,0:T(8,128)S(1)}, f32[8,64,256]{2,1,0:T(8,128)S(1)}, u32[]{:S(2)}, u32[]{:S(2)}) collective-permute-start(f32[8,64,256]{2,1,0:T(8,128)S(1)} %get-tuple-element.71.own), channel_id=1, source_target_pairs={{0,1},{1,0},{2,3},{3,2},{4,5},{5,4},{6,7},{7,6},{8,9},{9,8},{10,11... | collective-permute-start | bytes 1572872 | tf_op jit(solution)/shard_map/ppermute | solution.py:290
  16.4 16.4 %collective-permute-start.6 = (f32[8,64,256]{2,1,0:T(8,128)S(1)}, f32[8,64,256]{2,1,0:T(8,128)S(1)}, u32[]{:S(2)}, u32[]{:S(2)}) collective-permute-start(f32[8,64,256]{2,1,0:T(8,128)S(1)} %get-tuple-element.75), channel_id=1, source_target_pairs={{2,4},{3,5},{4,2},{5,3},{10,12},{11,13},{12,10},{13,11},{18,20},{1... | collective-permute-start | bytes 1572872 | tf_op jit(solution)/shard_map/ppermute | solution.py:290
  18.8 19.0 %collective-permute-start.7 = (f32[8,64,256]{2,1,0:T(8,128)S(1)}, f32[8,64,256]{2,1,0:T(8,128)S(1)}, u32[]{:S(2)}, u32[]{:S(2)}) collective-permute-start(f32[8,64,256]{2,1,0:T(8,128)S(1)} %get-tuple-element.78), channel_id=1, source_target_pairs={{0,1},{1,0},{2,3},{3,2},{4,5},{5,4},{6,7},{7,6},{8,9},{9,8},{10,11... | collective-permute-start | bytes 1572872 | tf_op jit(solution)/shard_map/ppermute | solution.py:290
  20.4 10.0 %collective-permute-start.8 = (f32[2,16,256]{2,1,0:T(8,128)S(1)}, f32[2,16,256]{2,1,0:T(8,128)S(1)}, u32[]{:S(2)}, u32[]{:S(2)}) collective-permute-start(f32[2,16,256]{2,1,0:T(8,128)S(1)} %pad_maximum_fusion.2), channel_id=1, source_target_pairs={{0,4},{1,5},{2,6},{3,7},{4,0},{5,1},{6,2},{7,3},{8,12},{9,13},{10,... | collective-permute-start | bytes 98312 | tf_op jit(solution)/shard_map/ppermute | solution.py:290
  20.4 20.6 %collective-permute-start.5 = (f32[8,64,256]{2,1,0:T(8,128)S(1)}, f32[8,64,256]{2,1,0:T(8,128)S(1)}, u32[]{:S(2)}, u32[]{:S(2)}) collective-permute-start(f32[8,64,256]{2,1,0:T(8,128)S(1)} %get-tuple-element.74), channel_id=1, source_target_pairs={{0,2},{1,3},{2,0},{3,1},{4,6},{5,7},{6,4},{7,5},{8,10},{9,11},{10,... | collective-permute-start | bytes 1572872 | tf_op jit(solution)/shard_map/ppermute | solution.py:290
  27.6 16.8 %collective-permute-start.3 = (f32[8,64,256]{2,1,0:T(8,128)S(1)}, f32[8,64,256]{2,1,0:T(8,128)S(1)}, u32[]{:S(2)}, u32[]{:S(2)}) collective-permute-start(f32[8,64,256]{2,1,0:T(8,128)S(1)} %get-tuple-element.73), channel_id=1, source_target_pairs={{0,2},{1,3},{2,0},{3,1},{4,6},{5,7},{6,4},{7,5},{8,10},{9,11},{10,... | collective-permute-start | bytes 1572872 | tf_op jit(solution)/shard_map/ppermute | solution.py:290
  30.3 17.4 %collective-permute-start.2 = (f32[8,64,256]{2,1,0:T(8,128)S(1)}, f32[8,64,256]{2,1,0:T(8,128)S(1)}, u32[]{:S(2)}, u32[]{:S(2)}) collective-permute-start(f32[8,64,256]{2,1,0:T(8,128)S(1)} %get-tuple-element.72), channel_id=1, source_target_pairs={{0,8},{1,9},{2,4},{3,5},{4,2},{5,3},{6,14},{7,15},{8,0},{9,1},{10,... | collective-permute-start | bytes 1572872 | tf_op jit(solution)/shard_map/ppermute | solution.py:290
  32.8 6.0 %collective-permute-start.9 = (f32[4,16,256]{2,1,0:T(8,128)S(1)}, f32[4,16,256]{2,1,0:T(8,128)S(1)}, u32[]{:S(2)}, u32[]{:S(2)}) collective-permute-start(f32[4,16,256]{2,1,0:T(8,128)S(1)} %pad_maximum_fusion.1), channel_id=1, source_target_pairs={{0,1},{1,0},{2,3},{3,2},{4,5},{5,4},{6,7},{7,6},{8,9},{9,8},{10,11... | collective-permute-start | bytes 196616 | tf_op jit(solution)/shard_map/ppermute | solution.py:290
  46.0 11.2 %collective-permute-start.11 = (f32[8,64,256]{2,1,0:T(8,128)S(1)}, f32[8,64,256]{2,1,0:T(8,128)S(1)}, u32[]{:S(2)}, u32[]{:S(2)}) collective-permute-start(f32[8,64,256]{2,1,0:T(8,128)S(1)} %get-tuple-element.92), channel_id=1, source_target_pairs={{0,2},{1,3},{2,0},{3,1},{4,6},{5,7},{6,4},{7,5},{8,10},{9,11},{10,... | collective-permute-start | bytes 1572872 | tf_op jit(solution)/shard_map/ppermute | solution.py:290
  49.3 11.6 %collective-permute-start.10 = (f32[8,64,256]{2,1,0:T(8,128)S(1)}, f32[8,64,256]{2,1,0:T(8,128)S(1)}, u32[]{:S(2)}, u32[]{:S(2)}) collective-permute-start(f32[8,64,256]{2,1,0:T(8,128)S(1)} %get-tuple-element.91), channel_id=1, source_target_pairs={{0,8},{1,9},{2,4},{3,5},{4,2},{5,3},{6,14},{7,15},{8,0},{9,1},{10,... | collective-permute-start | bytes 1572872 | tf_op jit(solution)/shard_map/ppermute | solution.py:290
  59.1 10.3 %collective-permute-start.13 = (f32[8,64,256]{2,1,0:T(8,128)S(1)}, f32[8,64,256]{2,1,0:T(8,128)S(1)}, u32[]{:S(2)}, u32[]{:S(2)}) collective-permute-start(f32[8,64,256]{2,1,0:T(8,128)S(1)} %get-tuple-element.101), channel_id=1, source_target_pairs={{0,2},{1,3},{2,0},{3,1},{4,6},{5,7},{6,4},{7,5},{8,10},{9,11},{10,... | collective-permute-start | bytes 1572872 | tf_op jit(solution)/shard_map/ppermute | solution.py:290
  62.9 10.3 %collective-permute-start.12 = (f32[8,64,256]{2,1,0:T(8,128)S(1)}, f32[8,64,256]{2,1,0:T(8,128)S(1)}, u32[]{:S(2)}, u32[]{:S(2)}) collective-permute-start(f32[8,64,256]{2,1,0:T(8,128)S(1)} %get-tuple-element.100), channel_id=1, source_target_pairs={{0,8},{1,9},{2,4},{3,5},{4,2},{5,3},{6,14},{7,15},{8,0},{9,1},{10,... | collective-permute-start | bytes 1572872 | tf_op jit(solution)/shard_map/ppermute | solution.py:290
  71.3 9.7 %collective-permute-start.15 = (f32[8,64,256]{2,1,0:T(8,128)S(1)}, f32[8,64,256]{2,1,0:T(8,128)S(1)}, u32[]{:S(2)}, u32[]{:S(2)}) collective-permute-start(f32[8,64,256]{2,1,0:T(8,128)S(1)} %get-tuple-element.109), channel_id=1, source_target_pairs={{0,2},{1,3},{2,0},{3,1},{4,6},{5,7},{6,4},{7,5},{8,10},{9,11},{10,... | collective-permute-start | bytes 1572872 | tf_op jit(solution)/shard_map/ppermute | solution.py:290
  75.1 9.8 %collective-permute-start.14 = (f32[8,64,256]{2,1,0:T(8,128)S(1)}, f32[8,64,256]{2,1,0:T(8,128)S(1)}, u32[]{:S(2)}, u32[]{:S(2)}) collective-permute-start(f32[8,64,256]{2,1,0:T(8,128)S(1)} %get-tuple-element.108), channel_id=1, source_target_pairs={{0,8},{1,9},{2,4},{3,5},{4,2},{5,3},{6,14},{7,15},{8,0},{9,1},{10,... | collective-permute-start | bytes 1572872 | tf_op jit(solution)/shard_map/ppermute | solution.py:290
  82.9 9.8 %collective-permute-start.17 = (f32[8,64,256]{2,1,0:T(8,128)S(1)}, f32[8,64,256]{2,1,0:T(8,128)S(1)}, u32[]{:S(2)}, u32[]{:S(2)}) collective-permute-start(f32[8,64,256]{2,1,0:T(8,128)S(1)} %get-tuple-element.117), channel_id=1, source_target_pairs={{0,2},{1,3},{2,0},{3,1},{4,6},{5,7},{6,4},{7,5},{8,10},{9,11},{10,... | collective-permute-start | bytes 1572872 | tf_op jit(solution)/shard_map/ppermute | solution.py:290
  86.9 9.8 %collective-permute-start.16 = (f32[8,64,256]{2,1,0:T(8,128)S(1)}, f32[8,64,256]{2,1,0:T(8,128)S(1)}, u32[]{:S(2)}, u32[]{:S(2)}) collective-permute-start(f32[8,64,256]{2,1,0:T(8,128)S(1)} %get-tuple-element.116), channel_id=1, source_target_pairs={{0,8},{1,9},{2,4},{3,5},{4,2},{5,3},{6,14},{7,15},{8,0},{9,1},{10,... | collective-permute-start | bytes 1572872 | tf_op jit(solution)/shard_map/ppermute | solution.py:290
  94.6 9.2 %collective-permute-start.19 = (f32[8,64,256]{2,1,0:T(8,128)S(1)}, f32[8,64,256]{2,1,0:T(8,128)S(1)}, u32[]{:S(2)}, u32[]{:S(2)}) collective-permute-start(f32[8,64,256]{2,1,0:T(8,128)S(1)} %get-tuple-element.125), channel_id=1, source_target_pairs={{0,2},{1,3},{2,0},{3,1},{4,6},{5,7},{6,4},{7,5},{8,10},{9,11},{10,... | collective-permute-start | bytes 1572872 | tf_op jit(solution)/shard_map/ppermute | solution.py:290
  98.7 9.2 %collective-permute-start.18 = (f32[8,64,256]{2,1,0:T(8,128)S(1)}, f32[8,64,256]{2,1,0:T(8,128)S(1)}, u32[]{:S(2)}, u32[]{:S(2)}) collective-permute-start(f32[8,64,256]{2,1,0:T(8,128)S(1)} %get-tuple-element.124), channel_id=1, source_target_pairs={{0,8},{1,9},{2,4},{3,5},{4,2},{5,3},{6,14},{7,15},{8,0},{9,1},{10,... | collective-permute-start | bytes 1572872 | tf_op jit(solution)/shard_map/ppermute | solution.py:290
  109.9 1.6 %collective-permute-start.20 = (f32[8,32,256]{2,1,0:T(8,128)S(1)}, f32[8,32,256]{2,1,0:T(8,128)S(1)}, u32[]{:S(2)}, u32[]{:S(2)}) collective-permute-start(f32[8,32,256]{2,1,0:T(8,128)S(1)} %get-tuple-element.135), channel_id=1, source_target_pairs={{0,8},{1,9},{2,10},{3,11},{4,12},{5,13},{6,14},{7,15},{8,0},{9,1},... | collective-permute-start | bytes 786440 | tf_op jit(solution)/shard_map/ppermute | solution.py:290
  112.1 5.6 %collective-permute-start.21 = (f32[8,16,256]{2,1,0:T(8,128)S(1)}, f32[8,16,256]{2,1,0:T(8,128)S(1)}, u32[]{:S(2)}, u32[]{:S(2)}) collective-permute-start(f32[8,16,256]{2,1,0:T(8,128)S(1)} %pair.1.late_ref), channel_id=1, source_target_pairs={{0,16},{1,17},{2,18},{3,19},{4,20},{5,21},{6,22},{7,23},{8,24},{9,... | collective-permute-start | bytes 393224 | tf_op jit(solution)/shard_map/ppermute | solution.py:290
  (2 other events, 17.2 us)
